TPU v7x, 32 devices: a whole 2x2x4 slice. The times are simulated.
32 devices in a mesh: shard: 2 (over y), ctx: 4 (over x, core), tp: 4 (over z).
Axes of the slice: x: 2, y: 2, z: 4, core: 2. Of those that a mesh axis runs over, the one named last changes fastest.
Arguments:
- hidden: bfloat16 [8, 4096, 768], P('shard', ('ctx', 'tp')), may hold values from -6 to 6
- bank: bfloat16 [8, 16384, 768], P(('shard', 'ctx'), 'tp'), may hold values from -6 to 6
- indices: int32 [8, 1024], P(('shard', 'ctx')), may hold values from 0 to 16383, as said below
- lengths: int32 [8], replicated, may hold values from 512 to 4096, as said below
- cotangent: bfloat16 [8, 4096, 768], P('shard', ('ctx', 'tp')), may hold values from -6 to 6
- query_self: bfloat16 [768, 768], P('shard', 'tp'), may hold values from -0.21875 to 0.21875
- key_self: bfloat16 [768, 768], P('shard', 'tp'), may hold values from -0.21875 to 0.21875
- value_self: bfloat16 [768, 768], P('shard', 'tp'), may hold values from -0.21875 to 0.21875
- out_self: bfloat16 [768, 768], P('tp', 'shard'), may hold values from -1.25 to 1.25
- query_cross: bfloat16 [768, 768], P('shard', 'tp'), may hold values from -0.21875 to 0.21875
- key_cross: bfloat16 [768, 768], P('shard', 'tp'), may hold values from -0.21875 to 0.21875
- value_cross: bfloat16 [768, 768], P('shard', 'tp'), may hold values from -0.21875 to 0.21875
- out_cross: bfloat16 [768, 768], P('tp', 'shard'), may hold values from -1.75 to 1.75
- up_weight: bfloat16 [768, 3072], P('shard', 'tp'), may hold values from -0.21875 to 0.21875
- down_weight: bfloat16 [3072, 768], P('tp', 'shard'), may hold values from -0.109375 to 0.109375
- norm_gain: bfloat16 [3, 768], P(None, 'shard'), may hold values from 0.5 to 1.5
- norm_bias: bfloat16 [3, 768], P(None, 'shard'), may hold values from -0.29882812 to 0.29882812
Outputs:
- output: bfloat16 [8, 4096, 768], P('shard', ('ctx', 'tp'))
- gradient_hidden: float32 [8, 4096, 768], P('shard', ('ctx', 'tp'))
- gradient_bank: float32 [8, 16384, 768], P(('shard', 'ctx'), 'tp')
- gradient_query_self: float32 [768, 768], P('shard', 'tp')
- gradient_key_self: float32 [768, 768], P('shard', 'tp')
- gradient_value_self: float32 [768, 768], P('shard', 'tp')
- gradient_out_self: float32 [768, 768], P('tp', 'shard')
- gradient_query_cross: float32 [768, 768], P('shard', 'tp')
- gradient_key_cross: float32 [768, 768], P('shard', 'tp')
- gradient_value_cross: float32 [768, 768], P('shard', 'tp')
- gradient_out_cross: float32 [768, 768], P('tp', 'shard')
- gradient_up_weight: float32 [768, 3072], P('shard', 'tp')
- gradient_down_weight: float32 [3072, 768], P('tp', 'shard')
- gradient_norm_gain: float32 [3, 768], P(None, 'shard')
- gradient_norm_bias: float32 [3, 768], P(None, 'shard')
- statistics: float32 [6], replicated
Inputs may be any that keep to these rules, and one draw needn't show every extreme that they name: The 1024 indices of one sequence are distinct, and each sequence's list holds row 0 and row 16383. `lengths`: the valid tokens of a sequence are its first positions; some sequence has all 4096 valid and some has 512.
All inputs are finite; a program needn't handle non-finite values.
Results may differ from a plain program's by a relative error of at most 0.025.
Values may be sent and summed in bfloat16 or wider, within the bound.
No kernel may reach another device: no remote copies, remote signals or barrier semaphores. Data moves between devices by JAX's collectives and lax.ppermute only.
A program may use at most 256 MiB of HBM per device.

v0:
```python
import jax
import jax.numpy as jnp
from jax import lax
from jax.sharding import PartitionSpec as P

HEADS = 12
HEAD_DIM = 64
BLK = 256
TILE = 512


EPSILON = 1e-05
NEGATIVE = -1e30


def layer_norm(summed, gain_row, bias_row):
    average = jnp.mean(summed, axis=-1, keepdims=True)
    centred = summed - average
    variance = jnp.mean(centred * centred, axis=-1, keepdims=True)
    return centred * lax.rsqrt(variance + EPSILON) * gain_row + bias_row


def gelu_exact(inner_act):
    return jax.nn.gelu(inner_act, approximate=False)


def pick_rows(bank_table, row_ids):
    return jnp.take(bank_table, row_ids, axis=0)


def add_rows(bank_table, row_ids, row_values):
    return bank_table.at[row_ids].add(row_values)


def tile_scores(query_rows, key_rows):
    scaling = query_rows.shape[-1] ** (-0.5)
    return (
        jnp.einsum("qhd,khd->hqk", query_rows, key_rows, preferred_element_type=jnp.float32)
        * scaling
    )


def block_allowed(query_start, key_start, length):
    query_block = (query_start + jnp.arange(TILE, dtype=jnp.int32)) // BLK
    key_place = key_start + jnp.arange(TILE, dtype=jnp.int32)
    return (key_place[None, :] // BLK <= query_block[:, None]) & (key_place[None, :] < length)


def self_forward(operands):
    queries, key_rows, value_rows, length = operands
    head_count = queries.shape[1]
    key_tiles = (length + TILE - 1) // TILE

    def self_one_tile(tile_index):
        tile_start = tile_index * TILE
        query_rows = lax.dynamic_slice_in_dim(queries, tile_start, TILE, 0)
        upper = jnp.minimum(tile_index + 1, key_tiles)

        def masked_scores(key_index):
            key_start = key_index * TILE
            scores = tile_scores(query_rows, lax.dynamic_slice_in_dim(key_rows, key_start, TILE, 0))
            return (
                jnp.where(block_allowed(tile_start, key_start, length)[None], scores, NEGATIVE),
                key_start,
            )

        def running_total(key_index, carry):
            largest, row_total = carry
            scores, key_start = masked_scores(key_index)
            updated = jnp.maximum(largest, jnp.max(scores, axis=-1))
            row_total = row_total * jnp.exp(largest - updated) + jnp.sum(
                jnp.exp(scores - updated[..., None]), axis=-1
            )
            return (updated, row_total)

        start_carry = (
            jnp.full((head_count, TILE), NEGATIVE, jnp.float32),
            jnp.zeros((head_count, TILE), jnp.float32),
        )
        largest, row_total = lax.fori_loop(0, upper, running_total, start_carry)
        log_total = largest + jnp.log(row_total)

        def add_values(key_index, accumulated):
            scores, key_start = masked_scores(key_index)
            softmax_out = jnp.exp(scores - log_total[..., None]).astype(jnp.bfloat16)
            value_tile = lax.dynamic_slice_in_dim(value_rows, key_start, TILE, 0)
            return accumulated + jnp.einsum(
                "hqk,khd->qhd", softmax_out, value_tile, preferred_element_type=jnp.float32
            )

        attended = lax.fori_loop(0, upper, add_values, jnp.zeros(query_rows.shape, jnp.float32))
        return (attended, log_total)

    tile_ids = jnp.arange(queries.shape[0] // TILE, dtype=jnp.int32)
    attended, log_total = lax.map(self_one_tile, tile_ids)
    return (attended.reshape(queries.shape), log_total)


def cross_forward(operands):
    queries, key_rows, value_rows = operands

    def cross_one_tile(tile_start):
        query_rows = lax.dynamic_slice_in_dim(queries, tile_start, TILE, 0)
        scores = tile_scores(query_rows, key_rows)
        largest = jnp.max(scores, axis=-1)
        log_total = largest + jnp.log(jnp.sum(jnp.exp(scores - largest[..., None]), axis=-1))
        softmax_out = jnp.exp(scores - log_total[..., None]).astype(jnp.bfloat16)
        return (
            jnp.einsum("hqk,khd->qhd", softmax_out, value_rows, preferred_element_type=jnp.float32),
            log_total,
        )

    starts = jnp.arange(queries.shape[0] // TILE, dtype=jnp.int32) * TILE
    attended, log_total = lax.map(cross_one_tile, starts)
    return (attended.reshape(queries.shape), log_total)


def tile_backward(query_rows, back_rows, delta_rows, log_total, key_tile, value_tile, allowed):
    scaling = query_rows.shape[-1] ** (-0.5)
    scores = tile_scores(query_rows, key_tile)
    if allowed is not None:
        scores = jnp.where(allowed[None], scores, NEGATIVE)
    chances = jnp.exp(scores - log_total[..., None])
    back_chances = jnp.einsum(
        "qhd,khd->hqk", back_rows, value_tile, preferred_element_type=jnp.float32
    )
    back_scores = (chances * (back_chances - delta_rows[..., None])).astype(jnp.bfloat16)
    back_query = (
        jnp.einsum("hqk,khd->qhd", back_scores, key_tile, preferred_element_type=jnp.float32)
        * scaling
    )
    back_key = (
        jnp.einsum("hqk,qhd->khd", back_scores, query_rows, preferred_element_type=jnp.float32)
        * scaling
    )
    back_value = jnp.einsum(
        "hqk,qhd->khd", chances.astype(jnp.bfloat16), back_rows, preferred_element_type=jnp.float32
    )
    return (back_query, back_key, back_value)


def tile_inputs(queries, attended, back_out, tile_start):
    query_rows = lax.dynamic_slice_in_dim(queries, tile_start, TILE, 0)
    back_rows = lax.dynamic_slice_in_dim(back_out, tile_start, TILE, 0)
    attended_rows = lax.dynamic_slice_in_dim(attended, tile_start, TILE, 0)
    delta_rows = jnp.einsum("qhd,qhd->hq", back_rows.astype(jnp.float32), attended_rows)
    return (query_rows, back_rows, delta_rows)


def self_backward(operands):
    queries, key_rows, value_rows, attended, log_total, back_out, length = operands
    key_tiles = (length + TILE - 1) // TILE
    zero_back = jnp.zeros(queries.shape, jnp.float32)

    def self_query_tile(tile_index, carry):
        back_queries, back_keys, back_values = carry
        tile_start = tile_index * TILE
        query_rows, back_rows, delta_rows = tile_inputs(queries, attended, back_out, tile_start)
        tile_total = log_total[tile_index]

        def key_step(key_index, inner_carry):
            back_query, back_keys, back_values = inner_carry
            key_start = key_index * TILE
            key_tile = lax.dynamic_slice_in_dim(key_rows, key_start, TILE, 0)
            value_tile = lax.dynamic_slice_in_dim(value_rows, key_start, TILE, 0)
            allowed = block_allowed(tile_start, key_start, length)
            part_query, part_key, part_value = tile_backward(
                query_rows, back_rows, delta_rows, tile_total, key_tile, value_tile, allowed
            )
            back_keys = lax.dynamic_update_slice_in_dim(
                back_keys,
                lax.dynamic_slice_in_dim(back_keys, key_start, TILE, 0) + part_key,
                key_start,
                0,
            )
            back_values = lax.dynamic_update_slice_in_dim(
                back_values,
                lax.dynamic_slice_in_dim(back_values, key_start, TILE, 0) + part_value,
                key_start,
                0,
            )
            return (back_query + part_query, back_keys, back_values)

        upper = jnp.minimum(tile_index + 1, key_tiles)
        start_carry = (jnp.zeros(query_rows.shape, jnp.float32), back_keys, back_values)
        back_query, back_keys, back_values = lax.fori_loop(0, upper, key_step, start_carry)
        back_queries = lax.dynamic_update_slice_in_dim(back_queries, back_query, tile_start, 0)
        return (back_queries, back_keys, back_values)

    return lax.fori_loop(0, key_tiles, self_query_tile, (zero_back, zero_back, zero_back))


def cross_backward(operands):
    queries, key_rows, value_rows, attended, log_total, back_out, length = operands
    query_tiles = (length + TILE - 1) // TILE

    def cross_query_tile(tile_index, carry):
        back_queries, back_keys, back_values = carry
        tile_start = tile_index * TILE
        query_rows, back_rows, delta_rows = tile_inputs(queries, attended, back_out, tile_start)
        part_query, part_key, part_value = tile_backward(
            query_rows, back_rows, delta_rows, log_total[tile_index], key_rows, value_rows, None
        )
        back_queries = lax.dynamic_update_slice_in_dim(back_queries, part_query, tile_start, 0)
        return (back_queries, back_keys + part_key, back_values + part_value)

    start_carry = (
        jnp.zeros(queries.shape, jnp.float32),
        jnp.zeros(key_rows.shape, jnp.float32),
        jnp.zeros(value_rows.shape, jnp.float32),
    )
    return lax.fori_loop(0, query_tiles, cross_query_tile, start_carry)


def per_device(
    hidden,
    bank,
    indices,
    lengths,
    cotangent,
    query_self,
    key_self,
    value_self,
    out_self,
    query_cross,
    key_cross,
    value_cross,
    out_cross,
    up_weight,
    down_weight,
    norm_gain,
    norm_bias,
):
    context_count = lax.axis_size("ctx")
    tensor_count = lax.axis_size("tp")
    shard_index = lax.axis_index("shard")
    context_index = lax.axis_index("ctx")
    tensor_index = lax.axis_index("tp")
    group_sequences, device_places, model_width = hidden.shape
    device_sequences = group_sequences // context_count
    row_count = group_sequences * device_places
    head_local = HEADS // tensor_count
    group_width = head_local * HEAD_DIM
    full_width = HEADS * HEAD_DIM
    sequence_len = device_places * context_count * tensor_count

    def context_part(weight, axis_dim):
        piece_size = weight.shape[axis_dim] // context_count
        return lax.dynamic_slice_in_dim(weight, context_index * piece_size, piece_size, axis_dim)

    part_query_self = context_part(query_self, 0)
    part_key_self = context_part(key_self, 0)
    part_value_self = context_part(value_self, 0)
    part_out_self = context_part(out_self, 1)
    part_query_cross = context_part(query_cross, 0)
    part_key_cross = context_part(key_cross, 0)
    part_value_cross = context_part(value_cross, 0)
    part_out_cross = context_part(out_cross, 1)
    part_up = context_part(up_weight, 0)
    part_down = context_part(down_weight, 1)
    part_gain = context_part(norm_gain, 1)
    part_bias = context_part(norm_bias, 1)
    (
        part_query_self,
        part_key_self,
        part_value_self,
        part_out_self,
        part_query_cross,
        part_out_cross,
        part_up,
        part_down,
    ) = (
        lax.all_gather(part_query_self, "tp", axis=1, tiled=True),
        lax.all_gather(part_key_self, "tp", axis=1, tiled=True),
        lax.all_gather(part_value_self, "tp", axis=1, tiled=True),
        lax.all_gather(part_out_self, "tp", axis=0, tiled=True),
        lax.all_gather(part_query_cross, "tp", axis=1, tiled=True),
        lax.all_gather(part_out_cross, "tp", axis=0, tiled=True),
        lax.all_gather(part_up, "tp", axis=1, tiled=True),
        lax.all_gather(part_down, "tp", axis=0, tiled=True),
    )
    (
        full_query_self,
        full_key_self,
        full_value_self,
        full_out_self,
        full_query_cross,
        own_key_cross,
        own_value_cross,
        full_out_cross,
        full_up,
        full_down,
        full_gain,
        full_bias,
    ) = (
        lax.all_gather(part_query_self, ("shard", "ctx"), axis=0, tiled=True),
        lax.all_gather(part_key_self, ("shard", "ctx"), axis=0, tiled=True),
        lax.all_gather(part_value_self, ("shard", "ctx"), axis=0, tiled=True),
        lax.all_gather(part_out_self, ("shard", "ctx"), axis=1, tiled=True),
        lax.all_gather(part_query_cross, ("shard", "ctx"), axis=0, tiled=True),
        lax.all_gather(part_key_cross, ("shard", "ctx"), axis=0, tiled=True),
        lax.all_gather(part_value_cross, ("shard", "ctx"), axis=0, tiled=True),
        lax.all_gather(part_out_cross, ("shard", "ctx"), axis=1, tiled=True),
        lax.all_gather(part_up, ("shard", "ctx"), axis=0, tiled=True),
        lax.all_gather(part_down, ("shard", "ctx"), axis=1, tiled=True),
        lax.all_gather(part_gain, ("shard", "ctx"), axis=1, tiled=True),
        lax.all_gather(part_bias, ("shard", "ctx"), axis=1, tiled=True),
    )
    gain_rows = full_gain.astype(jnp.float32)
    bias_rows = full_bias.astype(jnp.float32)
    group_lengths = lax.dynamic_slice_in_dim(
        lengths, shard_index * group_sequences, group_sequences
    )
    own_lengths = lax.dynamic_slice_in_dim(
        group_lengths, context_index * device_sequences, device_sequences
    )
    places = (context_index * tensor_count + tensor_index) * device_places + jnp.arange(
        device_places, dtype=jnp.int32
    )
    valid_rows = (
        (places[None, :] < group_lengths[:, None]).astype(jnp.float32).reshape(row_count, 1)
    )

    def row_view(matrix):
        return matrix.reshape(context_count, device_sequences, device_places, matrix.shape[-1])

    def to_sequences(blocks):
        merged = blocks.reshape(context_count * tensor_count * device_sequences, device_places, -1)
        return lax.all_to_all(merged, ("ctx", "tp"), split_axis=0, concat_axis=1, tiled=True)

    def to_positions(sequences):
        returned = lax.all_to_all(sequences, ("ctx", "tp"), split_axis=1, concat_axis=0, tiled=True)
        return returned.reshape(context_count, tensor_count, device_sequences, device_places, -1)

    hidden_view = hidden.reshape(context_count, device_sequences, device_places, model_width)
    self_stack = jnp.stack([full_query_self, full_key_self, full_value_self], axis=1).reshape(
        model_width, 3, tensor_count, group_width
    )
    projected = jnp.einsum(
        "cspd,dkth->ctspkh", hidden_view, self_stack, preferred_element_type=jnp.float32
    ).astype(jnp.bfloat16)
    self_sequences = to_sequences(projected).reshape(
        device_sequences, sequence_len, 3, head_local, HEAD_DIM
    )
    self_query = self_sequences[:, :, 0]
    self_key = self_sequences[:, :, 1]
    self_value = self_sequences[:, :, 2]
    self_out, self_total = lax.map(self_forward, (self_query, self_key, self_value, own_lengths))
    self_back = to_positions(
        self_out.astype(jnp.bfloat16).reshape(device_sequences, sequence_len, group_width)
    )
    self_out_view = full_out_self.reshape(tensor_count, group_width, model_width)
    branch_one = jnp.einsum(
        "ctsph,thd->cspd", self_back, self_out_view, preferred_element_type=jnp.float32
    ).reshape(row_count, model_width)
    hidden_float = hidden.reshape(row_count, model_width).astype(jnp.float32)
    first_sum = hidden_float + branch_one
    first = layer_norm(first_sum, gain_rows[0], bias_rows[0])
    first_low = first.astype(jnp.bfloat16)
    cross_query_view = full_query_cross.reshape(model_width, tensor_count, group_width)
    cross_projected = jnp.einsum(
        "cspd,dth->ctsph", row_view(first_low), cross_query_view, preferred_element_type=jnp.float32
    ).astype(jnp.bfloat16)
    cross_query = to_sequences(cross_projected).reshape(
        device_sequences, sequence_len, head_local, HEAD_DIM
    )
    bank_local = bank.shape[1]
    owner_tensor = indices // bank_local
    local_rows = indices - owner_tensor * bank_local
    owned_mask = (owner_tensor == tensor_index)[:, :, None]
    picked = jax.vmap(pick_rows)(bank, local_rows)
    picked = jnp.where(owned_mask, picked.astype(jnp.float32), 0.0)
    selected = lax.psum(picked.astype(jnp.bfloat16), "tp")
    retrieved = selected.shape[1]
    cross_key = (
        jnp.einsum("skd,dh->skh", selected, own_key_cross, preferred_element_type=jnp.float32)
        .astype(jnp.bfloat16)
        .reshape(device_sequences, retrieved, head_local, HEAD_DIM)
    )
    cross_value = (
        jnp.einsum("skd,dh->skh", selected, own_value_cross, preferred_element_type=jnp.float32)
        .astype(jnp.bfloat16)
        .reshape(device_sequences, retrieved, head_local, HEAD_DIM)
    )
    cross_out, cross_total = lax.map(cross_forward, (cross_query, cross_key, cross_value))
    cross_back = to_positions(
        cross_out.astype(jnp.bfloat16).reshape(device_sequences, sequence_len, group_width)
    )
    cross_out_view = full_out_cross.reshape(tensor_count, group_width, model_width)
    branch_two = jnp.einsum(
        "ctsph,thd->cspd", cross_back, cross_out_view, preferred_element_type=jnp.float32
    ).reshape(row_count, model_width)
    second_sum = first + branch_two
    second = layer_norm(second_sum, gain_rows[1], bias_rows[1])
    second_low = second.astype(jnp.bfloat16)
    inner_act = jnp.dot(second_low, full_up, preferred_element_type=jnp.float32)
    active_float, gelu_pull = jax.vjp(gelu_exact, inner_act)
    active = active_float.astype(jnp.bfloat16)
    ffn_partial = jnp.dot(active, full_down, preferred_element_type=jnp.float32)
    third_sum = second + ffn_partial
    output = layer_norm(third_sum, gain_rows[2], bias_rows[2])

    def valid_squares(matrix):
        return jnp.sum(valid_rows * matrix * matrix)

    square_terms = jnp.stack(
        [
            valid_squares(hidden_float),
            valid_squares(branch_one),
            valid_squares(first),
            valid_squares(branch_two),
            valid_squares(second),
            valid_squares(ffn_partial),
        ]
    )

    def norm_back(summed, layer_index, back_in):
        normed, pullback = jax.vjp(
            layer_norm, summed, gain_rows[layer_index], bias_rows[layer_index]
        )
        return pullback(back_in)

    back_output = cotangent.reshape(row_count, model_width).astype(jnp.float32) * valid_rows
    back_third, gain_three, bias_three = norm_back(third_sum, 2, back_output)
    back_branch_three = back_third.astype(jnp.bfloat16)
    back_active = jnp.einsum(
        "rd,fd->rf", back_branch_three, full_down, preferred_element_type=jnp.float32
    )
    back_inner = gelu_pull(back_active)[0].astype(jnp.bfloat16)
    back_down = jnp.einsum(
        "rf,rd->fd", active, back_branch_three, preferred_element_type=jnp.float32
    )
    back_up = jnp.einsum("rd,rf->df", second_low, back_inner, preferred_element_type=jnp.float32)
    back_ffn_in = jnp.einsum("rf,df->rd", back_inner, full_up, preferred_element_type=jnp.float32)
    back_second = back_third + back_ffn_in
    back_second_sum, gain_two, bias_two = norm_back(second_sum, 1, back_second)
    back_branch_two = row_view(back_second_sum.astype(jnp.bfloat16))
    back_out_cross = jnp.einsum(
        "ctsph,cspd->thd", cross_back, back_branch_two, preferred_element_type=jnp.float32
    ).reshape(full_width, model_width)
    back_cross_attended = jnp.einsum(
        "cspd,thd->ctsph", back_branch_two, cross_out_view, preferred_element_type=jnp.float32
    ).astype(jnp.bfloat16)
    back_cross_sequences = to_sequences(back_cross_attended).reshape(
        device_sequences, sequence_len, head_local, HEAD_DIM
    )
    back_cross_query, back_cross_key, back_cross_value = lax.map(
        cross_backward,
        (
            cross_query,
            cross_key,
            cross_value,
            cross_out,
            cross_total,
            back_cross_sequences,
            own_lengths,
        ),
    )
    back_key_low = back_cross_key.astype(jnp.bfloat16).reshape(
        device_sequences, retrieved, group_width
    )
    back_value_low = back_cross_value.astype(jnp.bfloat16).reshape(
        device_sequences, retrieved, group_width
    )
    back_key_cross = jnp.einsum(
        "skd,skh->dh", selected, back_key_low, preferred_element_type=jnp.float32
    )
    back_value_cross = jnp.einsum(
        "skd,skh->dh", selected, back_value_low, preferred_element_type=jnp.float32
    )
    back_selected = jnp.einsum(
        "skh,dh->skd", back_key_low, own_key_cross, preferred_element_type=jnp.float32
    ) + jnp.einsum(
        "skh,dh->skd", back_value_low, own_value_cross, preferred_element_type=jnp.float32
    )
    selected_total = lax.psum(back_selected.astype(jnp.bfloat16), "tp").astype(jnp.float32)
    owned_back = jnp.where(owned_mask, selected_total, 0.0)
    back_bank = jax.vmap(add_rows)(jnp.zeros(bank.shape, jnp.float32), local_rows, owned_back)
    back_query_rows = to_positions(
        back_cross_query.astype(jnp.bfloat16).reshape(device_sequences, sequence_len, group_width)
    )
    back_query_cross = jnp.einsum(
        "cspd,ctsph->dth", row_view(first_low), back_query_rows, preferred_element_type=jnp.float32
    ).reshape(model_width, full_width)
    back_first = back_second_sum + jnp.einsum(
        "ctsph,dth->cspd", back_query_rows, cross_query_view, preferred_element_type=jnp.float32
    ).reshape(row_count, model_width)
    back_first_sum, gain_one, bias_one = norm_back(first_sum, 0, back_first)
    back_branch_one = row_view(back_first_sum.astype(jnp.bfloat16))
    back_out_self = jnp.einsum(
        "ctsph,cspd->thd", self_back, back_branch_one, preferred_element_type=jnp.float32
    ).reshape(full_width, model_width)
    back_self_attended = jnp.einsum(
        "cspd,thd->ctsph", back_branch_one, self_out_view, preferred_element_type=jnp.float32
    ).astype(jnp.bfloat16)
    back_self_sequences = to_sequences(back_self_attended).reshape(
        device_sequences, sequence_len, head_local, HEAD_DIM
    )
    back_self_query, back_self_key, back_self_value = lax.map(
        self_backward,
        (self_query, self_key, self_value, self_out, self_total, back_self_sequences, own_lengths),
    )
    back_self_stack = (
        jnp.stack([back_self_query, back_self_key, back_self_value], axis=2)
        .astype(jnp.bfloat16)
        .reshape(device_sequences, sequence_len, 3 * group_width)
    )
    back_projected = to_positions(back_self_stack).reshape(
        context_count, tensor_count, device_sequences, device_places, 3, group_width
    )
    back_stack_weight = jnp.einsum(
        "cspd,ctspkh->dkth", hidden_view, back_projected, preferred_element_type=jnp.float32
    ).reshape(model_width, 3, full_width)
    back_query_self = back_stack_weight[:, 0]
    back_key_self = back_stack_weight[:, 1]
    back_value_self = back_stack_weight[:, 2]
    back_hidden = back_first_sum + jnp.einsum(
        "ctspkh,dkth->cspd", back_projected, self_stack, preferred_element_type=jnp.float32
    ).reshape(row_count, model_width)
    (
        back_query_self,
        back_key_self,
        back_value_self,
        back_out_self,
        back_query_cross,
        back_key_cross,
        back_value_cross,
        back_out_cross,
        back_up,
        back_down,
    ) = (
        lax.psum_scatter(
            back_query_self.astype(jnp.bfloat16), ("shard", "ctx"), scatter_dimension=0, tiled=True
        ).astype(jnp.float32),
        lax.psum_scatter(
            back_key_self.astype(jnp.bfloat16), ("shard", "ctx"), scatter_dimension=0, tiled=True
        ).astype(jnp.float32),
        lax.psum_scatter(
            back_value_self.astype(jnp.bfloat16), ("shard", "ctx"), scatter_dimension=0, tiled=True
        ).astype(jnp.float32),
        lax.psum_scatter(
            back_out_self.astype(jnp.bfloat16), ("shard", "ctx"), scatter_dimension=1, tiled=True
        ).astype(jnp.float32),
        lax.psum_scatter(
            back_query_cross.astype(jnp.bfloat16), ("shard", "ctx"), scatter_dimension=0, tiled=True
        ).astype(jnp.float32),
        lax.psum_scatter(
            back_key_cross.astype(jnp.bfloat16), ("shard", "ctx"), scatter_dimension=0, tiled=True
        ).astype(jnp.float32),
        lax.psum_scatter(
            back_value_cross.astype(jnp.bfloat16), ("shard", "ctx"), scatter_dimension=0, tiled=True
        ).astype(jnp.float32),
        lax.psum_scatter(
            back_out_cross.astype(jnp.bfloat16), ("shard", "ctx"), scatter_dimension=1, tiled=True
        ).astype(jnp.float32),
        lax.psum_scatter(
            back_up.astype(jnp.bfloat16), ("shard", "ctx"), scatter_dimension=0, tiled=True
        ).astype(jnp.float32),
        lax.psum_scatter(
            back_down.astype(jnp.bfloat16), ("shard", "ctx"), scatter_dimension=1, tiled=True
        ).astype(jnp.float32),
    )
    (
        back_query_self,
        back_key_self,
        back_value_self,
        back_out_self,
        back_query_cross,
        back_out_cross,
        back_up,
        back_down,
    ) = (
        lax.psum_scatter(
            back_query_self.astype(jnp.bfloat16), "tp", scatter_dimension=1, tiled=True
        ).astype(jnp.float32),
        lax.psum_scatter(
            back_key_self.astype(jnp.bfloat16), "tp", scatter_dimension=1, tiled=True
        ).astype(jnp.float32),
        lax.psum_scatter(
            back_value_self.astype(jnp.bfloat16), "tp", scatter_dimension=1, tiled=True
        ).astype(jnp.float32),
        lax.psum_scatter(
            back_out_self.astype(jnp.bfloat16), "tp", scatter_dimension=0, tiled=True
        ).astype(jnp.float32),
        lax.psum_scatter(
            back_query_cross.astype(jnp.bfloat16), "tp", scatter_dimension=1, tiled=True
        ).astype(jnp.float32),
        lax.psum_scatter(
            back_out_cross.astype(jnp.bfloat16), "tp", scatter_dimension=0, tiled=True
        ).astype(jnp.float32),
        lax.psum_scatter(
            back_up.astype(jnp.bfloat16), "tp", scatter_dimension=1, tiled=True
        ).astype(jnp.float32),
        lax.psum_scatter(
            back_down.astype(jnp.bfloat16), "tp", scatter_dimension=0, tiled=True
        ).astype(jnp.float32),
    )
    (
        back_query_self,
        back_key_self,
        back_value_self,
        back_out_self,
        back_query_cross,
        back_key_cross,
        back_value_cross,
        back_out_cross,
        back_up,
        back_down,
    ) = (
        lax.all_gather(back_query_self.astype(jnp.bfloat16), "ctx", axis=0, tiled=True).astype(
            back_query_self.dtype
        ),
        lax.all_gather(back_key_self.astype(jnp.bfloat16), "ctx", axis=0, tiled=True).astype(
            back_key_self.dtype
        ),
        lax.all_gather(back_value_self.astype(jnp.bfloat16), "ctx", axis=0, tiled=True).astype(
            back_value_self.dtype
        ),
        lax.all_gather(back_out_self.astype(jnp.bfloat16), "ctx", axis=1, tiled=True).astype(
            back_out_self.dtype
        ),
        lax.all_gather(back_query_cross.astype(jnp.bfloat16), "ctx", axis=0, tiled=True).astype(
            back_query_cross.dtype
        ),
        lax.all_gather(back_key_cross.astype(jnp.bfloat16), "ctx", axis=0, tiled=True).astype(
            back_key_cross.dtype
        ),
        lax.all_gather(back_value_cross.astype(jnp.bfloat16), "ctx", axis=0, tiled=True).astype(
            back_value_cross.dtype
        ),
        lax.all_gather(back_out_cross.astype(jnp.bfloat16), "ctx", axis=1, tiled=True).astype(
            back_out_cross.dtype
        ),
        lax.all_gather(back_up.astype(jnp.bfloat16), "ctx", axis=0, tiled=True).astype(
            back_up.dtype
        ),
        lax.all_gather(back_down.astype(jnp.bfloat16), "ctx", axis=1, tiled=True).astype(
            back_down.dtype
        ),
    )
    gain_terms = jnp.stack([gain_one, gain_two, gain_three])
    bias_terms = jnp.stack([bias_one, bias_two, bias_three])
    square_total, gain_total, bias_total = lax.psum(
        (square_terms, gain_terms, bias_terms), ("shard", "ctx", "tp")
    )
    token_total = jnp.sum(lengths).astype(jnp.float32) * model_width
    statistics = jnp.sqrt(square_total / token_total)
    shard_width = model_width // lax.axis_size("shard")
    back_gain = lax.dynamic_slice_in_dim(gain_total, shard_index * shard_width, shard_width, 1)
    back_bias = lax.dynamic_slice_in_dim(bias_total, shard_index * shard_width, shard_width, 1)
    return (
        output.astype(jnp.bfloat16).reshape(hidden.shape),
        back_hidden.reshape(hidden.shape),
        back_bank,
        back_query_self,
        back_key_self,
        back_value_self,
        back_out_self,
        back_query_cross,
        back_key_cross,
        back_value_cross,
        back_out_cross,
        back_up,
        back_down,
        back_gain,
        back_bias,
        statistics,
    )


def solution(mesh):
    return jax.shard_map(
        per_device,
        mesh=mesh,
        in_specs=(
            P("shard", ("ctx", "tp"), None),
            P(("shard", "ctx"), "tp", None),
            P(("shard", "ctx"), None),
            P(),
            P("shard", ("ctx", "tp"), None),
            P("shard", "tp"),
            P("shard", "tp"),
            P("shard", "tp"),
            P("tp", "shard"),
            P("shard", "tp"),
            P("shard", "tp"),
            P("shard", "tp"),
            P("tp", "shard"),
            P("shard", "tp"),
            P("tp", "shard"),
            P(None, "shard"),
            P(None, "shard"),
        ),
        out_specs=(
            P("shard", ("ctx", "tp"), None),
            P("shard", ("ctx", "tp"), None),
            P(("shard", "ctx"), "tp", None),
            P("shard", "tp"),
            P("shard", "tp"),
            P("shard", "tp"),
            P("tp", "shard"),
            P("shard", "tp"),
            P("shard", "tp"),
            P("shard", "tp"),
            P("tp", "shard"),
            P("shard", "tp"),
            P("tp", "shard"),
            P(None, "shard"),
            P(None, "shard"),
            P(),
        ),
        check_vma=False,
    )
```

profile of v0, /device:TPU:0, one launch (start us, length us, event | category | flops | bytes accessed | tf_op | source)
XLA Modules:
  0.0 2527.6 jit_solution(4026469167736254520)
XLA Ops:
  9.1 15.5 all_gather.90
  26.4 14.0 all_gather.92
  42.3 13.6 all_gather.94
  58.5 19.0 all-gather.13.cloned.1.call-done
  79.9 24.2 all-gather.15.cloned.1.call-done
  121.5 110.9 %all_gather.96 = bf16[768,96]{1,0:T(8,128)(2,1)S(1)} all-gather(bf16[192,96]{1,0:T(8,128)(2,1)S(1)} %constant_dynamic-slice_fusion.14), channel_id=1, replica_groups=mesh['shard'=2,'ctx'=4,'tp'=4] {'tp'}, dimensions={0}, use_global_device_ids=true | all-gather | bytes 184320 | tf_op jit(solution)/shard_map/all_gather | solution.py:276
  234.2 14.0 all_gather.100
  273.9 112.9 %while.175 = (s32[]{:T(128)}, f32[8,512,3,64]{1,3,2,0:T(8,128)}, f32[8,3,512]{2,1,0:T(4,128)S(1)}, s32[8]{0:T(128)S(1)}, s32[]{:T(128)}, /*index=5*/bf16[4096,3,...) while((s32[]{:T(128)}, f32[8,512,3,64]{1,3,2,0:T(8,128)}, ...), condition=%wide.region_7.8_spmd, body=%wide.region_0.7_spmd.sunk | while | flops 311826944 | bytes 11098501 | solution.py:95
  405.7 23.6 reduce.28
  432.6 109.8 %all-to-all-start.1 = ((bf16[16,2,24576]{2,1,0:T(2,128)(2,1)}), bf16[16,2,24576]{2,1,0:T(2,128)(2,1)}, u32[]{:S(2)}, u32[]{:S(2)}) async-start(bf16[16,2,24576]{2,1,0:T(2,128)(2,1)} %reshape.992), calls=%async_computation.1 | async-start | bytes 3145728 | tf_op jit(solution)/shard_map/all_to_all | solution.py:332
  542.4 14.0 gather_fusion
  559.3 48.0 %all_gather.104 = bf16[768,96]{1,0:T(8,128)(2,1)S(1)} all-gather(bf16[192,96]{1,0:T(8,128)(2,1)S(1)} %constant_dynamic-slice_fusion.8), channel_id=1, replica_groups=mesh['shard'=2,'ctx'=4,'tp'=4] {'tp'}, dimensions={0}, use_global_device_ids=true | all-gather | bytes 184320 | tf_op jit(solution)/shard_map/all_gather | solution.py:278
  608.8 14.7 all-gather
  683.3 48.8 %all_gather.106 = bf16[96,3072]{1,0:T(8,128)(2,1)} all-gather(bf16[96,768]{1,0:T(8,128)(2,1)S(1)} %constant_dynamic-slice_fusion.7), channel_id=1, replica_groups=mesh['shard'=2,'ctx'=4,'tp'=4] {'tp'}, dimensions={1}, use_global_device_ids=true | all-gather | bytes 737280 | tf_op jit(solution)/shard_map/all_gather | solution.py:279
  766.0 57.0 %while.176 = (s32[]{:T(128)}, f32[8,512,3,64]{1,3,2,0:T(8,128)}, f32[8,3,512]{2,1,0:T(4,128)S(1)}, s32[8]{0:T(128)S(1)}, bf16[4096,3,64]{0,2,1:T(8,128)(2,1)S(1)...) while((s32[]{:T(128)}, f32[8,512,3,64]{1,3,2,0:T(8,128)}, ...), condition=%wide.region_14.15_spmd, body=%wide.region_11.14_spmd.sunk | while | flops 415234560 | bytes 20308636 | solution.py:114
  841.6 23.6 reduce.29
  874.6 47.6 %all_gather.108 = bf16[3072,96]{0,1:T(8,128)(2,1)} all-gather(bf16[768,96]{0,1:T(8,128)(2,1)S(1)} %copy.428), channel_id=1, replica_groups=mesh['shard'=2,'ctx'=4,'tp'=4] {'tp'}, dimensions={0}, use_global_device_ids=true | all-gather | bytes 737280 | tf_op jit(solution)/shard_map/all_gather | solution.py:280
  958.2 38.1 %multiply_convert_fusion.1 = (bf16[1024,3072]{1,0:T(8,128)(2,1)}, f32[1024,3072]{1,0:T(8,128)}, f32[1024,3072]{1,0:T(8,128)}) fusion(bf16[768,3072]{1,0:T(8,128)(2,1)} %all-gather.23.cloned.1.call-done, f32[1024,768]{1,0:T(8,128)} %copy-done.23, f32[768]{0:T(1024)S(1)} %get-tuple-element.1194, f32[768]{0:T(1024)S(1)} %get-tuple-element.1191, ...), kind=kOutput, calls=%fused_computation.160 | convolution fusion | flops 5040242688 | bytes 39335936 | tf_op jit(solution)/shard_map/dot_general | solution.py:396
  1013.2 18.0 add_convert_fusion
  1031.2 13.0 multiply_reduce_fusion.5
  1065.2 27.5 %all-to-all-done.4 = bf16[16,256,192]{1,2,0:T(8,128)(2,1)S(1)} async-done(((bf16[16,256,192]{1,2,0:T(8,128)(2,1)}), bf16[16,256,192]{1,2,0:T(8,128)(2,1)S(1)}, u32[]{:S(2)}, u32[]{:S(2)}) %all-to-all-start.4) | async-done | bytes 1572896 | tf_op jit(solution)/shard_map/all_to_all | solution.py:329
  1099.7 40.6 %while.177 = (s32[]{:T(128)}, bf16[4096,3,64]{0,2,1:T(8,128)(2,1)}, f32[1024,3,64]{0,2,1:T(8,128)S(1)}, f32[1024,3,64]{0,2,1:T(8,128)}, s32[]{:T(128)}, /*index=...) while((s32[]{:T(128)}, bf16[4096,3,64]{0,2,1:T(8,128)(2,1)}, ...), condition=%wide.region_24.25_spmd, body=%wide.region_23.24_spmd.sunk | while | flops 1020197376 | bytes 61194604 | solution.py:212
  1150.4 24.9 reduce.30
  1180.9 104.0 %all-to-all-start.5 = ((bf16[16,2,24576]{2,1,0:T(2,128)(2,1)}), bf16[16,2,24576]{2,1,0:T(2,128)(2,1)}, u32[]{:S(2)}, u32[]{:S(2)}) async-start(bf16[16,2,24576]{2,1,0:T(2,128)(2,1)} %reshape.996), calls=%async_computation.5 | async-start | bytes 3145728 | tf_op jit(solution)/shard_map/all_to_all | solution.py:332
  1289.4 33.8 %all-to-all-done.5 = bf16[16,2,24576]{2,1,0:T(2,128)(2,1)} async-done(((bf16[16,2,24576]{2,1,0:T(2,128)(2,1)}), bf16[16,2,24576]{2,1,0:T(2,128)(2,1)}, u32[]{:S(2)}, u32[]{:S(2)}) %all-to-all-start.5) | async-done | bytes 1572896 | tf_op jit(solution)/shard_map/all_to_all | solution.py:332
  1397.3 15.3 all-to-all-done.6
  1421.0 41.8 %while.179 = (s32[]{:T(128)}, bf16[4096,3,64]{0,2,1:T(8,128)(2,1)S(1)}, f32[4096,3,64]{0,2,1:T(8,128)}, f32[4096,3,64]{0,2,1:T(8,128)}, s32[]{:T(128)}, /*index=...) while((s32[]{:T(128)}, ...), condition=%wide.region_30.31_spmd, body=%wide.region_27.30_spmd.sunk | while | flops 512507392 | bytes 22668980 | solution.py:190
  1425.2 11.0 while.182
  1440.5 22.0 while.182
  1468.5 21.5 copy.363
  1490.0 113.3 %reduce.31 = bf16[4096,576]{1,0:T(8,128)(2,1)} reduce(bf16[4096,1,576]{2,1,0:T(2,128)(2,1)} %bitcast.469, bf16[]{:T(256)} %broadcast.965), dimensions={1}, to_apply=%bitcast.322.reduce_sub_computation | reduce | bytes 9437186
  1603.3 13.1 reshape.998
  1616.4 299.2 %all-to-all-start.7 = ((bf16[16,2,73728]{2,1,0:T(2,128)(2,1)}), bf16[16,2,73728]{2,1,0:T(2,128)(2,1)}, u32[]{:S(2)}, u32[]{:S(2)}) async-start(bf16[16,2,73728]{2,1,0:T(2,128)(2,1)} %reshape.998), calls=%async_computation.7 | async-start | bytes 9437184 | tf_op jit(solution)/shard_map/all_to_all | solution.py:332
  1937.0 84.3 %all-to-all-done.7 = bf16[16,2,73728]{2,1,0:T(2,128)(2,1)} async-done(((bf16[16,2,73728]{2,1,0:T(2,128)(2,1)}), bf16[16,2,73728]{2,1,0:T(2,128)(2,1)}, u32[]{:S(2)}, u32[]{:S(2)}) %all-to-all-start.7) | async-done | bytes 4718624 | tf_op jit(solution)/shard_map/all_to_all | solution.py:332
  2021.3 15.1 reshape.999
  2036.4 21.0 copy.364
  2085.9 17.7 reduce-scatter.47.cloned.1.call-done
  2110.0 24.4 reduce-scatter.65.cloned.1.call-done
  2141.7 39.4 %reduce-scatter.41.cloned.1.call-done = bf16[96,192]{1,0:T(8,128)(2,1)} async-done(((bf16[768,192]{1,0:T(8,128)(2,1)}), bf16[96,192]{1,0:T(8,128)(2,1)}) %reduce-scatter.41.cloned.1.call-update) | async-done | bytes 36880 | tf_op jit(solution)/shard_map/reduce_scatter | solution.py:547
  2187.7 30.1 %reduce-scatter.43.cloned.1.call-done = bf16[96,192]{1,0:T(8,128)(2,1)} async-done(((bf16[768,192]{1,0:T(8,128)(2,1)}), bf16[96,192]{1,0:T(8,128)(2,1)}) %reduce-scatter.43.cloned.1.call-update) | async-done | bytes 36880 | tf_op jit(solution)/shard_map/reduce_scatter | solution.py:550
  2224.7 13.8 scatter_custom_fusion
  2242.4 94.2 %all-reduce = (f32[3,768]{1,0:T(4,128)S(1)}, f32[3,768]{1,0:T(4,128)S(1)}, f32[6]{0:T(128)S(1)}) all-reduce(f32[3,768]{1,0:T(4,128)S(1)} %pad_maximum_fusion.4, f32[3,768]{1,0:T(4,128)S(1)} %pad_maximum_fusion.5, f32[6]{0:T(128)S(1)} %stack.73), channel_id=1, replica_groups=mesh['shard'=2,'ctx'=4,'tp'=4] {'shard','ctx','tp'}, use_global_device_ids=true, to_apply=%region_54.55 | all-reduce | flops 4614 | bytes 36912 | tf_op jit(solution)/shard_map/psum | solution.py:643
  2367.0 22.5 reduce-scatter.53.cloned.1.call-done
  2398.5 13.8 reduce-scatter.49.cloned.1.call-done
  2436.7 13.9 reduce-scatter.59.cloned.1.call-done
  2461.7 11.1 reduce-scatter.31.cloned.1.call-done
  2480.1 13.1 reduce-scatter.33.cloned.1.call-done
  2500.6 12.4 reduce-scatter.35.cloned.1.call-done
  (825 shorter events, 873.2 us)
Async XLA Ops:
  8.0 675.3 %copy-start = (bf16[384,768]{1,0:T(8,128)(2,1)S(1)}, bf16[384,768]{1,0:T(8,128)(2,1)}, u32[]{:S(2)}) copy-start(bf16[384,768]{1,0:T(8,128)(2,1)} %param.44) | copy-start | bytes 1769476
  8.0 48.7 %all-gather.11.cloned.1.call-start = ((), (), s32[]{:S(2)}) async-start(), calls=%async_computation.26 | async-start | bytes 1327104 | tf_op jit(solution)/shard_map/all_gather | solution.py:296
  25.4 52.1 %all-gather.13.cloned.1.call-start = ((), (), s32[]{:S(2)}) async-start(), calls=%async_computation.27 | async-start | bytes 1327104 | tf_op jit(solution)/shard_map/all_gather | solution.py:297
  41.3 62.8 %all-gather.15.cloned.1.call-start = ((), (), s32[]{:S(2)}) async-start(), calls=%async_computation.28 | async-start | bytes 1327104 | tf_op jit(solution)/shard_map/all_gather | solution.py:298
  114.7 137.0 %all-to-all-start = ((bf16[16,256,576]{1,2,0:T(8,128)(2,1)}), bf16[16,256,576]{1,2,0:T(8,128)(2,1)}, u32[]{:S(2)}, u32[]{:S(2)}) async-start(bf16[16,256,576]{1,2,0:T(8,128)(2,1)} %bitcast.474), calls=%async_computation | async-start | bytes 9437184 | tf_op jit(solution)/shard_map/all_to_all | solution.py:329
  120.5 514.5 %all-gather.17.cloned.1.call-start = ((), (), s32[]{:S(2)}) async-start(), calls=%async_computation.29 | async-start | bytes 1327104 | tf_op jit(solution)/shard_map/all_gather | solution.py:299
  233.2 403.3 %all-gather.19.cloned.1.call-start = ((), (), s32[]{:S(2)}) async-start(), calls=%async_computation.30 | async-start | bytes 1327104 | tf_op jit(solution)/shard_map/all_gather | solution.py:300
  250.3 306.1 %copy-start.74 = (pred[1024]{0:T(1024)(128)(4,1)}, pred[1024]{0:T(1024)(128)(4,1)S(1)}, u32[]{:S(2)}) copy-start(pred[1024]{0:T(1024)(128)(4,1)S(1)} %get-tuple-element.1360) | copy-start | bytes 3076
  432.6 206.8 %all-to-all-start.1 = ((bf16[16,2,24576]{2,1,0:T(2,128)(2,1)}), bf16[16,2,24576]{2,1,0:T(2,128)(2,1)}, u32[]{:S(2)}, u32[]{:S(2)}) async-start(bf16[16,2,24576]{2,1,0:T(2,128)(2,1)} %reshape.992), calls=%async_computation.1 | async-start | bytes 3145728 | tf_op jit(solution)/shard_map/all_to_all | solution.py:332
  542.4 212.2 %all-reduce.4.cloned.1.call-start = ((), (), s32[]{:S(2)}) async-start(), calls=%async_computation.31 | async-start | bytes 3145728 | tf_op jit(solution)/shard_map/psum | solution.py:373
  558.2 364.8 %all-gather.21.cloned.1.call-start = ((), (), s32[]{:S(2)}) async-start(), calls=%async_computation.32 | async-start | bytes 1327104 | tf_op jit(solution)/shard_map/all_gather | solution.py:303
  634.3 315.6 %copy-start.55 = (f32[768]{0:T(1024)}, f32[768]{0:T(1024)S(1)}, u32[]{:S(2)}) copy-start(f32[768]{0:T(1024)S(1)} %get-tuple-element.1192) | copy-start | bytes 9220
  634.3 409.9 %copy-start.66 = (f32[768]{0:T(1024)}, f32[768]{0:T(1024)S(1)}, u32[]{:S(2)}) copy-start(f32[768]{0:T(1024)S(1)} %get-tuple-element.1191) | copy-start | bytes 9220
  634.9 315.0 %copy-start.68 = (f32[768]{0:T(1024)}, f32[768]{0:T(1024)S(1)}, u32[]{:S(2)}) copy-start(f32[768]{0:T(1024)S(1)} %get-tuple-element.1195) | copy-start | bytes 9220
  634.9 396.2 %copy-start.80 = (f32[768]{0:T(1024)}, f32[768]{0:T(1024)S(1)}, u32[]{:S(2)}) copy-start(f32[768]{0:T(1024)S(1)} %get-tuple-element.1194) | copy-start | bytes 9220
  673.3 276.7 %copy-start.48 = (f32[1024]{0:T(1024)}, f32[1024]{0:T(1024)S(1)}, u32[]{:S(2)}) copy-start(f32[1024]{0:T(1024)S(1)} %broadcast_multiply_fusion.2) | copy-start | bytes 12292
  673.8 276.1 %copy-start.53 = (f32[1024]{0:T(1024)}, f32[1024]{0:T(1024)S(1)}, u32[]{:S(2)}) copy-start(f32[1024]{0:T(1024)S(1)} %fusion.143) | copy-start | bytes 12292
  678.3 80.8 %all-to-all-start.2 = ((bf16[16,256,192]{1,2,0:T(8,128)(2,1)}), bf16[16,256,192]{1,2,0:T(8,128)(2,1)S(1)}, u32[]{:S(2)}, u32[]{:S(2)}) async-start(bf16[16,256,192]{1,2,0:T(8,128)(2,1)} %bitcast.491), calls=%async_computation.2 | async-start | bytes 3145728 | tf_op jit(solution)/shard_map/all_to_all | solution.py:329
  683.2 275.0 %all-gather.23.cloned.1.call-start = ((), (), s32[]{:S(2)}) async-start(), calls=%async_computation.33 | async-start | bytes 5308416 | tf_op jit(solution)/shard_map/all_gather | solution.py:304
  868.5 56.1 %all-to-all-start.3 = ((bf16[16,2,24576]{2,1,0:T(2,128)(2,1)}), bf16[16,2,24576]{2,1,0:T(2,128)(2,1)S(1)}, u32[]{:S(2)}, u32[]{:S(2)}) async-start(bf16[16,2,24576]{2,1,0:T(2,128)(2,1)} %reshape.994), calls=%async_computation.3 | async-start | bytes 3145728 | tf_op jit(solution)/shard_map/all_to_all | solution.py:332
  873.3 123.0 %all-gather.25.cloned.1.call-start = ((), (), s32[]{:S(2)}) async-start(), calls=%async_computation.34 | async-start | bytes 5308416 | tf_op jit(solution)/shard_map/all_gather | solution.py:305
  1049.3 43.4 %all-to-all-start.4 = ((bf16[16,256,192]{1,2,0:T(8,128)(2,1)}), bf16[16,256,192]{1,2,0:T(8,128)(2,1)S(1)}, u32[]{:S(2)}, u32[]{:S(2)}) async-start(bf16[16,256,192]{1,2,0:T(8,128)(2,1)} %bitcast.492), calls=%async_computation.4 | async-start | bytes 3145728 | tf_op jit(solution)/shard_map/all_to_all | solution.py:329
  1180.9 142.3 %all-to-all-start.5 = ((bf16[16,2,24576]{2,1,0:T(2,128)(2,1)}), bf16[16,2,24576]{2,1,0:T(2,128)(2,1)}, u32[]{:S(2)}, u32[]{:S(2)}) async-start(bf16[16,2,24576]{2,1,0:T(2,128)(2,1)} %reshape.996), calls=%async_computation.5 | async-start | bytes 3145728 | tf_op jit(solution)/shard_map/all_to_all | solution.py:332
  1284.9 641.3 %reduce-scatter.45.cloned.1.call-start = ((), (), s32[]{:S(2)}) async-start(), calls=%async_computation.43 | async-start | bytes 1327104 | tf_op jit(solution)/shard_map/reduce_scatter | solution.py:553
  1288.9 791.0 %reduce-scatter.39.cloned.1.call-start = ((), (), s32[]{:S(2)}) async-start(), calls=%async_computation.40 | async-start | bytes 1327104 | tf_op jit(solution)/shard_map/reduce_scatter | solution.py:544
  1370.0 42.6 %all-to-all-start.6 = ((bf16[16,256,192]{1,2,0:T(8,128)(2,1)}), bf16[16,256,192]{1,2,0:T(8,128)(2,1)}, u32[]{:S(2)}, u32[]{:S(2)}) async-start(bf16[16,256,192]{1,2,0:T(8,128)(2,1)} %bitcast.86), calls=%async_computation.6 | async-start | bytes 3145728 | tf_op jit(solution)/shard_map/all_to_all | solution.py:329
  1374.4 707.4 %reduce-scatter.37.cloned.1.call-start = ((), (), s32[]{:S(2)}) async-start(), calls=%async_computation.39 | async-start | bytes 1327104 | tf_op jit(solution)/shard_map/reduce_scatter | solution.py:541
  1386.7 698.5 %reduce-scatter.51.cloned.1.call-start = ((), (), s32[]{:S(2)}) async-start(), calls=%async_computation.46 | async-start | bytes 5308416 | tf_op jit(solution)/shard_map/reduce_scatter | solution.py:559
  1616.4 299.3 %copy-start.52 = (f32[1024]{0:T(1024)S(1)}, f32[1024]{0:T(1024)}, u32[]{:S(2)}) copy-start(f32[1024]{0:T(1024)} %copy-done.51) | copy-start | bytes 12292
  1616.4 299.3 %copy-start.65 = (f32[1024]{0:T(1024)S(1)}, f32[1024]{0:T(1024)}, u32[]{:S(2)}) copy-start(f32[1024]{0:T(1024)} %copy-done.64) | copy-start | bytes 12292
  1616.4 299.3 %copy-start.67 = (f32[768]{0:T(1024)S(1)}, f32[768]{0:T(1024)}, u32[]{:S(2)}) copy-start(f32[768]{0:T(1024)} %copy-done.66) | copy-start | bytes 9220
  1616.4 299.3 %copy-start.81 = (f32[768]{0:T(1024)S(1)}, f32[768]{0:T(1024)}, u32[]{:S(2)}) copy-start(f32[768]{0:T(1024)} %copy-done.80) | copy-start | bytes 9220
  1616.4 404.9 %all-to-all-start.7 = ((bf16[16,2,73728]{2,1,0:T(2,128)(2,1)}), bf16[16,2,73728]{2,1,0:T(2,128)(2,1)}, u32[]{:S(2)}, u32[]{:S(2)}) async-start(bf16[16,2,73728]{2,1,0:T(2,128)(2,1)} %reshape.998), calls=%async_computation.7 | async-start | bytes 9437184 | tf_op jit(solution)/shard_map/all_to_all | solution.py:332
  1915.6 187.9 %reduce-scatter.47.cloned.1.call-start = ((), (), s32[]{:S(2)}) async-start(), calls=%async_computation.44 | async-start | bytes 5308416 | tf_op jit(solution)/shard_map/reduce_scatter | solution.py:556
  1926.2 208.2 %reduce-scatter.65.cloned.1.call-start = ((), (), s32[]{:S(2)}) async-start(), calls=%async_computation.53 | async-start | bytes 245760
  1928.1 253.0 %reduce-scatter.41.cloned.1.call-start = ((), (), s32[]{:S(2)}) async-start(), calls=%async_computation.41 | async-start | bytes 442368 | tf_op jit(solution)/shard_map/reduce_scatter | solution.py:547
  1931.5 286.4 %reduce-scatter.43.cloned.1.call-start = ((), (), s32[]{:S(2)}) async-start(), calls=%async_computation.42 | async-start | bytes 442368 | tf_op jit(solution)/shard_map/reduce_scatter | solution.py:550
  1934.4 290.2 %all-reduce.6.cloned.1.call-start = ((), (), s32[]{:S(2)}) async-start(), calls=%async_computation.35 | async-start | bytes 3145728 | tf_op jit(solution)/shard_map/psum | solution.py:476
  1937.0 400.2 %reduce-scatter.55.cloned.1.call-start = ((), (), s32[]{:S(2)}) async-start(), calls=%async_computation.48 | async-start | bytes 1327104
  2079.9 259.6 %reduce-scatter.63.cloned.1.call-start = ((), (), s32[]{:S(2)}) async-start(), calls=%async_computation.52 | async-start | bytes 245760
  2081.7 265.7 %reduce-scatter.61.cloned.1.call-start = ((), (), s32[]{:S(2)}) async-start(), calls=%async_computation.51 | async-start | bytes 245760
  2083.5 281.7 %reduce-scatter.57.cloned.1.call-start = ((), (), s32[]{:S(2)}) async-start(), calls=%async_computation.49 | async-start | bytes 1327104
  2085.1 304.5 %reduce-scatter.53.cloned.1.call-start = ((), (), s32[]{:S(2)}) async-start(), calls=%async_computation.47 | async-start | bytes 737280 | tf_op jit(solution)/shard_map/reduce_scatter | solution.py:594
  2085.8 326.4 %reduce-scatter.49.cloned.1.call-start = ((), (), s32[]{:S(2)}) async-start(), calls=%async_computation.45 | async-start | bytes 737280 | tf_op jit(solution)/shard_map/reduce_scatter | solution.py:591
  2103.5 347.1 %reduce-scatter.59.cloned.1.call-start = ((), (), s32[]{:S(2)}) async-start(), calls=%async_computation.50 | async-start | bytes 1327104
  2105.1 367.6 %reduce-scatter.31.cloned.1.call-start = ((), (), s32[]{:S(2)}) async-start(), calls=%async_computation.36 | async-start | bytes 245760 | tf_op jit(solution)/shard_map/reduce_scatter | solution.py:573
  2338.9 154.3 %reduce-scatter.33.cloned.1.call-start = ((), (), s32[]{:S(2)}) async-start(), calls=%async_computation.37 | async-start | bytes 245760 | tf_op jit(solution)/shard_map/reduce_scatter | solution.py:576
  2367.0 146.0 %reduce-scatter.35.cloned.1.call-start = ((), (), s32[]{:S(2)}) async-start(), calls=%async_computation.38 | async-start | bytes 245760 | tf_op jit(solution)/shard_map/reduce_scatter | solution.py:579
  (81 other events, 1535.4 us)
Sparse Core Ops, SparseCore 0:
  25.5 25.4 all-gather.10
  53.4 24.0 all-gather.12
  80.0 24.0 all-gather.14
  233.3 23.3 all-gather.16
  259.1 24.0 all-gather.18
  608.2 31.0 all-gather.20
  732.3 39.9 all-gather.22
  922.4 39.3 all-gather.24
  1289.1 61.4 reduce-scatter.44
  1365.2 59.2 reduce-scatter.38
  1427.7 37.4 reduce-scatter.36
  1468.9 53.8 reduce-scatter.50
  1926.3 177.1 reduce-scatter.46
  2106.3 28.0 reduce-scatter.64
  2137.3 43.7 reduce-scatter.40
  2184.0 33.7 reduce-scatter.42
  2221.5 60.9 reduce-scatter.54
  2285.2 19.3 reduce-scatter.62
  2307.5 17.6 reduce-scatter.60
  2329.2 35.9 reduce-scatter.56
  2367.5 22.0 reduce-scatter.52
  2391.8 20.3 reduce-scatter.48
  2415.5 35.0 reduce-scatter.58
  2453.4 19.3 reduce-scatter.30
  2475.6 17.5 reduce-scatter.32
  2495.4 17.4 reduce-scatter.34
Sparse Core Ops, SparseCore 1:
  558.3 89.5 all-reduce.3
  1937.9 235.1 all-reduce.5
where the time goes:
time: 2560 us; the launch traced here: 2530 us
  starting transfers between devices  540 us (21%)
  blocking collectives  513 us (20%)
  local copies, waits for them, and re-layouts  421 us (16%)
  waiting for transfers between devices  413 us (16%)
  matrix products  298 us (12%)
  other arithmetic  294 us (11%)
  loops' own time  29.4 us (1%)
    all_to_all x4, starting transfers between devices, to_positions(): lax.all_to_all(sequences, ('ctx', 'tp'), split_axis=1, concat_axis=0, til...  518 us
    unnamed x9, other arithmetic  200 us
    all_to_all x4, waiting for transfers between devices, to_positions(): lax.all_to_all(sequences, ('ctx', 'tp'), split_axis=1, concat_axis=0, til...  118 us
    all_gather x1, blocking collectives, per_device(): lax.all_gather(part_out_self, 'tp', axis=0, tiled=True)  111 us
    unnamed x207, local copies, waits for them, and re-layouts  108 us
    psum x1, blocking collectives, per_device(): lax.psum((square_terms, gain_terms, bias_terms), ('shard', 'ctx', 'tp'))  94.2 us
  transfers between devices with their start and end apart: 36, of which 17 were waited for; matrix products, arithmetic and copies ran while one was open for 34% of the time, Pallas kernels for 0%

commit v1 on v0

v1 whole, which is shorter than its diff:
```python
import functools

import jax
import jax.numpy as jnp
from jax import lax
from jax.experimental import pallas as pl
from jax.experimental.pallas import tpu as pltpu
from jax.sharding import PartitionSpec as P

HEADS = 12
HEAD_DIM = 64
BLK = 256

EPSILON = 1e-05
NEGATIVE = -1e30
LOG2E = 1.4426950408889634
SCALING = HEAD_DIM**-0.5
QUERY_SCALE = SCALING * LOG2E

KEYS = 512
QUERIES = 1024
VMEM_LIMIT = 56 * 2**20

bf16 = jnp.bfloat16
f32 = jnp.float32


def dot_nn(left, right):
    return lax.dot_general(left, right, (((1,), (0,)), ((), ())), preferred_element_type=f32)


def dot_nt(left, right):
    return lax.dot_general(left, right, (((1,), (1,)), ((), ())), preferred_element_type=f32)


def row_index(rows, columns):
    return lax.broadcasted_iota(jnp.int32, (rows, columns), 0)


def place_index(rows, columns, start):
    return lax.broadcasted_iota(jnp.int32, (rows, columns), 1) + start


def three_parts(row, ones_row):
    high = row.astype(bf16).astype(f32)
    rest = row - high
    middle = rest.astype(bf16).astype(f32)
    lowest = rest - middle
    at = row_index(16, row.shape[1])
    last = jnp.where(at == 3, 1.0, 0.0) if ones_row else jnp.zeros_like(at, f32)
    rows = jnp.where(at == 0, high, jnp.where(at == 1, middle, jnp.where(at == 2, lowest, last)))
    return rows.astype(bf16)


def self_forward_kernel(length_ref, x_ref, out_ref, total_ref, keys, values, held):
    length = length_ref[pl.program_id(0)]
    places = x_ref.shape[2]
    quarter_tiles = out_ref.shape[3] // QUERIES
    per_query = QUERIES // KEYS
    half = BLK
    key_tiles = (length + KEYS - 1) // KEYS

    def prepare(tile, _):
        start = pl.multiple_of(tile * KEYS, KEYS)
        rows = x_ref[0, HEAD_DIM : 2 * HEAD_DIM, pl.ds(start, KEYS)].astype(f32)
        at, place = row_index(16, KEYS), place_index(16, KEYS, start)
        mask = jnp.where((at == 0) & (place >= length), NEGATIVE, 0.0)
        stacked = jnp.concatenate([rows, mask, jnp.zeros((48, KEYS), f32)], axis=0)
        keys[pl.ds(start, KEYS), :] = stacked.T.astype(bf16)
        values[0:HEAD_DIM, pl.ds(start, KEYS)] = x_ref[
            0, 2 * HEAD_DIM : 3 * HEAD_DIM, pl.ds(start, KEYS)
        ]
        return 0

    lax.fori_loop(0, key_tiles, prepare, 0)
    values[HEAD_DIM : HEAD_DIM + 16, :] = jnp.ones((16, places), bf16)

    def query_tile(index, _):
        first_query = pl.multiple_of(index * QUERIES, QUERIES)
        ones_row = jnp.where(row_index(16, QUERIES) == 0, 1.0, 0.0).astype(bf16)
        queries = jnp.concatenate(
            [x_ref[0, 0:HEAD_DIM, pl.ds(first_query, QUERIES)], ones_row, jnp.zeros((48, QUERIES), bf16)],
            axis=0,
        )

        def score(tile):
            start = pl.multiple_of(tile * KEYS, KEYS)
            scores = dot_nn(keys[pl.ds(start, KEYS), :], queries)
            held[lax.rem(tile, 2)] = scores
            return jnp.max(scores, axis=0, keepdims=True)

        def step(tile, carry):
            largest, total, next_largest = carry
            updated = jnp.maximum(largest, next_largest)
            start = pl.multiple_of(tile * KEYS, KEYS)
            chances = jnp.exp2(held[lax.rem(tile, 2)] - updated).astype(bf16)
            total = total * jnp.exp2(largest - updated) + dot_nn(
                values[:, pl.ds(start, KEYS)], chances
            )
            return updated, total, score(jnp.minimum(tile + 1, key_tiles - 1))

        largest = jnp.full((1, QUERIES), NEGATIVE, f32)
        total = jnp.zeros((HEAD_DIM + 16, QUERIES), f32)
        largest, total, _ = lax.fori_loop(
            0, jnp.minimum(index * per_query, key_tiles), step, (largest, total, score(0))
        )

        def part(low, high, start, size, largest, total):
            scores = dot_nn(keys[pl.ds(start, size), :], queries[:, low:high])
            before = largest[:, low:high]
            updated = jnp.maximum(before, jnp.max(scores, axis=0, keepdims=True))
            chances = jnp.exp2(scores - updated).astype(bf16)
            summed = dot_nn(values[:, pl.ds(start, size)], chances)
            return updated, total[:, low:high] * jnp.exp2(before - updated) + summed

        for at in range(per_query):

            def diagonal(_, carry):
                largest, total = carry
                low = at * KEYS
                start = pl.multiple_of(first_query + low, KEYS)
                pieces = [(largest[:, :low], total[:, :low])] if low else []
                pieces.append(part(low, low + half, start, half, largest, total))
                pieces.append(part(low + half, low + KEYS, start, KEYS, largest, total))
                if low + KEYS < QUERIES:
                    pieces.append(part(low + KEYS, QUERIES, start, KEYS, largest, total))
                return tuple(jnp.concatenate(piece, axis=1) for piece in zip(*pieces))

            present = (index * per_query + at < key_tiles).astype(jnp.int32)
            largest, total = lax.fori_loop(0, present, diagonal, (largest, total))
        row_total = total[HEAD_DIM : HEAD_DIM + 1]
        inner = pl.multiple_of(lax.rem(index, quarter_tiles) * QUERIES, QUERIES)
        out_ref[index // quarter_tiles, 0, :, pl.ds(inner, QUERIES)] = (
            total[:HEAD_DIM] / row_total
        ).astype(bf16)
        total_ref[0, :, pl.ds(first_query, QUERIES)] = largest + jnp.log2(row_total)
        return 0

    lax.fori_loop(0, places // QUERIES, query_tile, 0)


def self_forward(unit_lengths, projected, quarters):
    units, _, places = projected.shape
    return pl.pallas_call(
        self_forward_kernel,
        grid_spec=pltpu.PrefetchScalarGridSpec(
            num_scalar_prefetch=1,
            grid=(units,),
            in_specs=[pl.BlockSpec((1, 3 * HEAD_DIM, places), lambda u, n: (u, 0, 0))],
            out_specs=[
                pl.BlockSpec((quarters, 1, HEAD_DIM, places // quarters), lambda u, n: (0, u, 0, 0)),
                pl.BlockSpec((1, 1, places), lambda u, n: (u, 0, 0)),
            ],
            scratch_shapes=[
                pltpu.VMEM((places, 128), bf16),
                pltpu.VMEM((HEAD_DIM + 16, places), bf16),
                pltpu.VMEM((2, KEYS, QUERIES), f32),
            ],
        ),
        out_shape=[
            jax.ShapeDtypeStruct((quarters, units, HEAD_DIM, places // quarters), bf16),
            jax.ShapeDtypeStruct((units, 1, places), f32),
        ],
        compiler_params=pltpu.CompilerParams(vmem_limit_bytes=VMEM_LIMIT),
        name="self_forward",
    )(unit_lengths, projected)


def self_backward_kernel(
    length_ref, x_ref, out_ref, back_ref, total_ref, grad_ref, keys, values, queries, backs, query_sum
):
    length = length_ref[pl.program_id(0)]
    places = x_ref.shape[2]
    quarter_tiles = out_ref.shape[3] // KEYS
    half = BLK
    key_tiles = (length + KEYS - 1) // KEYS

    def prepare(tile, _):
        start = pl.multiple_of(tile * KEYS, KEYS)
        key_rows = x_ref[0, HEAD_DIM : 2 * HEAD_DIM, pl.ds(start, KEYS)].astype(f32)
        value_rows = x_ref[0, 2 * HEAD_DIM : 3 * HEAD_DIM, pl.ds(start, KEYS)].astype(f32)
        at, place = row_index(16, KEYS), place_index(16, KEYS, start)
        ones = jnp.where(at < 3, 1.0, 0.0)
        mask = jnp.where((at == 3) & (place >= length), NEGATIVE, ones)
        blank = jnp.zeros((48, KEYS), f32)
        keys[pl.ds(start, KEYS), :] = jnp.concatenate([key_rows, mask, blank], axis=0).T.astype(bf16)
        values[pl.ds(start, KEYS), :] = jnp.concatenate([value_rows, ones, blank], axis=0).T.astype(
            bf16
        )
        blank = blank.astype(bf16)
        queries[:, pl.ds(start, KEYS)] = jnp.concatenate(
            [
                x_ref[0, 0:HEAD_DIM, pl.ds(start, KEYS)],
                three_parts(-total_ref[0, :, pl.ds(start, KEYS)], True),
                blank,
            ],
            axis=0,
        )
        inner = pl.multiple_of(lax.rem(tile, quarter_tiles) * KEYS, KEYS)
        back = back_ref[tile // quarter_tiles, 0, :, pl.ds(inner, KEYS)]
        out = out_ref[tile // quarter_tiles, 0, :, pl.ds(inner, KEYS)]
        delta = jnp.sum(back.astype(f32) * out.astype(f32), axis=0, keepdims=True)
        backs[:, pl.ds(start, KEYS)] = jnp.concatenate(
            [back, three_parts(-delta, False), blank], axis=0
        )
        query_sum[:, pl.ds(start, KEYS)] = jnp.zeros((HEAD_DIM, KEYS), f32)
        return 0

    lax.fori_loop(0, key_tiles, prepare, 0)

    def tile_terms(key_start, key_size, query_start, query_size, back_key, back_value):
        query = queries[:, pl.ds(query_start, query_size)]
        back = backs[:, pl.ds(query_start, query_size)]
        chances = jnp.exp2(dot_nn(keys[pl.ds(key_start, key_size), :], query))
        back_chances = dot_nn(values[pl.ds(key_start, key_size), :], back)
        back_scores = (chances * back_chances).astype(bf16)
        back_value = back_value + dot_nt(back[:HEAD_DIM], chances.astype(bf16))
        back_key = back_key + dot_nt(query[:HEAD_DIM], back_scores)
        query_sum[:, pl.ds(query_start, query_size)] += dot_nn(
            x_ref[0, HEAD_DIM : 2 * HEAD_DIM, pl.ds(key_start, key_size)], back_scores
        )
        return back_key, back_value

    def place_of(tile):
        inner = pl.multiple_of(lax.rem(tile, quarter_tiles) * KEYS, KEYS)
        return tile // quarter_tiles, inner

    def key_tile(index, _):
        start = pl.multiple_of(index * KEYS, KEYS)
        second = pl.multiple_of(start + half, half)
        blank = jnp.zeros((HEAD_DIM, half), f32)
        first_part = tile_terms(start, half, start, KEYS, blank, blank)
        second_part = tile_terms(second, half, second, half, blank, blank)
        begun = tuple(jnp.concatenate(pair, axis=1) for pair in zip(first_part, second_part))

        def step(tile, carry):
            return tile_terms(start, KEYS, pl.multiple_of(tile * KEYS, KEYS), KEYS, *carry)

        back_key, back_value = lax.fori_loop(index + 1, key_tiles, step, begun)
        quarter, inner = place_of(index)
        grad_ref[quarter, 0, HEAD_DIM : 2 * HEAD_DIM, pl.ds(inner, KEYS)] = (
            back_key * (1.0 / LOG2E)
        ).astype(bf16)
        grad_ref[quarter, 0, 2 * HEAD_DIM : 3 * HEAD_DIM, pl.ds(inner, KEYS)] = back_value.astype(
            bf16
        )
        return 0

    lax.fori_loop(0, key_tiles, key_tile, 0)

    def finish(tile, _):
        quarter, inner = place_of(tile)
        start = pl.multiple_of(tile * KEYS, KEYS)
        grad_ref[quarter, 0, 0:HEAD_DIM, pl.ds(inner, KEYS)] = (
            query_sum[:, pl.ds(start, KEYS)] * SCALING
        ).astype(bf16)
        return 0

    lax.fori_loop(0, key_tiles, finish, 0)

    def clear(tile, _):
        quarter, inner = place_of(tile)
        grad_ref[quarter, 0, :, pl.ds(inner, KEYS)] = jnp.zeros((3 * HEAD_DIM, KEYS), bf16)
        return 0

    lax.fori_loop(key_tiles, places // KEYS, clear, 0)


def self_backward(unit_lengths, projected, attended, back, totals):
    units, _, places = projected.shape
    quarters = attended.shape[0]
    quarter = places // quarters
    spread = pl.BlockSpec((quarters, 1, HEAD_DIM, quarter), lambda u, n: (0, u, 0, 0))
    return pl.pallas_call(
        self_backward_kernel,
        grid_spec=pltpu.PrefetchScalarGridSpec(
            num_scalar_prefetch=1,
            grid=(units,),
            in_specs=[
                pl.BlockSpec((1, 3 * HEAD_DIM, places), lambda u, n: (u, 0, 0)),
                spread,
                spread,
                pl.BlockSpec((1, 1, places), lambda u, n: (u, 0, 0)),
            ],
            out_specs=pl.BlockSpec((quarters, 1, 3 * HEAD_DIM, quarter), lambda u, n: (0, u, 0, 0)),
            scratch_shapes=[
                pltpu.VMEM((places, 128), bf16),
                pltpu.VMEM((places, 128), bf16),
                pltpu.VMEM((128, places), bf16),
                pltpu.VMEM((128, places), bf16),
                pltpu.VMEM((HEAD_DIM, places), f32),
            ],
        ),
        out_shape=jax.ShapeDtypeStruct((quarters, units, 3 * HEAD_DIM, quarter), bf16),
        compiler_params=pltpu.CompilerParams(vmem_limit_bytes=VMEM_LIMIT),
        name="self_backward",
    )(unit_lengths, projected, attended, back, totals)


def cross_forward_kernel(query_ref, pair_ref, out_ref, total_ref):
    places = query_ref.shape[1]
    keys = pair_ref[0, 0, 0:HEAD_DIM, :].astype(f32).T.astype(bf16)
    values = jnp.concatenate(
        [pair_ref[0, 0, HEAD_DIM:, :], jnp.ones((16, pair_ref.shape[3]), bf16)], axis=0
    )
    for start in range(0, places, KEYS):
        scores = dot_nn(keys, query_ref[:, start : start + KEYS])
        largest = jnp.max(scores, axis=0, keepdims=True)
        chances = jnp.exp2(scores - largest).astype(bf16)
        total = dot_nn(values, chances)
        row_total = total[HEAD_DIM : HEAD_DIM + 1]
        out_ref[:, start : start + KEYS] = (total[:HEAD_DIM] / row_total).astype(bf16)
        total_ref[0, :, start : start + KEYS] = largest + jnp.log2(row_total)


def cross_forward(queries, pairs):
    width, places = queries.shape
    units = pairs.shape[1]
    rows = pl.BlockSpec((HEAD_DIM, places), lambda h: (h, 0))
    return pl.pallas_call(
        cross_forward_kernel,
        grid=(width // HEAD_DIM,),
        in_specs=[
            rows,
            pl.BlockSpec((1, 1) + pairs.shape[2:], lambda h: (h // units, h % units, 0, 0)),
        ],
        out_specs=[rows, pl.BlockSpec((1, 1, places), lambda h: (h, 0, 0))],
        out_shape=[
            jax.ShapeDtypeStruct((width, places), bf16),
            jax.ShapeDtypeStruct((width // HEAD_DIM, 1, places), f32),
        ],
        compiler_params=pltpu.CompilerParams(vmem_limit_bytes=VMEM_LIMIT),
        name="cross_forward",
    )(queries, pairs)


def cross_backward_kernel(query_ref, pair_ref, out_ref, back_ref, total_ref, grad_ref, pair_grad_ref):
    places = query_ref.shape[1]
    rows = pair_ref.shape[3]
    at = row_index(64, rows)
    ones = jnp.where(at < 3, 1.0, 0.0)
    key_major = pair_ref[0, 0, 0:HEAD_DIM, :]
    keys = jnp.concatenate([key_major.astype(f32), ones], axis=0).T.astype(bf16)
    values = jnp.concatenate([pair_ref[0, 0, HEAD_DIM:, :].astype(f32), ones], axis=0).T.astype(bf16)
    blank = jnp.zeros((48, KEYS), bf16)
    back_key = jnp.zeros((HEAD_DIM, rows), f32)
    back_value = jnp.zeros((HEAD_DIM, rows), f32)
    for start in range(0, places, KEYS):
        span = slice(start, start + KEYS)
        plain, back = query_ref[:, span], back_ref[:, span]
        query = jnp.concatenate([plain, three_parts(-total_ref[0, :, span], False), blank], axis=0)
        delta = jnp.sum(back.astype(f32) * out_ref[:, span].astype(f32), axis=0, keepdims=True)
        back_rows = jnp.concatenate([back, three_parts(-delta, False), blank], axis=0)
        chances = jnp.exp2(dot_nn(keys, query))
        back_scores = (chances * dot_nn(values, back_rows)).astype(bf16)
        back_value = back_value + dot_nt(back, chances.astype(bf16))
        back_key = back_key + dot_nt(plain, back_scores)
        grad_ref[:, span] = (dot_nn(key_major, back_scores) * SCALING).astype(bf16)
    pair_grad_ref[0, 0, 0:HEAD_DIM, :] = (back_key * (1.0 / LOG2E)).astype(bf16)
    pair_grad_ref[0, 0, HEAD_DIM:, :] = back_value.astype(bf16)


def cross_backward(queries, pairs, attended, back, totals):
    width, places = queries.shape
    units = pairs.shape[1]
    rows = pl.BlockSpec((HEAD_DIM, places), lambda h: (h, 0))
    pair = pl.BlockSpec((1, 1) + pairs.shape[2:], lambda h: (h // units, h % units, 0, 0))
    return pl.pallas_call(
        cross_backward_kernel,
        grid=(width // HEAD_DIM,),
        in_specs=[rows, pair, rows, rows, pl.BlockSpec((1, 1, places), lambda h: (h, 0, 0))],
        out_specs=[rows, pair],
        out_shape=[
            jax.ShapeDtypeStruct((width, places), bf16),
            jax.ShapeDtypeStruct(pairs.shape, bf16),
        ],
        compiler_params=pltpu.CompilerParams(vmem_limit_bytes=VMEM_LIMIT),
        name="cross_backward",
    )(queries, pairs, attended, back, totals)


def layer_norm(summed, gain_row, bias_row):
    average = jnp.mean(summed, axis=-1, keepdims=True)
    centred = summed - average
    variance = jnp.mean(centred * centred, axis=-1, keepdims=True)
    return centred * lax.rsqrt(variance + EPSILON) * gain_row + bias_row


def gelu_exact(inner_act):
    return jax.nn.gelu(inner_act, approximate=False)


def product(spec, left, right):
    return jnp.einsum(spec, left, right, preferred_element_type=f32)


def per_device(
    hidden,
    bank,
    indices,
    lengths,
    cotangent,
    query_self,
    key_self,
    value_self,
    out_self,
    query_cross,
    key_cross,
    value_cross,
    out_cross,
    up_weight,
    down_weight,
    norm_gain,
    norm_bias,
):
    shard_count = lax.axis_size("shard")
    context_count = lax.axis_size("ctx")
    tensor_count = lax.axis_size("tp")
    shard_index = lax.axis_index("shard")
    context_index = lax.axis_index("ctx")
    tensor_index = lax.axis_index("tp")
    group_sequences, device_places, model_width = hidden.shape
    units = HEADS // context_count
    group_width = units * HEAD_DIM
    quarter = device_places * tensor_count
    shard_rows = query_self.shape[0]
    piece_rows = shard_rows // context_count

    swap = [
        (c * tensor_count + z, z * context_count + c)
        for c in range(context_count)
        for z in range(tensor_count)
    ]

    def to_plane(rows):
        received = lax.all_to_all(rows, "tp", split_axis=0, concat_axis=0, tiled=True)
        return received.reshape(quarter, rows.shape[-1])

    def from_plane(rows):
        blocks = rows.reshape(tensor_count, device_places, rows.shape[-1])
        return lax.all_to_all(blocks, "tp", split_axis=0, concat_axis=0, tiled=True)

    def over_context(parts):
        return lax.all_to_all(parts, "ctx", split_axis=0, concat_axis=0, tiled=True)

    group_lengths = lax.dynamic_slice_in_dim(
        lengths, shard_index * group_sequences, group_sequences
    )
    length = group_lengths[tensor_index]
    unit_lengths = jnp.full((units,), length, jnp.int32)

    def by_unit(weights):
        stacked = jnp.stack([w.reshape(-1, units, HEAD_DIM) for w in weights], axis=2)
        return stacked.reshape(weights[0].shape[0], -1)

    local_self = by_unit([query_self, key_self, value_self])
    local_pair = by_unit([key_cross, value_cross])
    self_width, pair_width = local_self.shape[1], local_pair.shape[1]
    own = lax.ppermute(jnp.concatenate([local_self, local_pair], axis=1), ("ctx", "tp"), swap)
    own = lax.all_gather(own, "shard", axis=0, tiled=True)
    own_self, own_pair = own[:, :self_width], own[:, self_width:]

    def gather_all(columns):
        rows = lax.dynamic_slice_in_dim(columns, context_index * piece_rows, piece_rows, 0)
        everything = lax.all_gather(rows, ("tp", "shard", "ctx"), axis=0, tiled=True)
        return everything.reshape(tensor_count, model_width, columns.shape[1])

    norms = jnp.concatenate([norm_gain, norm_bias], axis=0).T
    bundle = gather_all(
        jnp.concatenate([out_self.T, query_cross, out_cross.T, local_self, norms], axis=1)
    )
    out_self_t = bundle[:, :, :group_width]
    query_cross_w = bundle[:, :, group_width : 2 * group_width]
    out_cross_t = bundle[:, :, 2 * group_width : 3 * group_width]
    self_w = bundle[:, :, 3 * group_width : 3 * group_width + self_width]
    norm_rows = bundle[0, :, 3 * group_width + self_width :].T.astype(f32)
    gain_rows, bias_rows = norm_rows[:3], norm_rows[3:]
    feed = gather_all(jnp.concatenate([up_weight, down_weight.T], axis=1))
    feed_width = up_weight.shape[1]
    up_w, down_t = feed[:, :, :feed_width], feed[:, :, feed_width:]

    places = context_index * quarter + jnp.arange(quarter, dtype=jnp.int32)
    valid_rows = (places < length).astype(f32)[:, None]

    x_low = to_plane(hidden)
    x_all = lax.all_gather(x_low, "ctx", axis=0, tiled=True)
    query_scale = jnp.where(jnp.arange(3 * HEAD_DIM) < HEAD_DIM, QUERY_SCALE, 1.0).astype(f32)
    projected = product("df,pd->fp", own_self, x_all).reshape(units, 3 * HEAD_DIM, -1)
    projected = (projected * query_scale[None, :, None]).astype(bf16)
    self_out, self_total = self_forward(unit_lengths, projected, context_count)
    self_att = over_context(self_out).reshape(context_count, group_width, quarter)

    bank_local = bank.shape[1]
    retrieved = indices.shape[1]
    owner_tensor = indices[0] // bank_local
    local_rows = indices[0] - owner_tensor * bank_local
    owned = (owner_tensor == tensor_index)[:, None]
    picked = jnp.where(owned, jnp.take(bank[0], local_rows, axis=0), jnp.zeros((), bf16))
    picked = lax.all_to_all(
        picked.reshape(tensor_count, -1, model_width), "tp", split_axis=0, concat_axis=0, tiled=True
    )
    picked = jnp.sum(picked.astype(f32), axis=0).astype(bf16)
    lists = lax.all_gather(picked, "ctx", axis=0, tiled=False)
    selected = lax.all_to_all(lists, "tp", split_axis=0, concat_axis=0, tiled=True).reshape(
        retrieved, model_width
    )
    own_pairs = product("df,kd->fk", own_pair, selected).astype(bf16)
    pairs = lax.all_gather(
        own_pairs.reshape(units, 2 * HEAD_DIM, retrieved), "ctx", axis=0, tiled=False
    )

    x_float = x_low.astype(f32)
    branch_one = product("tnp,tdn->pd", self_att, out_self_t)
    first_sum = x_float + branch_one
    first = layer_norm(first_sum, gain_rows[0], bias_rows[0])
    first_low = first.astype(bf16)
    cross_query = (product("tdn,pd->tnp", query_cross_w, first_low) * QUERY_SCALE).astype(bf16)
    cross_query = cross_query.reshape(HEADS * HEAD_DIM, quarter)
    cross_out, cross_total = cross_forward(cross_query, pairs)
    cross_att = cross_out.reshape(tensor_count, group_width, quarter)
    branch_two = product("tnp,tdn->pd", cross_att, out_cross_t)
    second_sum = first + branch_two
    second = layer_norm(second_sum, gain_rows[1], bias_rows[1])
    second_low = second.astype(bf16)
    inner_act = product("pd,tdf->tpf", second_low, up_w)
    active_float, gelu_pull = jax.vjp(gelu_exact, inner_act)
    active = active_float.astype(bf16)
    branch_three = product("tpf,tdf->pd", active, down_t)
    third_sum = second + branch_three
    output = layer_norm(third_sum, gain_rows[2], bias_rows[2])
    output = from_plane(output.astype(bf16))

    def valid_squares(matrix):
        return jnp.sum(valid_rows * matrix * matrix)

    square_terms = jnp.stack(
        [
            valid_squares(matrix)
            for matrix in (x_float, branch_one, first, branch_two, second, branch_three)
        ]
    )

    def norm_back(summed, layer_index, back_in):
        normed, pullback = jax.vjp(
            layer_norm, summed, gain_rows[layer_index], bias_rows[layer_index]
        )
        return pullback(back_in)

    back_output = to_plane(cotangent).astype(f32) * valid_rows
    back_third, gain_three, bias_three = norm_back(third_sum, 2, back_output)
    back_three = back_third.astype(bf16)
    back_active = product("pd,tdf->tpf", back_three, down_t)
    back_inner = gelu_pull(back_active)[0].astype(bf16)
    back_down = product("pd,tpf->tdf", back_three, active)
    back_up = product("pd,tpf->tdf", second_low, back_inner)
    back_second = back_third + product("tpf,tdf->pd", back_inner, up_w)
    back_second_sum, gain_two, bias_two = norm_back(second_sum, 1, back_second)
    back_two = back_second_sum.astype(bf16)
    back_cross = product("tdn,pd->tnp", out_cross_t, back_two).astype(bf16)
    back_out_cross = product("pd,tnp->tdn", back_two, cross_att)
    back_query, back_pairs = cross_backward(
        cross_query, pairs, cross_out, back_cross.reshape(cross_out.shape), cross_total
    )
    back_query = back_query.reshape(tensor_count, group_width, quarter)
    back_query_cross = product("pd,tnp->tdn", first_low, back_query)
    back_first = back_second_sum + product("tnp,tdn->pd", back_query, query_cross_w)
    back_first_sum, gain_one, bias_one = norm_back(first_sum, 0, back_first)
    back_one = back_first_sum.astype(bf16)
    back_self = product("tdn,pd->tnp", out_self_t, back_one).astype(bf16)
    back_out_self = product("pd,tnp->tdn", back_one, self_att)
    back_self = over_context(back_self.reshape(context_count, units, HEAD_DIM, quarter))

    back_pairs = jnp.sum(over_context(back_pairs).astype(f32), axis=0).astype(bf16)
    back_pairs = back_pairs.reshape(pair_width, retrieved)
    back_selected = product("fk,df->kd", back_pairs, own_pair).astype(bf16)
    back_selected = over_context(back_selected.reshape(context_count, -1, model_width))
    back_selected = jnp.sum(back_selected.astype(f32), axis=0).astype(bf16)
    back_lists = lax.all_gather(back_selected, "tp", axis=0, tiled=False)
    back_rows = over_context(back_lists).reshape(retrieved, model_width)
    back_rows = jnp.where(owned, back_rows.astype(f32), 0.0)
    back_bank = jnp.zeros(bank.shape[1:], f32).at[local_rows].add(back_rows)[None]

    back_projected = self_backward(unit_lengths, projected, self_out, back_self, self_total)
    back_parts = over_context(back_projected).reshape(context_count, self_width, quarter)
    back_hidden = back_first_sum + product("tfp,tdf->pd", back_parts, self_w)
    back_hidden = from_plane(back_hidden.astype(bf16)).astype(f32)

    def reduce_own(gradient):
        pieces = gradient.astype(bf16).reshape(shard_count * tensor_count, -1, gradient.shape[1])
        pieces = lax.all_to_all(pieces, ("shard", "tp"), split_axis=0, concat_axis=0, tiled=True)
        piece = jnp.sum(pieces.astype(f32), axis=0).astype(bf16)
        piece = lax.ppermute(piece, ("ctx", "tp"), swap)
        return lax.all_gather(piece, "ctx", axis=0, tiled=True)

    def reduce_all(gradient):
        rows = gradient.astype(bf16).reshape(tensor_count * model_width, gradient.shape[2])
        piece = lax.psum_scatter(rows, ("tp", "shard", "ctx"), scatter_dimension=0, tiled=True)
        return lax.all_gather(piece, "ctx", axis=0, tiled=True)

    back_pair_w = reduce_own(product("kd,fk->df", selected, back_pairs))
    back_feed = reduce_all(jnp.concatenate([back_up, back_down], axis=2))
    back_mixed = reduce_all(
        jnp.concatenate([back_out_self, back_query_cross, back_out_cross], axis=2)
    )
    back_self_w = reduce_own(
        product(
            "qpd,qfp->df",
            x_all.reshape(context_count, quarter, model_width),
            back_projected.reshape(context_count, self_width, quarter),
        )
    )

    def apart(stacked, count):
        split = stacked.reshape(shard_rows, units, count, HEAD_DIM)
        return [split[:, :, at].reshape(shard_rows, group_width).astype(f32) for at in range(count)]

    back_query_self, back_key_self, back_value_self = apart(back_self_w, 3)
    back_key_cross, back_value_cross = apart(back_pair_w, 2)
    back_mixed = back_mixed.astype(f32)
    back_feed = back_feed.astype(f32)

    square_total, gain_total, bias_total = lax.psum(
        (
            square_terms,
            jnp.stack([gain_one, gain_two, gain_three]),
            jnp.stack([bias_one, bias_two, bias_three]),
        ),
        ("shard", "ctx", "tp"),
    )
    token_total = jnp.sum(lengths).astype(f32) * model_width
    statistics = jnp.sqrt(square_total / token_total)
    back_gain = lax.dynamic_slice_in_dim(gain_total, shard_index * shard_rows, shard_rows, 1)
    back_bias = lax.dynamic_slice_in_dim(bias_total, shard_index * shard_rows, shard_rows, 1)
    return (
        output,
        back_hidden,
        back_bank,
        back_query_self,
        back_key_self,
        back_value_self,
        back_mixed[:, :group_width].T,
        back_mixed[:, group_width : 2 * group_width],
        back_key_cross,
        back_value_cross,
        back_mixed[:, 2 * group_width :].T,
        back_feed[:, :feed_width],
        back_feed[:, feed_width:].T,
        back_gain,
        back_bias,
        statistics,
    )


def solution(mesh):
    return jax.shard_map(
        per_device,
        mesh=mesh,
        in_specs=(
            P("shard", ("ctx", "tp"), None),
            P(("shard", "ctx"), "tp", None),
            P(("shard", "ctx"), None),
            P(),
            P("shard", ("ctx", "tp"), None),
            P("shard", "tp"),
            P("shard", "tp"),
            P("shard", "tp"),
            P("tp", "shard"),
            P("shard", "tp"),
            P("shard", "tp"),
            P("shard", "tp"),
            P("tp", "shard"),
            P("shard", "tp"),
            P("tp", "shard"),
            P(None, "shard"),
            P(None, "shard"),
        ),
        out_specs=(
            P("shard", ("ctx", "tp"), None),
            P("shard", ("ctx", "tp"), None),
            P(("shard", "ctx"), "tp", None),
            P("shard", "tp"),
            P("shard", "tp"),
            P("shard", "tp"),
            P("tp", "shard"),
            P("shard", "tp"),
            P("shard", "tp"),
            P("shard", "tp"),
            P("tp", "shard"),
            P("shard", "tp"),
            P("tp", "shard"),
            P(None, "shard"),
            P(None, "shard"),
            P(),
        ),
        check_vma=False,
    )
```

time: 2560 us -> 1120 us (0.44)
  starting transfers between devices: 540 us -> 98.2 us
  local copies, waits for them, and re-layouts: 421 us -> 74 us
  blocking collectives: 513 us -> 229 us
  other arithmetic: 294 us -> 63.5 us
  Pallas kernels: 0 us -> 171 us
  waiting for transfers between devices: 413 us -> 274 us
  matrix products: 298 us -> 181 us
  loops' own time: 29.4 us -> 0 us
    all_to_all x8 -> x10, starting transfers between devices: 538 us -> 95.4 us  [the longest x2 45.9 us: reduce_own(): lax.all_to_all(pieces, ('shard', 'tp'), split_axis=0, concat_axis=0, tile...]
    all_gather x22 -> x3, blocking collectives: 419 us -> 39.8 us  [the longest x2 32.4 us: reduce_own(): return lax.all_gather(piece, 'ctx', axis=0, tiled=True)]
    unnamed x9 -> x1, other arithmetic: 200 us -> 1.35 us
    pallas_call x0 -> x4, Pallas kernels: none -> 171 us  [the longest x1 55.3 us: self_backward(): pl.pallas_call(self_backward_kernel, grid_spec=pltpu.PrefetchScalarGridSp...]
    reduce_scatter x12 -> x2, waiting for transfers between devices: 160 us -> 0.01 us  [reduce_all(): lax.psum_scatter(rows, ('tp', 'shard', 'ctx'), scatter_dimension=0, tiled...]
    all_to_all x0 -> x4, blocking collectives: none -> 131 us  [the longest x3 87.4 us: over_context(): return lax.all_to_all(parts, 'ctx', split_axis=0, concat_axis=0, tiled=True)]
    dot_general x95 -> x21, matrix products: 298 us -> 181 us  [product(): return jnp.einsum(spec, left, right, preferred_element_type=f32)]
    unnamed x207 -> x119, local copies, waits for them, and re-layouts: 108 us -> 35.1 us
  transfers between devices with their start and end apart: 36 -> 23, of which waited for: 17 -> 12; matrix products, arithmetic and copies ran while one was open for 34% -> 21% of each run, Pallas kernels for 0% -> 12%
where the time goes in v1:
time: 1120 us; the launch traced here: 1110 us
  waiting for transfers between devices  274 us (24%)
  blocking collectives  229 us (20%)
  matrix products  181 us (16%)
  Pallas kernels  171 us (15%)
  starting transfers between devices  98.2 us (9%)
  local copies, waits for them, and re-layouts  74 us (7%)
  other arithmetic  63.5 us (6%)
  between operations  16.2 us (1%)
    dot_general x21, matrix products, product(): return jnp.einsum(spec, left, right, preferred_element_type=f32)  181 us
    all_to_all x3, blocking collectives, over_context(): return lax.all_to_all(parts, 'ctx', split_axis=0, concat_axis=0, tiled=True)  87.4 us
    all_gather x2, waiting for transfers between devices, gather_all(): lax.all_gather(rows, ('tp', 'shard', 'ctx'), axis=0, tiled=True)  65.5 us
    psum x1, blocking collectives, per_device(): lax.psum((square_terms, jnp.stack([gain_one, gain_two, gain_three]), jnp....  58.9 us
    all_to_all x3, waiting for transfers between devices, over_context(): return lax.all_to_all(parts, 'ctx', split_axis=0, concat_axis=0, tiled=True)  56.1 us
    pallas_call x1, Pallas kernels, self_backward(): pl.pallas_call(self_backward_kernel, grid_spec=pltpu.PrefetchScalarGridSp...  55.3 us
    pallas_call x1, Pallas kernels, self_forward(): pl.pallas_call(self_forward_kernel, grid_spec=pltpu.PrefetchScalarGridSpe...  53.4 us
    all_to_all x2, waiting for transfers between devices, to_plane(): lax.all_to_all(rows, 'tp', split_axis=0, concat_axis=0, tiled=True)  50.9 us
  transfers between devices with their start and end apart: 23, of which 12 were waited for; matrix products, arithmetic and copies ran while one was open for 21% of the time, Pallas kernels for 12%

profile of v1, /device:TPU:0, one launch (start us, length us, event | category | flops | bytes accessed | tf_op | source)
XLA Modules:
  0.0 1107.3 jit_solution(14552273648063053228)
XLA Ops:
  9.9 8.1 gather_fusion
  18.4 43.1 %all_to_all.70 = bf16[4,256,768]{2,1,0:T(8,128)(2,1)S(1)} all-to-all(bf16[4,256,768]{2,1,0:T(8,128)(2,1)S(1)} %select_select_fusion), channel_id=1, replica_groups=mesh['shard'=2,'ctx'=4,'tp'=4] {'tp'}, dimensions={0} | all-to-all | bytes 3145728 | tf_op jit(solution)/shard_map/all_to_all | solution.py:499
  68.2 50.9 %all-to-all-done = bf16[4,256,768]{2,1,0:T(8,128)(2,1)S(1)} async-done(((bf16[4,256,768]{2,1,0:T(8,128)(2,1)}), bf16[4,256,768]{2,1,0:T(8,128)(2,1)S(1)}, u32[]{:S(2)}, u32[]{:S(2)}) %all-to-all-start) | async-done | bytes 1572896 | tf_op jit(solution)/shard_map/all_to_all | solution.py:436
  121.7 16.6 %all-to-all-start.3 = ((bf16[4,256,768]{2,1,0:T(8,128)(2,1)}), bf16[4,256,768]{2,1,0:T(8,128)(2,1)S(1)}, u32[]{:S(2)}, u32[]{:S(2)}) async-start(bf16[4,256,768]{2,1,0:T(8,128)(2,1)} %bitcast.301), calls=%async_computation.3 | async-start | bytes 3145728 | tf_op jit(solution)/shard_map/all_to_all | solution.py:504
  138.3 20.9 %all-gather.11.cloned.1.call-done = bf16[768,960]{0,1:T(8,128)(2,1)} async-done(((bf16[384,960]{0,1:T(8,128)(2,1)}), bf16[768,960]{0,1:T(8,128)(2,1)}) %all-gather.11.cloned.1.call-update) | async-done | bytes 1474576 | tf_op jit(solution)/shard_map/all_gather | solution.py:460
  159.2 17.1 %all-to-all-done.3 = bf16[4,256,768]{2,1,0:T(8,128)(2,1)S(1)} async-done(((bf16[4,256,768]{2,1,0:T(8,128)(2,1)}), bf16[4,256,768]{2,1,0:T(8,128)(2,1)S(1)}, u32[]{:S(2)}, u32[]{:S(2)}) %all-to-all-start.3) | async-done | bytes 1572896 | tf_op jit(solution)/shard_map/all_to_all | solution.py:504
  181.2 26.5 %all-gather.13.cloned.1.call-done = bf16[4096,768]{1,0:T(8,128)(2,1)} async-done(((bf16[1024,768]{1,0:T(8,128)(2,1)}), bf16[4096,768]{1,0:T(8,128)(2,1)}) %all-gather.13.cloned.1.call-update) | async-done | bytes 6291472 | tf_op jit(solution)/shard_map/all_gather | solution.py:486
  207.8 6.2 fusion.66
  218.5 53.4 %self_forward.1 = (bf16[4,3,64,1024]{3,2,1,0:T(8,128)(2,1)}, f32[3,1,4096]{2,1,0:T(1,128)}) custom-call(s32[3]{0:T(128)} %broadcast_in_dim.85.length_ref, bf16[3,192,4096]{2,1,0:T(8,128)(2,1)} %multiply_convert_fusion.x_ref), custom_call_target="tpu_custom_call" | custom-call | tf_op jit(solution)/shard_map/self_forward/pallas_call | solution.py:144
  276.3 11.1 %all-gather.15.cloned.1.call-done = bf16[3072,1158]{1,0:T(8,128)(2,1)} async-done(((bf16[96,1158]{1,0:T(8,128)(2,1)}), bf16[3072,1158]{1,0:T(8,128)(2,1)}) %all-gather.15.cloned.1.call-update) | async-done | bytes 7114768 | tf_op jit(solution)/shard_map/all_gather | solution.py:465
  289.9 5.8 all-to-all-done.1
  295.7 9.1 all-to-all-start.5
  305.0 5.1 fusion.97
  311.7 5.5 multiply_convert_fusion.1
  320.0 25.7 %cross_forward.1 = (bf16[768,1024]{1,0:T(8,128)(2,1)}, f32[12,1,1024]{2,1,0:T(1,128)}) custom-call(bf16[768,1024]{1,0:T(8,128)(2,1)} %bitcast.282, bf16[4,3,128,1024]{3,2,1,0:T(8,128)(2,1)} %all-gather.17.cloned.1.call-done.pair_ref), custom_call_target="tpu_custom_call" | custom-call | tf_op jit(solution)/shard_map/cross_forward/pallas_call | solution.py:320
  345.7 6.0 fusion.96
  353.8 54.4 %all-gather.19.cloned.1.call-done = bf16[3072,1536]{1,0:T(8,128)(2,1)} async-done(((bf16[96,1536]{1,0:T(8,128)(2,1)}), bf16[3072,1536]{1,0:T(8,128)(2,1)}) %all-gather.19.cloned.1.call-update) | async-done | bytes 9437200 | tf_op jit(solution)/shard_map/all_gather | solution.py:465
  408.2 38.5 %fusion.9 = (bf16[4,1024,768]{1,2,0:T(8,128)(2,1)S(1)}, f32[4,1024,768]{1,2,0:T(8,128)}, f32[4,768,1024]{2,1,0:T(8,128)}) fusion(f32[1024,768]{1,0:T(8,128)} %copy-done.6, f32[768]{0:T(1024)S(1)} %get-tuple-element.88, f32[768]{0:T(1024)S(1)} %get-tuple-element.89, f32[1024]{0:T(1024)S(1)} %fusion.85, f32[1024]{0:T(1024)S(1)} %broadcast_multiply_fusion.1, ...), kind=kOutput, calls=%fused_computation.19 | convolution fusion | flops 5040242688 | bytes 39335936 | tf_op jit(solution)/shard_map/pd,tdf->tpf/dot_general | solution.py:394
  446.8 7.3 fusion.94
  461.6 17.5 %fusion.6 = bf16[4,1024,768]{1,2,0:T(8,128)(2,1)} fusion(f32[4,1024,768]{1,2,0:T(8,128)} %get-tuple-element.109, f32[4,768,1024]{2,1,0:T(8,128)} %get-tuple-element.126, bf16[4,768,1536]{2,1,0:T(8,128)(2,1)} %bitcast.331, f32[1024,768]{1,0:T(8,128)} %get-tuple-element.105, f32[1024]{0:T(1024)S(1)} %negate_multiply_fusion.3), kind=kOutput, calls=%fused_computation.11 | convolution fusion | flops 4877451264 | bytes 39325696 | tf_op jit(solution)/shard_map/pd,tdf->tpf/dot_general | solution.py:394
  479.1 15.8 %multiply_reduce_fusion.2 = (f32[768]{0:T(1024)S(1)}, f32[1024]{0:T(1024)S(1)}, f32[]{:T(128)}, f32[768]{0:T(1024)S(1)}, f32[]{:T(128)}, /*index=5*/f32[]{:T(128)}, f32[]{:T(128)}, f32[1024,768]{1,0:T(8,128)S(1)}) fusion(f32[1024,768]{1,0:T(8,128)S(1)} %copy-done.8, f32[1024]{0:T(1024)S(1)} %fusion.85, f32[1024]{0:T(1024)S(1)} %broadcast_multiply_fusion.1, ...), kind=kOutput, calls=%fused_computation.73 | convolution fusion | flops 4850709504 | bytes 29917200 | tf_op jit(solution)/shard_map/tpf,tdf->pd/dot_general | solution.py:394
  496.4 5.8 convolution_convert_fusion.4
  502.2 36.6 %cross_backward.1 = (bf16[768,1024]{1,0:T(8,128)(2,1)}, bf16[4,3,128,1024]{3,2,1,0:T(8,128)(2,1)}) custom-call(bf16[768,1024]{1,0:T(8,128)(2,1)} %bitcast.283, bf16[4,3,128,1024]{3,2,1,0:T(8,128)(2,1)} %all-gather.17.cloned.1.call-done.pair_ref, bf16[768,1024]{1,0:T(8,128)(2,1)} %get-tuple-element.23.out_ref, bf16[768,1024]{1,0:T(8,128)(2,1)} %bitcast.306, ...), custom_call_target="tpu_custom_call" | custom-call | tf_op jit(solution)/shard_map/cross_backward/pallas_call | solution.py:368
  538.8 40.6 %all_to_all.71 = bf16[4,3,128,1024]{3,2,1,0:T(8,128)(2,1)S(1)} all-to-all(bf16[4,3,128,1024]{3,2,1,0:T(8,128)(2,1)} %get-tuple-element.27), channel_id=1, replica_groups=mesh['shard'=2,'ctx'=4,'tp'=4] {'ctx'}, dimensions={0} | all-to-all | bytes 6291456 | tf_op jit(solution)/shard_map/all_to_all | solution.py:444
  583.4 23.6 %all_to_all.72 = bf16[4,256,768]{2,1,0:T(8,128)(2,1)} all-to-all(bf16[4,256,768]{2,1,0:T(8,128)(2,1)S(1)} %bitcast.302), channel_id=1, replica_groups=mesh['shard'=2,'ctx'=4,'tp'=4] {'ctx'}, dimensions={0} | all-to-all | bytes 3145728 | tf_op jit(solution)/shard_map/all_to_all | solution.py:444
  609.6 10.3 convolution_convert_fusion.1
  619.9 6.8 copy.93
  626.7 9.7 convolution_convert_fusion
  636.4 6.6 copy.94
  643.0 9.1 pad_maximum_fusion
  652.1 12.7 %copy.117 = bf16[3072,1536]{1,0:T(8,128)(2,1)} copy(bf16[3072,1536]{0,1:T(8,128)(2,1)} %pad_maximum_fusion) | data formatting | bytes 18874368
  666.7 8.2 multiply_reduce_fusion.3
  681.3 23.3 %all_to_all.73.back_ref = bf16[4,3,64,1024]{3,2,1,0:T(8,128)(2,1)} all-to-all(bf16[4,3,64,1024]{3,2,1,0:T(8,128)(2,1)S(1)} %bitcast.303), channel_id=1, replica_groups=mesh['shard'=2,'ctx'=4,'tp'=4] {'ctx'}, dimensions={0} | all-to-all | bytes 3145728 | tf_op jit(solution)/shard_map/all_to_all | solution.py:444
  708.9 55.3 %self_backward.1 = bf16[4,3,192,1024]{3,2,1,0:T(8,128)(2,1)} custom-call(s32[3]{0:T(128)} %broadcast_in_dim.85.length_ref, bf16[3,192,4096]{2,1,0:T(8,128)(2,1)} %multiply_convert_fusion.x_ref, bf16[4,3,64,1024]{3,2,1,0:T(8,128)(2,1)} %get-tuple-element.22.out_ref, bf16[4,3,64,1024]{3,2,1,0:T(8,128)(2,1)} %all_to_all.73.back_ref, ...), custom_call_target="tpu_custom_call" | custom-call | tf_op jit(solution)/shard_map/self_backward/pallas_call | solution.py:274
  764.2 9.1 fusion.65
  775.6 41.7 %all-to-all-start.12 = ((bf16[8,96,576]{2,1,0:T(8,128)(2,1)}), bf16[8,96,576]{2,1,0:T(8,128)(2,1)}, u32[]{:S(2)}, u32[]{:S(2)}) async-start(bf16[8,96,576]{2,1,0:T(8,128)(2,1)} %bitcast.292), calls=%async_computation.12 | async-start | bytes 1966080 | tf_op jit(solution)/shard_map/all_to_all | solution.py:590
  820.7 25.5 %all-to-all-done.12 = bf16[8,96,576]{2,1,0:T(8,128)(2,1)} async-done(((bf16[8,96,576]{2,1,0:T(8,128)(2,1)}), bf16[8,96,576]{2,1,0:T(8,128)(2,1)}, u32[]{:S(2)}, u32[]{:S(2)}) %all-to-all-start.12) | async-done | bytes 884768 | tf_op jit(solution)/shard_map/all_to_all | solution.py:590
  850.4 5.0 fusion.56
  858.1 8.5 all-to-all-done.13
  866.6 4.9 all-to-all-start.7
  887.2 38.2 %all-to-all-done.7 = bf16[4,3,192,1024]{3,2,1,0:T(8,128)(2,1)} async-done(((bf16[4,3,192,1024]{3,2,1,0:T(8,128)(2,1)}), bf16[4,3,192,1024]{3,2,1,0:T(8,128)(2,1)}, u32[]{:S(2)}, u32[]{:S(2)}) %all-to-all-start.7) | async-done | bytes 4718624 | tf_op jit(solution)/shard_map/all_to_all | solution.py:444
  929.0 11.8 %fusion.39 = bf16[1024,768]{1,0:T(8,128)(2,1)} fusion(f32[1024,768]{1,0:T(8,128)} %copy-done.12, bf16[4,576,1024]{2,1,0:T(8,128)(2,1)} %bitcast.45, bf16[4,768,1158]{2,1,0:T(8,128)(2,1)} %bitcast.329, f32[1024]{0:T(1024)S(1)} %negate_multiply_fusion.1), kind=kOutput, calls=%fused_computation.64 | convolution fusion | flops 3626237952 | bytes 13373440 | tf_op jit(solution)/shard_map/tfp,tdf->pd/dot_general | solution.py:394
  940.8 12.2 %all-to-all-done.11 = bf16[4,256,768]{2,1,0:T(8,128)(2,1)S(1)} async-done(((bf16[4,256,768]{2,1,0:T(8,128)(2,1)}), bf16[4,256,768]{2,1,0:T(8,128)(2,1)S(1)}, u32[]{:S(2)}, u32[]{:S(2)}) %all-to-all-start.11) | async-done | bytes 1572896 | tf_op jit(solution)/shard_map/all_to_all | solution.py:444
  960.6 58.9 %all-reduce = (f32[3,768]{1,0:T(4,128)S(1)}, f32[3,768]{1,0:T(4,128)S(1)}, f32[6]{0:T(128)S(1)}) all-reduce(f32[3,768]{1,0:T(4,128)S(1)} %pad_maximum_fusion.5, f32[3,768]{1,0:T(4,128)S(1)} %pad_maximum_fusion.6, f32[6]{0:T(128)S(1)} %stack.49), channel_id=1, replica_groups=mesh['shard'=2,'ctx'=4,'tp'=4] {'shard','ctx','tp'}, use_global_device_ids=true, to_apply=%region_23.24 | all-reduce | flops 4614 | bytes 36912 | tf_op jit(solution)/shard_map/psum | solution.py:622
  1022.7 19.1 %all_gather.48 = bf16[384,576]{1,0:T(8,128)(2,1)} all-gather(bf16[96,576]{1,0:T(8,128)(2,1)S(1)} %collective-permute-done.1), channel_id=1, replica_groups=mesh['shard'=2,'ctx'=4,'tp'=4] {'ctx'}, dimensions={0}, use_global_device_ids=true | all-gather | bytes 552960 | tf_op jit(solution)/shard_map/all_gather | solution.py:593
  1048.4 13.3 %all_gather.50 = bf16[384,384]{1,0:T(8,128)(2,1)} all-gather(bf16[96,384]{1,0:T(8,128)(2,1)S(1)} %collective-permute-done.2), channel_id=1, replica_groups=mesh['shard'=2,'ctx'=4,'tp'=4] {'ctx'}, dimensions={0}, use_global_device_ids=true | all-gather | bytes 368640 | tf_op jit(solution)/shard_map/all_gather | solution.py:593
  1063.7 7.4 all_gather.49
  1077.8 13.5 %scatter_custom_fusion = f32[4096,768]{1,0:T(8,128)} fusion(s32[1024]{0:T(1024)} %bitcast.321, f32[]{:T(128)} %constant.47.clone.1, bf16[1024,768]{1,0:T(8,128)(2,1)S(1)} %bitcast.281, pred[1024]{0:T(1024)(128)(4,1)S(1)} %copy-done.44), kind=kCustom, calls=%fused_computation.35 | custom fusion | flops 2359296 | bytes 14157824 | tf_op jit(solution)/shard_map/scatter-add | solution.py:581
  (243 shorter events, 128.9 us)
Async XLA Ops:
  7.2 114.5 %all-gather.23.cloned.1.call-start = ((), (), s32[]{:S(2)}) async-start(), calls=%async_computation.22 | async-start | bytes 1966080 | tf_op jit(solution)/shard_map/all_gather | solution.py:503
  62.6 56.5 %all-to-all-start = ((bf16[4,256,768]{2,1,0:T(8,128)(2,1)}), bf16[4,256,768]{2,1,0:T(8,128)(2,1)S(1)}, u32[]{:S(2)}, u32[]{:S(2)}) async-start(bf16[4,256,768]{2,1,0:T(8,128)(2,1)} %param.17), calls=%async_computation | async-start | bytes 3145728 | tf_op jit(solution)/shard_map/all_to_all | solution.py:436
  66.2 54.2 %copy-start.25 = (bf16[192,384]{1,0:T(8,128)(2,1)S(1)}, bf16[192,384]{1,0:T(8,128)(2,1)}, u32[]{:S(2)}) copy-start(bf16[192,384]{1,0:T(8,128)(2,1)} %param.25) | copy-start | bytes 442372
  66.2 54.2 %copy-start.26 = (bf16[384,192]{0,1:T(8,128)(2,1)S(1)}, bf16[384,192]{0,1:T(8,128)(2,1)}, u32[]{:S(2)}) copy-start(bf16[384,192]{0,1:T(8,128)(2,1)} %param.26) | copy-start | bytes 442372
  66.2 54.2 %copy-start.27 = (bf16[192,384]{1,0:T(8,128)(2,1)S(1)}, bf16[192,384]{1,0:T(8,128)(2,1)}, u32[]{:S(2)}) copy-start(bf16[192,384]{1,0:T(8,128)(2,1)} %param.29) | copy-start | bytes 442372
  66.2 93.0 %all-gather.11.cloned.1.call-start = ((), (), s32[]{:S(2)}) async-start(), calls=%async_computation.16 | async-start | bytes 2211840 | tf_op jit(solution)/shard_map/all_gather | solution.py:460
  66.4 54.2 %copy-start.45 = (bf16[3,384]{1,0:T(4,128)(2,1)S(1)}, bf16[3,384]{1,0:T(4,128)(2,1)}, u32[]{:S(2)}) copy-start(bf16[3,384]{1,0:T(4,128)(2,1)} %param.33) | copy-start | bytes 6916
  66.4 54.2 %copy-start.46 = (bf16[3,384]{1,0:T(4,128)(2,1)S(1)}, bf16[3,384]{1,0:T(4,128)(2,1)}, u32[]{:S(2)}) copy-start(bf16[3,384]{1,0:T(4,128)(2,1)} %param.32) | copy-start | bytes 6916
  66.6 0.7 collective-permute-start
  68.2 139.6 %all-gather.13.cloned.1.call-start = ((), (), s32[]{:S(2)}) async-start(), calls=%async_computation.17 | async-start | bytes 7864320 | tf_op jit(solution)/shard_map/all_gather | solution.py:486
  120.3 167.1 %all-gather.15.cloned.1.call-start = ((), (), s32[]{:S(2)}) async-start(), calls=%async_computation.18 | async-start | bytes 8110080 | tf_op jit(solution)/shard_map/all_gather | solution.py:465
  121.7 57.9 %copy-start.20 = (bf16[768,384]{1,0:T(8,128)(2,1)S(1)}, bf16[768,384]{1,0:T(8,128)(2,1)}, u32[]{:S(2)}) copy-start(bf16[768,384]{1,0:T(8,128)(2,1)} %param.31) | copy-start | bytes 1769476
  121.7 54.6 %all-to-all-start.3 = ((bf16[4,256,768]{2,1,0:T(8,128)(2,1)}), bf16[4,256,768]{2,1,0:T(8,128)(2,1)S(1)}, u32[]{:S(2)}, u32[]{:S(2)}) async-start(bf16[4,256,768]{2,1,0:T(8,128)(2,1)} %bitcast.301), calls=%async_computation.3 | async-start | bytes 3145728 | tf_op jit(solution)/shard_map/all_to_all | solution.py:504
  138.3 41.5 %copy-start.21 = (bf16[384,768]{1,0:T(8,128)(2,1)S(1)}, bf16[384,768]{1,0:T(8,128)(2,1)}, u32[]{:S(2)}) copy-start(bf16[384,768]{1,0:T(8,128)(2,1)} %param.30) | copy-start | bytes 1769476
  138.3 181.7 %all-gather.17.cloned.1.call-start = ((), (), s32[]{:S(2)}) async-start(), calls=%async_computation.19 | async-start | bytes 3932160 | tf_op jit(solution)/shard_map/all_gather | solution.py:508
  179.5 228.7 %all-gather.19.cloned.1.call-start = ((), (), s32[]{:S(2)}) async-start(), calls=%async_computation.20 | async-start | bytes 9732096 | tf_op jit(solution)/shard_map/all_gather | solution.py:465
  271.9 33.1 %copy-start.1 = (bf16[4,256,768]{2,1,0:T(8,128)(2,1)S(1)}, bf16[4,256,768]{2,1,0:T(8,128)(2,1)}, u32[]{:S(2)}) copy-start(bf16[4,256,768]{2,1,0:T(8,128)(2,1)} %copy-done) | copy-start | bytes 4718596
  271.9 23.7 %all-to-all-start.1 = ((bf16[4,3,64,1024]{3,2,1,0:T(8,128)(2,1)}), bf16[4,3,64,1024]{3,2,1,0:T(8,128)(2,1)S(1)}, u32[]{:S(2)}, u32[]{:S(2)}) async-start(bf16[4,3,64,1024]{3,2,1,0:T(8,128)(2,1)} %get-tuple-element.22.out_ref), calls=%async_computation.1 | async-start | bytes 3145728 | tf_op jit(solution)/shard_map/all_to_all | solution.py:444
  289.9 55.8 %copy-start.37 = (f32[768]{0:T(1024)}, f32[768]{0:T(1024)S(1)}, u32[]{:S(2)}) copy-start(f32[768]{0:T(1024)S(1)} %get-tuple-element.91) | copy-start | bytes 9220
  289.9 55.8 %copy-start.42 = (f32[768]{0:T(1024)}, f32[768]{0:T(1024)S(1)}, u32[]{:S(2)}) copy-start(f32[768]{0:T(1024)S(1)} %get-tuple-element.90) | copy-start | bytes 9220
  295.7 14.4 %copy-start.16 = (bf16[4,3,64,1024]{3,2,1,0:T(8,128)(2,1)}, bf16[4,3,64,1024]{3,2,1,0:T(8,128)(2,1)S(1)}, u32[]{:S(2)}) copy-start(bf16[4,3,64,1024]{3,2,1,0:T(8,128)(2,1)S(1)} %all-to-all-done.1) | copy-start | bytes 4718596
  295.7 158.9 %all-to-all-start.5 = ((bf16[4,256,768]{2,1,0:T(8,128)(2,1)}), bf16[4,256,768]{2,1,0:T(8,128)(2,1)}, u32[]{:S(2)}, u32[]{:S(2)}) async-start(bf16[4,256,768]{2,1,0:T(8,128)(2,1)} %param.21), calls=%async_computation.5 | async-start | bytes 3145728 | tf_op jit(solution)/shard_map/all_to_all | solution.py:436
  304.8 620.6 %all-gather.25.cloned.1.call-start = ((), (), s32[]{:S(2)}) async-start(), calls=%async_computation.23 | async-start | bytes 1966080 | tf_op jit(solution)/shard_map/all_gather | solution.py:578
  310.1 35.6 %copy-start.30 = (f32[1024]{0:T(1024)}, f32[1024]{0:T(1024)S(1)}, u32[]{:S(2)}) copy-start(f32[1024]{0:T(1024)S(1)} %broadcast_multiply_fusion.2) | copy-start | bytes 12292
  310.6 6.6 copy-start.32
  310.6 35.1 %copy-start.35 = (f32[1024]{0:T(1024)}, f32[1024]{0:T(1024)S(1)}, u32[]{:S(2)}) copy-start(f32[1024]{0:T(1024)S(1)} %fusion.84) | copy-start | bytes 12292
  317.2 28.5 %copy-start.4 = (f32[1024,768]{1,0:T(8,128)S(1)}, f32[1024,768]{1,0:T(8,128)}, u32[]{:S(2)}) copy-start(f32[1024,768]{1,0:T(8,128)} %copy-done.3) | copy-start | bytes 9437188
  408.2 38.6 %copy-start.7 = (f32[1024,768]{1,0:T(8,128)S(1)}, f32[1024,768]{1,0:T(8,128)}, u32[]{:S(2)}) copy-start(f32[1024,768]{1,0:T(8,128)} %copy-done.6) | copy-start | bytes 9437188
  408.2 38.6 %copy-start.47 = (bf16[3072,1536]{1,0:T(8,128)(2,1)S(1)}, bf16[3072,1536]{1,0:T(8,128)(2,1)}, u32[]{:S(2)}) copy-start(bf16[3072,1536]{1,0:T(8,128)(2,1)} %all-gather.19.cloned.1.call-done) | copy-start | bytes 28311556
  446.8 7.3 copy-start.51
  461.6 17.5 %copy-start.8 = (f32[1024,768]{1,0:T(8,128)S(1)}, f32[1024,768]{1,0:T(8,128)}, u32[]{:S(2)}) copy-start(f32[1024,768]{1,0:T(8,128)} %copy-done.6) | copy-start | bytes 9437188
  583.4 26.1 %copy-start.9 = (f32[1024,768]{1,0:T(8,128)S(1)}, f32[1024,768]{1,0:T(8,128)}, u32[]{:S(2)}) copy-start(f32[1024,768]{1,0:T(8,128)} %copy-done.6) | copy-start | bytes 9437188
  609.5 413.2 %reduce-scatter.9.cloned.1.call-start = ((), (), s32[]{:S(2)}) async-start(), calls=%async_computation.25 | async-start | bytes 9732096 | tf_op jit(solution)/shard_map/reduce_scatter | solution.py:597
  619.9 6.8 copy-start.11
  666.7 8.2 copy-start.33
  704.5 71.1 %all-to-all-start.4 = ((bf16[4,256,768]{2,1,0:T(8,128)(2,1)}), bf16[4,256,768]{2,1,0:T(8,128)(2,1)}, u32[]{:S(2)}, u32[]{:S(2)}) async-start(bf16[4,256,768]{2,1,0:T(8,128)(2,1)} %bitcast.280), calls=%async_computation.4 | async-start | bytes 3145728 | tf_op jit(solution)/shard_map/all_to_all | solution.py:441
  775.6 70.6 %all-to-all-start.12 = ((bf16[8,96,576]{2,1,0:T(8,128)(2,1)}), bf16[8,96,576]{2,1,0:T(8,128)(2,1)}, u32[]{:S(2)}, u32[]{:S(2)}) async-start(bf16[8,96,576]{2,1,0:T(8,128)(2,1)} %bitcast.292), calls=%async_computation.12 | async-start | bytes 1966080 | tf_op jit(solution)/shard_map/all_to_all | solution.py:590
  846.2 20.4 %all-to-all-start.13 = ((bf16[8,96,384]{2,1,0:T(8,128)(2,1)}), bf16[8,96,384]{2,1,0:T(8,128)(2,1)}, u32[]{:S(2)}, u32[]{:S(2)}) async-start(bf16[8,96,384]{2,1,0:T(8,128)(2,1)} %bitcast.312), calls=%async_computation.13 | async-start | bytes 1179648 | tf_op jit(solution)/shard_map/all_to_all | solution.py:590
  858.1 13.7 %copy-start.13 = (f32[1024,768]{1,0:T(8,128)S(1)}, f32[1024,768]{1,0:T(8,128)}, u32[]{:S(2)}) copy-start(f32[1024,768]{1,0:T(8,128)} %copy-done.12) | copy-start | bytes 9437188
  866.6 58.8 %all-to-all-start.7 = ((bf16[4,3,192,1024]{3,2,1,0:T(8,128)(2,1)}), bf16[4,3,192,1024]{3,2,1,0:T(8,128)(2,1)}, u32[]{:S(2)}, u32[]{:S(2)}) async-start(bf16[4,3,192,1024]{3,2,1,0:T(8,128)(2,1)} %self_backward.1), calls=%async_computation.7 | async-start | bytes 9437184 | tf_op jit(solution)/shard_map/all_to_all | solution.py:444
  871.6 192.2 %reduce-scatter.7.cloned.1.call-start = ((), (), s32[]{:S(2)}) async-start(), calls=%async_computation.24 | async-start | bytes 4055040 | tf_op jit(solution)/shard_map/reduce_scatter | solution.py:597
  925.4 27.6 %all-to-all-start.11 = ((bf16[4,256,768]{2,1,0:T(8,128)(2,1)}), bf16[4,256,768]{2,1,0:T(8,128)(2,1)S(1)}, u32[]{:S(2)}, u32[]{:S(2)}) async-start(bf16[4,256,768]{2,1,0:T(8,128)(2,1)} %bitcast.299), calls=%async_computation.11 | async-start | bytes 3145728 | tf_op jit(solution)/shard_map/all_to_all | solution.py:444
  940.8 15.9 %copy-start.40 = (f32[768]{0:T(1024)S(1)}, f32[768]{0:T(1024)}, u32[]{:S(2)}) copy-start(f32[768]{0:T(1024)} %get-tuple-element.84) | copy-start | bytes 9220
  953.0 138.3 %all-to-all-start.8 = ((bf16[4,256,768]{2,1,0:T(8,128)(2,1)}), bf16[4,256,768]{2,1,0:T(8,128)(2,1)S(1)}, u32[]{:S(2)}, u32[]{:S(2)}) async-start(bf16[4,256,768]{2,1,0:T(8,128)(2,1)} %bitcast.300), calls=%async_computation.8 | async-start | bytes 3145728 | tf_op jit(solution)/shard_map/all_to_all | solution.py:441
  956.7 136.6 %all-gather.21.cloned.1.call-start = ((), (), s32[]{:S(2)}) async-start(), calls=%async_computation.21 | async-start | bytes 1474560 | tf_op jit(solution)/shard_map/all_gather | solution.py:598
  1021.4 1.3 collective-permute-start.1
  1046.9 1.4 collective-permute-start.2
  1063.7 14.1 %copy-start.44 = (pred[1024]{0:T(1024)(128)(4,1)S(1)}, pred[1024]{0:T(1024)(128)(4,1)}, u32[]{:S(2)}) copy-start(pred[1024]{0:T(1024)(128)(4,1)} %fusion.79) | copy-start | bytes 3076
  (27 other events, 82.8 us)
Sparse Core Ops, SparseCore 0:
  62.7 18.7 all-gather.22
  83.7 75.4 all-gather.10
  161.4 46.3 all-gather.12
  211.1 76.2 all-gather.14
  289.4 30.5 all-gather.16
  323.3 84.8 all-gather.18
  609.6 35.6 all-gather.24
  665.0 165.7 reduce-scatter.8
  880.8 128.3 reduce-scatter.6
  1022.8 22.5 all-gather.20

commit v2 on v1

v2 whole, which is shorter than its diff:
```python
import functools

import jax
import jax.numpy as jnp
from jax import lax
from jax.experimental import pallas as pl
from jax.experimental.pallas import tpu as pltpu
from jax.sharding import PartitionSpec as P

HEADS = 12
HEAD_DIM = 64
BLK = 256

EPSILON = 1e-05
NEGATIVE = -1e30
LOG2E = 1.4426950408889634
SCALING = HEAD_DIM**-0.5
QUERY_SCALE = SCALING * LOG2E

KEYS = 512
QUERIES = 1024
VMEM_LIMIT = 56 * 2**20

bf16 = jnp.bfloat16
f32 = jnp.float32

CONTEXT, TENSOR, LENGTH, UNIT_LENGTHS = 0, 1, 2, 3


def lasting(microseconds):
    return pl.CostEstimate(
        flops=int(microseconds * 1.1e9), bytes_accessed=0, transcendentals=0
    )


def dot_nn(left, right):
    return lax.dot_general(left, right, (((1,), (0,)), ((), ())), preferred_element_type=f32)


def dot_nt(left, right):
    return lax.dot_general(left, right, (((1,), (1,)), ((), ())), preferred_element_type=f32)


def dot_tn(left, right):
    return lax.dot_general(left, right, (((0,), (0,)), ((), ())), preferred_element_type=f32)


def dot_tt(left, right):
    return lax.dot_general(left, right, (((0,), (1,)), ((), ())), preferred_element_type=f32)


def row_index(rows, columns):
    return lax.broadcasted_iota(jnp.int32, (rows, columns), 0)


def place_index(rows, columns, start):
    return lax.broadcasted_iota(jnp.int32, (rows, columns), 1) + start


def three_parts(row, ones_row):
    high = row.astype(bf16).astype(f32)
    rest = row - high
    middle = rest.astype(bf16).astype(f32)
    lowest = rest - middle
    at = row_index(16, row.shape[1])
    last = jnp.where(at == 3, 1.0, 0.0) if ones_row else jnp.zeros_like(at, f32)
    rows = jnp.where(at == 0, high, jnp.where(at == 1, middle, jnp.where(at == 2, lowest, last)))
    return rows.astype(bf16)


def self_forward_kernel(meta_ref, x_ref, *refs, begin):
    out_refs, (total_ref, keys, values, held) = refs[:-4], refs[-4:]
    length = meta_ref[UNIT_LENGTHS + begin + pl.program_id(0)]
    places = x_ref.shape[2]
    quarter_tiles = out_refs[0].shape[2] // QUERIES
    per_query = QUERIES // KEYS
    half = BLK
    key_tiles = (length + KEYS - 1) // KEYS

    def prepare(tile, _):
        start = pl.multiple_of(tile * KEYS, KEYS)
        rows = x_ref[0, HEAD_DIM : 2 * HEAD_DIM, pl.ds(start, KEYS)].astype(f32)
        at, place = row_index(16, KEYS), place_index(16, KEYS, start)
        mask = jnp.where((at == 0) & (place >= length), NEGATIVE, 0.0)
        stacked = jnp.concatenate([rows, mask, jnp.zeros((48, KEYS), f32)], axis=0)
        keys[pl.ds(start, KEYS), :] = stacked.T.astype(bf16)
        values[0:HEAD_DIM, pl.ds(start, KEYS)] = x_ref[
            0, 2 * HEAD_DIM : 3 * HEAD_DIM, pl.ds(start, KEYS)
        ]
        return 0

    lax.fori_loop(0, key_tiles, prepare, 0)
    values[HEAD_DIM : HEAD_DIM + 16, :] = jnp.ones((16, places), bf16)

    def query_tile(index, _):
        first_query = pl.multiple_of(index * QUERIES, QUERIES)
        ones_row = jnp.where(row_index(16, QUERIES) == 0, 1.0, 0.0).astype(bf16)
        queries = jnp.concatenate(
            [x_ref[0, 0:HEAD_DIM, pl.ds(first_query, QUERIES)], ones_row, jnp.zeros((48, QUERIES), bf16)],
            axis=0,
        )

        def score(tile):
            start = pl.multiple_of(tile * KEYS, KEYS)
            scores = dot_nn(keys[pl.ds(start, KEYS), :], queries)
            held[lax.rem(tile, 2)] = scores
            return jnp.max(scores, axis=0, keepdims=True)

        def step(tile, carry):
            largest, total, next_largest = carry
            updated = jnp.maximum(largest, next_largest)
            start = pl.multiple_of(tile * KEYS, KEYS)
            chances = jnp.exp2(held[lax.rem(tile, 2)] - updated).astype(bf16)
            total = total * jnp.exp2(largest - updated) + dot_nn(
                values[:, pl.ds(start, KEYS)], chances
            )
            return updated, total, score(jnp.minimum(tile + 1, key_tiles - 1))

        largest = jnp.full((1, QUERIES), NEGATIVE, f32)
        total = jnp.zeros((HEAD_DIM + 16, QUERIES), f32)
        largest, total, _ = lax.fori_loop(
            0, jnp.minimum(index * per_query, key_tiles), step, (largest, total, score(0))
        )

        def part(low, high, start, size, largest, total):
            scores = dot_nn(keys[pl.ds(start, size), :], queries[:, low:high])
            before = largest[:, low:high]
            updated = jnp.maximum(before, jnp.max(scores, axis=0, keepdims=True))
            chances = jnp.exp2(scores - updated).astype(bf16)
            summed = dot_nn(values[:, pl.ds(start, size)], chances)
            return updated, total[:, low:high] * jnp.exp2(before - updated) + summed

        for at in range(per_query):

            def diagonal(_, carry):
                largest, total = carry
                low = at * KEYS
                start = pl.multiple_of(first_query + low, KEYS)
                pieces = [(largest[:, :low], total[:, :low])] if low else []
                pieces.append(part(low, low + half, start, half, largest, total))
                pieces.append(part(low + half, low + KEYS, start, KEYS, largest, total))
                if low + KEYS < QUERIES:
                    pieces.append(part(low + KEYS, QUERIES, start, KEYS, largest, total))
                return tuple(jnp.concatenate(piece, axis=1) for piece in zip(*pieces))

            present = (index * per_query + at < key_tiles).astype(jnp.int32)
            largest, total = lax.fori_loop(0, present, diagonal, (largest, total))
        row_total = total[HEAD_DIM : HEAD_DIM + 1]
        inner = pl.multiple_of(lax.rem(index, quarter_tiles) * QUERIES, QUERIES)
        result = (total[:HEAD_DIM] / row_total).astype(bf16)
        slot = (index // quarter_tiles) ^ meta_ref[CONTEXT]
        for at, out_ref in enumerate(out_refs):

            @pl.when(slot == at)
            def _():
                out_ref[0, :, pl.ds(inner, QUERIES)] = result

        total_ref[0, :, pl.ds(first_query, QUERIES)] = largest + jnp.log2(row_total)
        return 0

    lax.fori_loop(0, places // QUERIES, query_tile, 0)


def self_forward(meta, projected, quarters, begin, units):
    places = projected.shape[2]
    quarter = places // quarters
    return pl.pallas_call(
        functools.partial(self_forward_kernel, begin=begin),
        grid_spec=pltpu.PrefetchScalarGridSpec(
            num_scalar_prefetch=1,
            grid=(units,),
            in_specs=[pl.BlockSpec((1, 3 * HEAD_DIM, places), lambda u, n: (begin + u, 0, 0))],
            out_specs=[pl.BlockSpec((1, HEAD_DIM, quarter), lambda u, n: (u, 0, 0))] * quarters
            + [pl.BlockSpec((1, 1, places), lambda u, n: (u, 0, 0))],
            scratch_shapes=[
                pltpu.VMEM((places, 128), bf16),
                pltpu.VMEM((HEAD_DIM + 16, places), bf16),
                pltpu.VMEM((2, KEYS, QUERIES), f32),
            ],
        ),
        out_shape=[jax.ShapeDtypeStruct((units, HEAD_DIM, quarter), bf16)] * quarters
        + [jax.ShapeDtypeStruct((units, 1, places), f32)],
        cost_estimate=lasting(20 * units),
        compiler_params=pltpu.CompilerParams(vmem_limit_bytes=VMEM_LIMIT),
        name="self_forward",
    )(meta, projected)


def self_backward_kernel(meta_ref, x_ref, total_ref, *refs, begin):
    keys, values, queries, backs, query_sum = refs[-5:]
    quarters = (len(refs) - 5) // 3
    out_refs, back_refs, grad_refs = (refs[at * quarters : (at + 1) * quarters] for at in range(3))
    length = meta_ref[UNIT_LENGTHS + begin + pl.program_id(0)]
    places = x_ref.shape[2]
    quarter_tiles = out_refs[0].shape[2] // KEYS
    half = BLK
    key_tiles = (length + KEYS - 1) // KEYS

    def prepare(tile, _):
        start = pl.multiple_of(tile * KEYS, KEYS)
        key_rows = x_ref[0, HEAD_DIM : 2 * HEAD_DIM, pl.ds(start, KEYS)].astype(f32)
        value_rows = x_ref[0, 2 * HEAD_DIM : 3 * HEAD_DIM, pl.ds(start, KEYS)].astype(f32)
        at, place = row_index(16, KEYS), place_index(16, KEYS, start)
        ones = jnp.where(at < 3, 1.0, 0.0)
        mask = jnp.where((at == 3) & (place >= length), NEGATIVE, ones)
        blank = jnp.zeros((48, KEYS), f32)
        keys[pl.ds(start, KEYS), :] = jnp.concatenate([key_rows, mask, blank], axis=0).T.astype(bf16)
        values[pl.ds(start, KEYS), :] = jnp.concatenate([value_rows, ones, blank], axis=0).T.astype(
            bf16
        )
        blank = blank.astype(bf16)
        queries[:, pl.ds(start, KEYS)] = jnp.concatenate(
            [
                x_ref[0, 0:HEAD_DIM, pl.ds(start, KEYS)],
                three_parts(-total_ref[0, :, pl.ds(start, KEYS)], True),
                blank,
            ],
            axis=0,
        )
        slot = (tile // quarter_tiles) ^ meta_ref[CONTEXT]
        inner = pl.multiple_of(lax.rem(tile, quarter_tiles) * KEYS, KEYS)
        for at in range(quarters):

            @pl.when(slot == at)
            def _():
                back = back_refs[at][0, :, pl.ds(inner, KEYS)]
                out = out_refs[at][0, :, pl.ds(inner, KEYS)]
                delta = jnp.sum(back.astype(f32) * out.astype(f32), axis=0, keepdims=True)
                backs[:, pl.ds(start, KEYS)] = jnp.concatenate(
                    [back, three_parts(-delta, False), blank], axis=0
                )

        query_sum[:, pl.ds(start, KEYS)] = jnp.zeros((HEAD_DIM, KEYS), f32)
        return 0

    lax.fori_loop(0, key_tiles, prepare, 0)

    def tile_terms(key_start, key_size, query_start, query_size, back_key, back_value):
        query = queries[:, pl.ds(query_start, query_size)]
        back = backs[:, pl.ds(query_start, query_size)]
        chances = jnp.exp2(dot_nn(keys[pl.ds(key_start, key_size), :], query))
        back_chances = dot_nn(values[pl.ds(key_start, key_size), :], back)
        back_scores = (chances * back_chances).astype(bf16)
        back_value = back_value + dot_nt(back[:HEAD_DIM], chances.astype(bf16))
        back_key = back_key + dot_nt(query[:HEAD_DIM], back_scores)
        query_sum[:, pl.ds(query_start, query_size)] += dot_nn(
            x_ref[0, HEAD_DIM : 2 * HEAD_DIM, pl.ds(key_start, key_size)], back_scores
        )
        return back_key, back_value

    def write(tile, rows, value):
        inner = pl.multiple_of(lax.rem(tile, quarter_tiles) * KEYS, KEYS)
        slot = (tile // quarter_tiles) ^ meta_ref[CONTEXT]
        for at in range(quarters):

            @pl.when(slot == at)
            def _():
                grad_refs[at][0, rows, pl.ds(inner, KEYS)] = value

    def key_tile(index, _):
        start = pl.multiple_of(index * KEYS, KEYS)
        second = pl.multiple_of(start + half, half)
        blank = jnp.zeros((HEAD_DIM, half), f32)
        first_part = tile_terms(start, half, start, KEYS, blank, blank)
        second_part = tile_terms(second, half, second, half, blank, blank)
        begun = tuple(jnp.concatenate(pair, axis=1) for pair in zip(first_part, second_part))

        def step(tile, carry):
            return tile_terms(start, KEYS, pl.multiple_of(tile * KEYS, KEYS), KEYS, *carry)

        back_key, back_value = lax.fori_loop(index + 1, key_tiles, step, begun)
        both = jnp.concatenate([back_key * (1.0 / LOG2E), back_value], axis=0).astype(bf16)
        write(index, slice(HEAD_DIM, 3 * HEAD_DIM), both)
        return 0

    lax.fori_loop(0, key_tiles, key_tile, 0)

    def finish(tile, _):
        start = pl.multiple_of(tile * KEYS, KEYS)
        write(tile, slice(0, HEAD_DIM), (query_sum[:, pl.ds(start, KEYS)] * SCALING).astype(bf16))
        return 0

    lax.fori_loop(0, key_tiles, finish, 0)

    def clear(tile, _):
        write(tile, slice(0, 3 * HEAD_DIM), jnp.zeros((3 * HEAD_DIM, KEYS), bf16))
        return 0

    lax.fori_loop(key_tiles, places // KEYS, clear, 0)


def self_backward(meta, projected, totals, attended, back, begin, origin):
    units, places = 1, projected.shape[2]
    quarters = len(attended)
    quarter = places // quarters
    return pl.pallas_call(
        functools.partial(self_backward_kernel, begin=begin),
        grid_spec=pltpu.PrefetchScalarGridSpec(
            num_scalar_prefetch=1,
            grid=(units,),
            in_specs=[
                pl.BlockSpec((1, 3 * HEAD_DIM, places), lambda u, n: (begin + u, 0, 0)),
                pl.BlockSpec((1, 1, places), lambda u, n: (begin - origin + u, 0, 0)),
            ]
            + [pl.BlockSpec((1, HEAD_DIM, quarter), lambda u, n: (begin - origin + u, 0, 0))]
            * quarters
            + [pl.BlockSpec((1, HEAD_DIM, quarter), lambda u, n: (begin + u, 0, 0))] * quarters,
            out_specs=[pl.BlockSpec((1, 3 * HEAD_DIM, quarter), lambda u, n: (u, 0, 0))] * quarters,
            scratch_shapes=[
                pltpu.VMEM((places, 128), bf16),
                pltpu.VMEM((places, 128), bf16),
                pltpu.VMEM((128, places), bf16),
                pltpu.VMEM((128, places), bf16),
                pltpu.VMEM((HEAD_DIM, places), f32),
            ],
        ),
        out_shape=[jax.ShapeDtypeStruct((units, 3 * HEAD_DIM, quarter), bf16)] * quarters,
        cost_estimate=lasting(30 * units),
        compiler_params=pltpu.CompilerParams(vmem_limit_bytes=VMEM_LIMIT),
        name="self_backward",
    )(meta, projected, totals, *attended, *back)


def cross_forward_kernel(meta_ref, query_ref, pair_ref, out_ref, total_ref):
    places = query_ref.shape[1]
    keys = pair_ref[0, 0, 0:HEAD_DIM, :].astype(f32).T.astype(bf16)
    values = jnp.concatenate(
        [pair_ref[0, 0, HEAD_DIM:, :], jnp.ones((16, pair_ref.shape[3]), bf16)], axis=0
    )
    for start in range(0, places, KEYS):
        scores = dot_nn(keys, query_ref[:, start : start + KEYS])
        largest = jnp.max(scores, axis=0, keepdims=True)
        chances = jnp.exp2(scores - largest).astype(bf16)
        total = dot_nn(values, chances)
        row_total = total[HEAD_DIM : HEAD_DIM + 1]
        out_ref[:, start : start + KEYS] = (total[:HEAD_DIM] / row_total).astype(bf16)
        total_ref[0, :, start : start + KEYS] = largest + jnp.log2(row_total)


def pair_spec(pairs):
    units = pairs.shape[1]

    def place(h, meta):
        return h // units, h % units, 0, 0

    return pl.BlockSpec((1, 1) + pairs.shape[2:], place)


def cross_forward(meta, queries, pairs):
    width, places = queries.shape
    rows = pl.BlockSpec((HEAD_DIM, places), lambda h, n: (h, 0))
    return pl.pallas_call(
        cross_forward_kernel,
        grid_spec=pltpu.PrefetchScalarGridSpec(
            num_scalar_prefetch=1,
            grid=(width // HEAD_DIM,),
            in_specs=[rows, pair_spec(pairs)],
            out_specs=[rows, pl.BlockSpec((1, 1, places), lambda h, n: (h, 0, 0))],
        ),
        out_shape=[
            jax.ShapeDtypeStruct((width, places), bf16),
            jax.ShapeDtypeStruct((width // HEAD_DIM, 1, places), f32),
        ],
        cost_estimate=lasting(25),
        compiler_params=pltpu.CompilerParams(vmem_limit_bytes=VMEM_LIMIT),
        name="cross_forward",
    )(meta, queries, pairs)


def cross_backward_kernel(
    meta_ref, query_ref, pair_ref, out_ref, back_ref, total_ref, grad_ref, pair_grad_ref
):
    places = query_ref.shape[1]
    rows = pair_ref.shape[3]
    at = row_index(64, rows)
    ones = jnp.where(at < 3, 1.0, 0.0)
    key_major = pair_ref[0, 0, 0:HEAD_DIM, :]
    keys = jnp.concatenate([key_major.astype(f32), ones], axis=0).T.astype(bf16)
    values = jnp.concatenate([pair_ref[0, 0, HEAD_DIM:, :].astype(f32), ones], axis=0).T.astype(bf16)
    blank = jnp.zeros((48, KEYS), bf16)
    back_key = jnp.zeros((HEAD_DIM, rows), f32)
    back_value = jnp.zeros((HEAD_DIM, rows), f32)
    for start in range(0, places, KEYS):
        span = slice(start, start + KEYS)
        plain, back = query_ref[:, span], back_ref[:, span]
        query = jnp.concatenate([plain, three_parts(-total_ref[0, :, span], False), blank], axis=0)
        delta = jnp.sum(back.astype(f32) * out_ref[:, span].astype(f32), axis=0, keepdims=True)
        back_rows = jnp.concatenate([back, three_parts(-delta, False), blank], axis=0)
        chances = jnp.exp2(dot_nn(keys, query))
        back_scores = (chances * dot_nn(values, back_rows)).astype(bf16)
        back_value = back_value + dot_nt(back, chances.astype(bf16))
        back_key = back_key + dot_nt(plain, back_scores)
        grad_ref[:, span] = (dot_nn(key_major, back_scores) * SCALING).astype(bf16)
    pair_grad_ref[0, 0, 0:HEAD_DIM, :] = (back_key * (1.0 / LOG2E)).astype(bf16)
    pair_grad_ref[0, 0, HEAD_DIM:, :] = back_value.astype(bf16)


def cross_backward(meta, queries, pairs, attended, back, totals):
    width, places = queries.shape
    rows = pl.BlockSpec((HEAD_DIM, places), lambda h, n: (h, 0))
    return pl.pallas_call(
        cross_backward_kernel,
        grid_spec=pltpu.PrefetchScalarGridSpec(
            num_scalar_prefetch=1,
            grid=(width // HEAD_DIM,),
            in_specs=[
                rows,
                pair_spec(pairs),
                rows,
                rows,
                pl.BlockSpec((1, 1, places), lambda h, n: (h, 0, 0)),
            ],
            out_specs=[rows, pair_spec(pairs)],
        ),
        out_shape=[
            jax.ShapeDtypeStruct((width, places), bf16),
            jax.ShapeDtypeStruct(pairs.shape, bf16),
        ],
        cost_estimate=lasting(36),
        compiler_params=pltpu.CompilerParams(vmem_limit_bytes=VMEM_LIMIT),
        name="cross_backward",
    )(meta, queries, pairs, attended, back, totals)


def normed(summed):
    centred = summed - jnp.mean(summed, axis=-1, keepdims=True)
    variance = jnp.mean(centred * centred, axis=-1, keepdims=True)
    inverse = lax.rsqrt(variance + EPSILON)
    return centred * inverse, inverse


def normed_back(normal, inverse, scaled):
    shared = jnp.mean(scaled, axis=-1, keepdims=True)
    along = jnp.mean(scaled * normal, axis=-1, keepdims=True)
    return (scaled - shared - normal * along) * inverse


def valid_column(meta_ref, quarter, rows):
    start = meta_ref[CONTEXT] * quarter + pl.program_id(0) * rows
    place = lax.broadcasted_iota(jnp.int32, (rows, 1), 0) + start
    return jnp.where(place < meta_ref[LENGTH], 1.0, 0.0)


def add_rows(sum_ref, *terms):
    @pl.when(pl.program_id(0) == 0)
    def _():
        sum_ref[...] = jnp.zeros_like(sum_ref)

    for at, term in enumerate(terms):
        sum_ref[at : at + 1, :] += jnp.sum(term, axis=0, keepdims=True)


def project_kernel(meta_ref, weight_ref, *refs, parts, rows):
    piece_refs, (x_ref, out_ref) = refs[:-2], refs[-2:]
    at_row = lax.broadcasted_iota(jnp.int32, (weight_ref.shape[0], 1), 0)
    scale = jnp.where(lax.rem(at_row, 3 * HEAD_DIM) < HEAD_DIM, QUERY_SCALE, 1.0)
    quarter = x_ref.shape[0] // (len(piece_refs) // parts)
    for at, piece_ref in enumerate(piece_refs):
        step, part = divmod(at, parts)
        result = (dot_nt(weight_ref[...], piece_ref[...]) * scale).astype(bf16)
        for block in range(quarter // (rows * parts)):
            place = (block * parts + part) * rows
            start = pl.multiple_of((meta_ref[CONTEXT] ^ step) * quarter + place, rows)
            run = slice(block * rows, (block + 1) * rows)
            x_ref[pl.ds(start, rows), :] = piece_ref[run, :]
            out_ref[:, pl.ds(start, rows)] = result[:, run]


def project(meta, weight, pieces, parts, rows):
    places, width = pieces[0].shape[0] * len(pieces), pieces[0].shape[1]
    whole = pl.BlockSpec(memory_space=pltpu.VMEM)
    return pl.pallas_call(
        functools.partial(project_kernel, parts=parts, rows=rows),
        in_specs=[pl.BlockSpec(memory_space=pltpu.SMEM)] + [whole] * (1 + len(pieces)),
        out_specs=[whole, whole],
        out_shape=[
            jax.ShapeDtypeStruct((places, width), bf16),
            jax.ShapeDtypeStruct((weight.shape[0], places), bf16),
        ],
        cost_estimate=lasting(10),
        compiler_params=pltpu.CompilerParams(vmem_limit_bytes=VMEM_LIMIT),
        name="project",
    )(meta, weight, *pieces)


def first_kernel(
    meta_ref, x_ref, norm_ref, out_w_ref, query_w_ref, *refs, quarter
):
    att_refs, (sum_ref, low_ref, query_ref, total_ref) = refs[:-4], refs[-4:]
    groups = query_w_ref.shape[0]
    branch = None
    for at in range(groups):
        att = jnp.concatenate([ref[...] for ref in att_refs[at::groups]], axis=0)
        term = dot_tt(att, out_w_ref[meta_ref[CONTEXT] ^ at])
        branch = term if branch is None else branch + term
    x = x_ref[...].astype(f32)
    summed = x + branch
    normal, _ = normed(summed)
    first = normal * norm_ref[0:1, :] + norm_ref[3:4, :]
    first_low = first.astype(bf16)
    sum_ref[...] = summed
    low_ref[...] = first_low
    query = jnp.concatenate([dot_nn(first_low, query_w_ref[at]) for at in range(groups)], axis=1)
    query_ref[...] = (query * QUERY_SCALE).T.astype(bf16)
    valid = valid_column(meta_ref, quarter, x.shape[0])
    add_rows(total_ref, valid * x * x, valid * branch * branch, valid * first * first)


def whole_spec(array):
    zeros = (0,) * array.ndim
    return pl.BlockSpec(array.shape, lambda b, n: zeros, pipeline_mode=pl.Buffered(1))


def first_step(meta, x_all, norms, out_w, query_w, att, rows):
    width = x_all.shape[1]
    quarter = att[0].shape[1]
    blocks = quarter // rows
    tokens = pl.BlockSpec((rows, width), lambda b, n: (b, 0))
    turned = pl.BlockSpec((width, rows), lambda b, n: (0, b))
    return pl.pallas_call(
        functools.partial(first_kernel, quarter=quarter),
        grid_spec=pltpu.PrefetchScalarGridSpec(
            num_scalar_prefetch=1,
            grid=(blocks,),
            in_specs=[
                pl.BlockSpec((rows, width), lambda b, n: (n[CONTEXT] * blocks + b, 0)),
                whole_spec(norms),
                whole_spec(out_w),
                whole_spec(query_w),
            ]
            + [pl.BlockSpec((piece.shape[0], rows), lambda b, n: (0, b)) for piece in att],
            out_specs=[tokens, tokens, turned, pl.BlockSpec((8, width), lambda b, n: (0, 0))],
        ),
        out_shape=[
            jax.ShapeDtypeStruct((quarter, width), f32),
            jax.ShapeDtypeStruct((quarter, width), bf16),
            jax.ShapeDtypeStruct((width, quarter), bf16),
            jax.ShapeDtypeStruct((8, width), f32),
        ],
        cost_estimate=lasting(8),
        compiler_params=pltpu.CompilerParams(vmem_limit_bytes=VMEM_LIMIT),
        name="first_step",
    )(meta, x_all, norms, out_w, query_w, *att)


def gelu_and_slope(inner):
    chance = 0.5 * (1.0 + lax.erf(inner * 0.7071067811865476))
    density = jnp.exp2(inner * inner * (-0.5 * LOG2E)) * 0.3989422804014327
    return inner * chance, chance + inner * density


def feed_kernel(
    meta_ref, att_ref, sum_ref, norm_ref, out_w_ref, feed_ref, *refs, quarter
):
    groups, width = feed_ref.shape[0], sum_ref.shape[1]
    cot_ref, output_ref, *refs = refs
    low_ref, active_ref, inner_ref, back_three_ref, back_two_ref, back_sum_ref, back_att_ref = refs[:7]
    total_ref, slope_ref = refs[7:]
    rows = sum_ref.shape[0]
    part = out_w_ref.shape[2]
    gain = [norm_ref[at : at + 1, :] for at in range(3)]
    bias = [norm_ref[3 + at : 4 + at, :] for at in range(3)]
    branch_two = None
    for at in range(groups):
        term = dot_tt(att_ref[at * part : (at + 1) * part, :], out_w_ref[at])
        branch_two = term if branch_two is None else branch_two + term
    normal, _ = normed(sum_ref[...])
    normal_two, inverse_two = normed(normal * gain[0] + bias[0] + branch_two)
    second = normal_two * gain[1] + bias[1]
    second_low = second.astype(bf16)
    low_ref[...] = second_low
    branch_three = None
    for at in range(groups):
        inner = dot_nn(second_low, feed_ref[at, :, :width])
        active, slope = gelu_and_slope(inner)
        active = active.astype(bf16)
        active_ref[:, at * width : (at + 1) * width] = active
        slope_ref[:, at * width : (at + 1) * width] = slope
        term = dot_nt(active, feed_ref[at, :, width:])
        branch_three = term if branch_three is None else branch_three + term
    normal_three, inverse_three = normed(second + branch_three)
    output_ref[...] = (normal_three * gain[2] + bias[2]).astype(bf16)
    valid = valid_column(meta_ref, quarter, rows)
    back_output = cot_ref[...].astype(f32) * valid
    back_third = normed_back(normal_three, inverse_three, back_output * gain[2])
    back_three = back_third.astype(bf16)
    back_three_ref[...] = back_three
    back_second = back_third
    for at in range(groups):
        back_active = dot_nn(back_three, feed_ref[at, :, width:])
        back_inner = (back_active * slope_ref[:, at * width : (at + 1) * width]).astype(bf16)
        inner_ref[:, at * width : (at + 1) * width] = back_inner
        back_second = back_second + dot_nt(back_inner, feed_ref[at, :, :width])
    back_second_sum = normed_back(normal_two, inverse_two, back_second * gain[1])
    back_sum_ref[...] = back_second_sum
    back_two = back_second_sum.astype(bf16)
    back_two_ref[...] = back_two
    back_att = jnp.concatenate([dot_nn(back_two, out_w_ref[at]) for at in range(groups)], axis=1)
    back_att_ref[...] = back_att.T.astype(bf16)
    add_rows(
        total_ref,
        valid * branch_two * branch_two,
        valid * second * second,
        valid * branch_three * branch_three,
        back_second * normal_two,
        back_output * normal_three,
        back_second,
        back_output,
    )


def feed_step(meta, att, first_sum, norms, out_w, feed, cotangent, rows):
    quarter, width = first_sum.shape
    groups = feed.shape[0]
    hidden_width = groups * width
    tokens = pl.BlockSpec((rows, width), lambda b, n: (b, 0))
    wide = pl.BlockSpec((rows, hidden_width), lambda b, n: (b, 0))
    turned = pl.BlockSpec((width, rows), lambda b, n: (0, b))
    return pl.pallas_call(
        functools.partial(feed_kernel, quarter=quarter),
        grid_spec=pltpu.PrefetchScalarGridSpec(
            num_scalar_prefetch=1,
            grid=(quarter // rows,),
            in_specs=[
                turned,
                tokens,
                whole_spec(norms),
                whole_spec(out_w),
                whole_spec(feed),
                tokens,
            ],
            out_specs=[tokens, tokens, wide, wide, tokens, tokens, tokens, turned]
            + [pl.BlockSpec((8, width), lambda b, n: (0, 0))],
            scratch_shapes=[pltpu.VMEM((rows, hidden_width), f32)],
        ),
        out_shape=[
            jax.ShapeDtypeStruct((quarter, width), bf16),
            jax.ShapeDtypeStruct((quarter, width), bf16),
            jax.ShapeDtypeStruct((quarter, hidden_width), bf16),
            jax.ShapeDtypeStruct((quarter, hidden_width), bf16),
            jax.ShapeDtypeStruct((quarter, width), bf16),
            jax.ShapeDtypeStruct((quarter, width), bf16),
            jax.ShapeDtypeStruct((quarter, width), f32),
            jax.ShapeDtypeStruct((width, quarter), bf16),
            jax.ShapeDtypeStruct((8, width), f32),
        ],
        cost_estimate=lasting(45),
        compiler_params=pltpu.CompilerParams(vmem_limit_bytes=VMEM_LIMIT),
        name="feed_step",
    )(meta, att, first_sum, norms, out_w, feed, cotangent)


def last_kernel(meta_ref, query_ref, back_sum_ref, sum_ref, norm_ref, query_w_ref, out_w_ref, *refs):
    back_refs, (back_ref, low_ref, total_ref) = refs[:-3], refs[-3:]
    groups, _, part = query_w_ref.shape
    back_first = back_sum_ref[...]
    for at in range(groups):
        back_first = back_first + dot_tt(query_ref[at * part : (at + 1) * part, :], query_w_ref[at])
    normal, inverse = normed(sum_ref[...])
    back_first_sum = normed_back(normal, inverse, back_first * norm_ref[0:1, :])
    back_ref[...] = back_first_sum
    back_one = back_first_sum.astype(bf16)
    low_ref[...] = back_one
    for at, ref in enumerate(back_refs):
        ref[...] = dot_nn(back_one, out_w_ref[meta_ref[CONTEXT] ^ at]).T.astype(bf16)
    add_rows(total_ref, back_first * normal, back_first)


def last_step(meta, back_query, back_second_sum, first_sum, norms, query_w, out_w, rows):
    quarter, width = first_sum.shape
    groups, _, part = query_w.shape
    tokens = pl.BlockSpec((rows, width), lambda b, n: (b, 0))
    turned = pl.BlockSpec((width, rows), lambda b, n: (0, b))
    return pl.pallas_call(
        last_kernel,
        grid_spec=pltpu.PrefetchScalarGridSpec(
            num_scalar_prefetch=1,
            grid=(quarter // rows,),
            in_specs=[
                turned,
                tokens,
                tokens,
                whole_spec(norms),
                whole_spec(query_w),
                whole_spec(out_w),
            ],
            out_specs=[pl.BlockSpec((part, rows), lambda b, n: (0, b))] * groups
            + [tokens, tokens, pl.BlockSpec((8, width), lambda b, n: (0, 0))],
        ),
        out_shape=[jax.ShapeDtypeStruct((part, quarter), bf16)] * groups
        + [
            jax.ShapeDtypeStruct((quarter, width), f32),
            jax.ShapeDtypeStruct((quarter, width), bf16),
            jax.ShapeDtypeStruct((8, width), f32),
        ],
        cost_estimate=lasting(8),
        compiler_params=pltpu.CompilerParams(vmem_limit_bytes=VMEM_LIMIT),
        name="last_step",
    )(meta, back_query, back_second_sum, first_sum, norms, query_w, out_w)


def hidden_kernel(meta_ref, back_ref, weight_ref, *refs):
    groups = weight_ref.shape[0]
    whole_refs, part_refs, out_ref = refs[: -1 - groups], refs[-1 - groups : -1], refs[-1]
    total = back_ref[...]
    for at in range(groups):
        group = meta_ref[CONTEXT] ^ at
        part = jnp.concatenate([ref[group] for ref in whole_refs] + [part_refs[at][...]], axis=0)
        total = total + dot_tt(part, weight_ref[group])
    out_ref[...] = total.astype(bf16)


def hidden_step(meta, back_first_sum, weights, parts, rows):
    quarter, width = back_first_sum.shape

    def columns(part):
        lead = part.shape[:-1]
        zeros = (0,) * len(lead)
        return pl.BlockSpec(lead + (rows,), lambda b, n: zeros + (b,))

    return pl.pallas_call(
        hidden_kernel,
        grid_spec=pltpu.PrefetchScalarGridSpec(
            num_scalar_prefetch=1,
            grid=(quarter // rows,),
            in_specs=[
                pl.BlockSpec((rows, width), lambda b, n: (b, 0)),
                whole_spec(weights),
            ]
            + [columns(part) for part in parts],
            out_specs=pl.BlockSpec((rows, width), lambda b, n: (b, 0)),
        ),
        out_shape=jax.ShapeDtypeStruct((quarter, width), bf16),
        cost_estimate=lasting(8),
        compiler_params=pltpu.CompilerParams(vmem_limit_bytes=VMEM_LIMIT),
        name="hidden_step",
    )(meta, back_first_sum, weights, *parts)


def turned_once(pairs):
    @pl.when(pl.program_id(0) == 0)
    def _():
        for source, target in pairs:
            target[...] = source[...].astype(f32).T.astype(bf16)


def put_halves(meta_ref, keep_ref, send_ref, low, high, result):
    shards, rows = keep_ref.shape[1:3]
    core = lax.rem(meta_ref[CONTEXT], 2)
    result = result.astype(bf16)
    for half, (even_ref, odd_ref) in enumerate(((keep_ref, send_ref), (send_ref, keep_ref))):

        @pl.when(core == half)
        def _():
            for shard in range(shards):
                start = 2 * shard * rows
                even_ref[0, shard, :, low:high] = result[start : start + rows]
                odd_ref[0, shard, :, low:high] = result[start + rows : start + 2 * rows]


def feed_grad_kernel(
    meta_ref, low_ref, inner_ref, back_ref, active_ref, two_ref, cross_ref, keep_ref, send_ref, *turned
):
    width = low_ref.shape[1]
    put = functools.partial(put_halves, meta_ref, keep_ref, send_ref)
    turned_once(zip((low_ref, back_ref, two_ref), turned))
    put(0, width, dot_nn(turned[0][...], inner_ref[...]))
    put(width, 2 * width, dot_nn(turned[1][...], active_ref[...]))
    put(2 * width, keep_ref.shape[3], dot_nt(turned[2][...], cross_ref[...]))


def feed_grad(meta, second_low, back_inner, back_three, active, back_two, cross_att, shards):
    tokens, width = second_low.shape
    groups = active.shape[1] // width
    part = width // groups
    left = pl.BlockSpec((tokens, width), lambda b, n: (0, 0))
    right = pl.BlockSpec((tokens, width), lambda b, n: (0, b))
    half = (shards, width // (2 * shards), 2 * width + part)
    return pl.pallas_call(
        feed_grad_kernel,
        grid_spec=pltpu.PrefetchScalarGridSpec(
            num_scalar_prefetch=1,
            grid=(groups,),
            in_specs=[
                left,
                right,
                left,
                right,
                left,
                pl.BlockSpec((part, tokens), lambda b, n: (b, 0)),
            ],
            out_specs=[pl.BlockSpec((1,) + half, lambda b, n: (b, 0, 0, 0))] * 2,
            scratch_shapes=[pltpu.VMEM((width, tokens), bf16)] * 3,
        ),
        out_shape=[jax.ShapeDtypeStruct((groups,) + half, bf16)] * 2,
        cost_estimate=lasting(18),
        compiler_params=pltpu.CompilerParams(vmem_limit_bytes=VMEM_LIMIT),
        name="feed_grad",
    )(meta, second_low, back_inner, back_three, active, back_two, cross_att)


def mixed_grad_kernel(
    meta_ref, one_ref, low_ref, selected_ref, query_ref, pair_ref, *refs
):
    keep_ref, send_ref, *turned = refs[-5:]
    att_refs = refs[:-5]
    turned_once(zip((one_ref, low_ref, selected_ref), turned))
    slot = pl.program_id(0) ^ meta_ref[CONTEXT]
    att = None
    for at in range(4):
        piece = jnp.concatenate([ref[...] for ref in att_refs[at::4]], axis=0)
        att = piece if att is None else jnp.where(slot == at, piece, att)
    result = jnp.concatenate(
        [
            dot_nt(turned[0][...], att),
            dot_nt(turned[1][...], query_ref[...]),
            dot_nt(turned[2][...], pair_ref[0]),
        ],
        axis=1,
    )
    put_halves(meta_ref, keep_ref, send_ref, 0, result.shape[1], result)


def mixed_grad(meta, back_one, first_low, selected, back_query, back_pairs, att, shards):
    tokens, width = back_one.shape
    groups = 4
    part = width // groups
    pair_width, retrieved = back_pairs.shape[1:]
    half = (shards, width // (2 * shards), 2 * part + pair_width)
    return pl.pallas_call(
        mixed_grad_kernel,
        grid_spec=pltpu.PrefetchScalarGridSpec(
            num_scalar_prefetch=1,
            grid=(groups,),
            in_specs=[
                whole_spec(back_one),
                whole_spec(first_low),
                whole_spec(selected),
                pl.BlockSpec((part, tokens), lambda b, n: (b, 0)),
                pl.BlockSpec((1, pair_width, retrieved), lambda b, n: (b, 0, 0)),
            ]
            + [whole_spec(piece) for piece in att],
            out_specs=[pl.BlockSpec((1,) + half, lambda b, n: (b, 0, 0, 0))] * 2,
            scratch_shapes=[
                pltpu.VMEM((width, tokens), bf16),
                pltpu.VMEM((width, tokens), bf16),
                pltpu.VMEM((width, retrieved), bf16),
            ],
        ),
        out_shape=[jax.ShapeDtypeStruct((groups,) + half, bf16)] * 2,
        cost_estimate=lasting(14),
        compiler_params=pltpu.CompilerParams(vmem_limit_bytes=VMEM_LIMIT),
        name="mixed_grad",
    )(meta, back_one, first_low, selected, back_query, back_pairs, *att)


def own_grad_kernel(meta_ref, x_ref, *refs):
    part_refs, out_ref = refs[:-1], refs[-1]
    quarter = part_refs[0].shape[1]
    total = None
    for at, part_ref in enumerate(part_refs):
        start = pl.multiple_of((meta_ref[CONTEXT] ^ at) * quarter, quarter)
        term = dot_nn(part_ref[...], x_ref[pl.ds(start, quarter), :])
        total = term if total is None else total + term
    out_ref[...] = total.T.astype(bf16)


def own_grad(meta, x_all, parts):
    whole = pl.BlockSpec(memory_space=pltpu.VMEM)
    return pl.pallas_call(
        own_grad_kernel,
        in_specs=[pl.BlockSpec(memory_space=pltpu.SMEM)] + [whole] * (1 + len(parts)),
        out_specs=whole,
        out_shape=jax.ShapeDtypeStruct((x_all.shape[1], parts[0].shape[0]), bf16),
        cost_estimate=lasting(7),
        compiler_params=pltpu.CompilerParams(vmem_limit_bytes=VMEM_LIMIT),
        name="own_grad",
    )(meta, x_all, *parts)


def product(spec, left, right):
    return jnp.einsum(spec, left, right, preferred_element_type=f32)


def turn(array, axis, step):
    count = lax.axis_size(axis)
    return lax.ppermute(array, axis, [(at, at ^ step) for at in range(count)])


def to_others(parts, axis):
    return [parts[0]] + [turn(parts[at], axis, at) for at in range(1, len(parts))]


def gather_context(array):
    far = turn(array, "ctx", 2)
    return [array, turn(array, "ctx", 1), far, turn(far, "ctx", 1)]


def gather(array, axis, dim):
    step = 1
    while step < lax.axis_size(axis):
        other = turn(array, axis, step)
        later = (lax.axis_index(axis) & step) > 0
        array = jnp.concatenate(
            [jnp.where(later, other, array), jnp.where(later, array, other)], axis=dim
        )
        step *= 2
    return array


def in_slots(pieces, index):
    for step in (1, 2):
        later = (index & step) > 0
        pieces = [jnp.where(later, pieces[at ^ step], pieces[at]) for at in range(len(pieces))]
    return pieces


def gather_direct(array, axis, dim):
    pieces = [array] + [turn(array, axis, at) for at in range(1, 4)]
    return jnp.concatenate(in_slots(pieces, lax.axis_index(axis)), axis=dim)


def exchange(parts, axes):
    return lax.all_to_all(parts, axes, split_axis=0, concat_axis=0, tiled=True)


def add_up(pieces):
    total = pieces[0].astype(f32)
    for piece in pieces[1:]:
        total = total + piece.astype(f32)
    return total


def sum_everywhere(vector):
    steps = []
    for axis in ("ctx", "tp", "shard"):
        step = 1
        while step < lax.axis_size(axis):
            vector = vector + turn(vector, axis, step)
            steps.append(vector)
            step *= 2
    return steps


class StagedSum:
    def __init__(self, keep, send):
        self.terms, self.send = [keep], send

    def beside(self, kernel):
        self.terms[1:] = [after(term, kernel) for term in self.terms[1:]]

    def over_core(self):
        self.terms.append(turn(self.send, "ctx", 1))

    def over_shard(self):
        count, index = lax.axis_size("shard"), lax.axis_index("shard")

        def part(at):
            return add_up([lax.dynamic_index_in_dim(t, at, 1, keepdims=False) for t in self.terms])

        if count == 2:
            self.send = part(1 - index).astype(bf16)
            own = [lax.dynamic_index_in_dim(t, index, 1, keepdims=False) for t in self.terms]
            self.terms = own + [turn(self.send, "shard", 1)]
        else:
            self.send = jnp.moveaxis(add_up(self.terms).astype(bf16), 1, 0)
            self.terms = [jnp.sum(exchange(self.send, "shard").astype(f32), axis=0).astype(bf16)]

    def over_x(self):
        rows = self.terms[0].shape[1] // 2
        index = lax.axis_index("ctx") // 2

        def part(at):
            return [lax.dynamic_slice_in_dim(t, at * rows, rows, 1) for t in self.terms]

        self.send = add_up(part(1 - index)).astype(bf16)
        self.terms = part(index) + [turn(self.send, "ctx", 2)]

    def send_of_quarter(self):
        self.terms = [add_up(self.terms).astype(bf16)]
        return self.terms[0]

    def over_tensor(self):
        self.send = add_up(self.terms).astype(bf16)
        index = lax.axis_index("tp")
        parts = [
            lax.dynamic_index_in_dim(self.send, index ^ at, 0, keepdims=False)
            for at in range(self.send.shape[0])
        ]
        self.terms = to_others(parts, "tp")

    def total(self):
        self.send = add_up(self.terms).astype(bf16)
        return self.send

    def spread(self):
        total = self.send
        for step in (2, 1):
            other = turn(total, "ctx", step)
            later = (lax.axis_index("ctx") & step) > 0
            total = jnp.concatenate(
                [jnp.where(later, other, total), jnp.where(later, total, other)], axis=0
            )
        return total.astype(f32)


def after(value, *earlier):
    return lax.optimization_barrier((value,) + earlier)[0]


def per_device(
    hidden,
    bank,
    indices,
    lengths,
    cotangent,
    query_self,
    key_self,
    value_self,
    out_self,
    query_cross,
    key_cross,
    value_cross,
    out_cross,
    up_weight,
    down_weight,
    norm_gain,
    norm_bias,
):
    context_count = lax.axis_size("ctx")
    tensor_count = lax.axis_size("tp")
    shard_index = lax.axis_index("shard")
    context_index = lax.axis_index("ctx")
    tensor_index = lax.axis_index("tp")
    group_sequences, device_places, model_width = hidden.shape
    units = HEADS // context_count
    group_width = units * HEAD_DIM
    quarter = device_places * tensor_count
    shard_rows = query_self.shape[0]
    piece_rows = shard_rows // context_count
    feed_width = up_weight.shape[1]

    swap = [
        (c * tensor_count + z, z * context_count + c)
        for c in range(context_count)
        for z in range(tensor_count)
    ]

    group_lengths = lax.dynamic_slice_in_dim(
        lengths, shard_index * group_sequences, group_sequences
    )
    length = group_lengths[tensor_index]
    meta = jnp.stack([context_index, tensor_index, length] + [length] * units).astype(jnp.int32)

    def by_unit(weights):
        stacked = jnp.stack([w.reshape(-1, units, HEAD_DIM) for w in weights], axis=2)
        return stacked.reshape(weights[0].shape[0], -1)

    local_self = by_unit([query_self, key_self, value_self])
    local_pair = by_unit([key_cross, value_cross])
    self_width, pair_width = local_self.shape[1], local_pair.shape[1]

    def gather_all(columns):
        rows = lax.dynamic_slice_in_dim(columns, context_index * piece_rows, piece_rows, 0)
        everything = lax.all_gather(rows, ("tp", "shard", "ctx"), axis=0, tiled=True)
        return everything.reshape(tensor_count, model_width, columns.shape[1])

    bank_local = bank.shape[1]
    retrieved = indices.shape[1]
    owner_tensor = indices[0] // bank_local
    local_rows = indices[0] - owner_tensor * bank_local
    owned = (owner_tensor == tensor_index)[:, None]
    picked = jnp.where(owned, jnp.take(bank[0], local_rows, axis=0), jnp.zeros((), bf16))

    half = device_places // 2
    own_self = lax.ppermute(local_self.T, ("ctx", "tp"), swap)
    low, far = [], []
    for at in range(2):
        part = hidden[:, at * half : (at + 1) * half]
        part = exchange(after(part, own_self) if at else part, "tp").reshape(quarter // 2, model_width)
        low.append(part)
        far.append(turn(after(part, *far), "ctx", 2))
    own_self = gather(own_self, "shard", 1)
    far[1] = after(far[1], own_self)
    x_low = low[1]
    beside = [turn(part, "ctx", 1) for part in low]
    across = [turn(part, "ctx", 1) for part in far]
    picked = exchange(after(picked, x_low).reshape(tensor_count, -1, model_width), "tp")
    x_all, projected = project(meta, own_self, low + beside + far + across, 2, half)
    projected = projected.reshape(units, 3 * HEAD_DIM, -1)

    norms = jnp.concatenate([norm_gain, norm_bias], axis=0).T
    bundle = jnp.concatenate([out_self.T, query_cross, out_cross.T, local_pair, norms], axis=1)
    bundle = gather_all(after(bundle, x_low))
    out_self_t = bundle[:, :, :group_width]
    query_cross_w = bundle[:, :, group_width : 2 * group_width]
    out_cross_t = bundle[:, :, 2 * group_width : 3 * group_width]
    pair_w = bundle[:, :, 3 * group_width : 3 * group_width + pair_width]
    norm_rows = bundle[0, :, 3 * group_width + pair_width :].T.astype(f32)
    norm_rows = jnp.pad(norm_rows, ((0, 2), (0, 0)))
    feed = gather_all(after(jnp.concatenate([up_weight, down_weight.T], axis=1), x_low))

    self_out, self_totals, self_att = [], [], []

    def forward(begin, *ready):
        *out, total = self_forward(meta, after(projected, *ready), context_count, begin, 1)
        self_out.append(out)
        self_totals.append(total)
        self_att.extend(piece.reshape(-1, quarter) for piece in to_others(out, "ctx"))
        return total

    picked = jnp.sum(after(picked, projected).astype(f32), axis=0).astype(bf16)
    done = forward(0, picked)
    picked = after(lax.ppermute(picked, ("ctx", "tp"), swap), done)
    done = forward(1, picked, done)
    lists = [picked] + [turn(picked, "ctx", at) for at in range(1, context_count)]
    lists = [after(piece, done) for piece in lists]
    done = forward(2, *lists, done)
    selected = jnp.concatenate(in_slots(lists, context_index))
    cot = exchange(after(cotangent, done), "tp")
    pairs = product("tdf,kd->tfk", pair_w, selected).astype(bf16)
    pairs = pairs.reshape(context_count, units, 2 * HEAD_DIM, retrieved)
    first_sum, first_low, cross_query, first_totals = first_step(
        meta, after(x_all, pairs), norm_rows, out_self_t, query_cross_w, self_att, device_places
    )
    cross_att, cross_total = cross_forward(meta, cross_query, pairs)
    cot = after(cot, cross_att).reshape(quarter, model_width)
    fed = feed_step(meta, cross_att, first_sum, norm_rows, out_cross_t, feed, cot, device_places)
    output, second_low, active, back_inner, back_three, back_two, back_second_sum, back_cross, totals = fed
    shard_count = lax.axis_size("shard")
    feed_sum = StagedSum(
        *feed_grad(
            meta, second_low, back_inner, back_three, active, back_two, cross_att, shard_count
        )
    )
    feed_sum.over_core()
    output = exchange(output.reshape(tensor_count, device_places, model_width), "tp")
    back_query, back_pairs = cross_backward(
        meta, cross_query, pairs, cross_att, after(back_cross, feed_sum.send), cross_total
    )
    back_pairs = back_pairs.reshape(context_count, pair_width, retrieved)
    feed_sum.over_shard()
    back_selected = product("tfk,tdf->kd", back_pairs, pair_w).astype(bf16)
    back_selected = back_selected.reshape(context_count, -1, model_width)
    *back_self, back_first_sum, back_one, last_totals = last_step(
        meta,
        back_query,
        after(back_second_sum, output, feed_sum.send, back_selected),
        first_sum,
        norm_rows,
        query_cross_w,
        out_self_t,
        device_places,
    )
    back_selected = after(exchange(back_selected, "ctx"), back_one)
    back_self = [piece.reshape(units, HEAD_DIM, quarter) for piece in to_others(back_self, "ctx")]
    mixed_sum = StagedSum(
        *mixed_grad(
            meta, back_one, first_low, selected, back_query, back_pairs, self_att, shard_count
        )
    )
    self_w = gather_all(after(local_self, first_low))

    squares = jnp.sum(jnp.concatenate([first_totals[:3], totals[:3]], axis=0), axis=1)
    rows = jnp.stack(
        [
            last_totals[0],
            totals[3],
            totals[4],
            last_totals[1],
            totals[5],
            totals[6],
            jnp.pad(squares, (0, model_width - squares.shape[0])),
        ]
    )

    def backward(begin, *ready):
        return self_backward(
            meta,
            after(projected, *ready),
            self_totals[begin],
            self_out[begin],
            back_self,
            begin,
            begin,
        )

    def parts_of(grads):
        return [piece.reshape(-1, quarter) for piece in to_others(grads, "ctx")]

    back_selected = jnp.sum(back_selected.astype(f32), axis=0).astype(bf16)
    grads = [backward(0, mixed_sum.send, back_selected)]
    mixed_sum.over_core()
    back_rows = lax.ppermute(back_selected, ("ctx", "tp"), swap)
    for running in (feed_sum, mixed_sum):
        running.beside(grads[0][0])
    back_rows = after(back_rows, grads[0][0])
    feed_sum.over_x()
    mixed_sum.over_shard()

    back_parts = [exchange(jnp.concatenate(in_slots(grads[0], context_index)), "ctx")]
    grads.append(backward(1, back_rows, feed_sum.send, mixed_sum.send, *grads[0]))
    back_rows = [back_rows] + [turn(back_rows, "tp", at) for at in range(1, tensor_count)]
    back_rows = [after(piece, grads[1][0]) for piece in back_rows]
    back_parts = [after(back_parts[0], grads[1][0])]
    own_grads = []
    for running in (feed_sum, mixed_sum):
        running.beside(grads[1][0])
    feed_sum.over_tensor()
    mixed_sum.over_x()

    back_parts.append(exchange(jnp.concatenate(in_slots(grads[1], context_index)), "ctx"))
    ready = (feed_sum.send, mixed_sum.send, back_parts[0], *back_rows)
    grads.append(backward(2, *ready, *grads[1]))
    back_parts[1] = after(back_parts[1], grads[2][0])
    for running in (feed_sum, mixed_sum):
        running.beside(grads[2][0])
    back_parts += parts_of(grads[2])
    ready = (feed_sum.total(), mixed_sum.send_of_quarter(), back_parts[1])
    for at in range(units):
        own_grads.append(
            own_grad(meta, after(x_all, *ready), [p.reshape(-1, quarter) for p in grads[at]])
        )
    mixed_sum.terms = [after(term, back_parts[-1]) for term in mixed_sum.terms]
    mixed_sum.over_tensor()
    mixed_sum.total()
    rows_steps = sum_everywhere(after(rows, own_grads[2]))

    own_sum = jnp.concatenate(own_grads, axis=1)
    own_sum = own_sum.reshape(shard_count, -1, own_sum.shape[1])
    if shard_count == 2:
        mine = lax.dynamic_index_in_dim(own_sum, shard_index, 0, keepdims=False)
        other = lax.dynamic_index_in_dim(own_sum, 1 - shard_index, 0, keepdims=False)
        own_sum = add_up([mine, turn(other, "shard", 1)])
    else:
        own_sum = jnp.sum(exchange(own_sum, "shard").astype(f32), axis=0)
    own_sum = own_sum.astype(bf16).reshape(tensor_count, -1, own_sum.shape[-1])
    own_sum = [
        lax.dynamic_index_in_dim(own_sum, tensor_index ^ at, 0, keepdims=False)
        for at in range(tensor_count)
    ]
    own_sum = add_up(to_others(own_sum, "tp")).astype(bf16)
    own_sum = lax.ppermute(own_sum, ("ctx", "tp"), swap)

    back_hidden = hidden_step(meta, back_first_sum, self_w, back_parts, device_places)
    back_rows = jnp.concatenate(in_slots([after(p, back_hidden, own_sum) for p in back_rows], tensor_index))
    back_hidden = exchange(back_hidden.reshape(tensor_count, device_places, model_width), "tp")
    back_rows = jnp.where(owned, back_rows.astype(f32), 0.0)
    back_bank = jnp.zeros(bank.shape[1:], f32).at[local_rows].add(back_rows)[None]

    own_all = gather_direct(own_sum, "ctx", 0)
    back_mixed = mixed_sum.spread()
    back_feed = feed_sum.spread()
    rows = rows_steps[-1]
    shard_columns = lax.dynamic_slice_in_dim(rows, shard_index * shard_rows, shard_rows, 1)
    back_gain, back_bias = shard_columns[:3], shard_columns[3:6]
    token_total = jnp.sum(lengths).astype(f32) * model_width
    statistics = jnp.sqrt(rows[6, : squares.shape[0]] / token_total)

    def apart(stacked, count):
        split = stacked.reshape(shard_rows, units, count, HEAD_DIM)
        return [split[:, :, at].reshape(shard_rows, group_width).astype(f32) for at in range(count)]

    back_query_self, back_key_self, back_value_self = apart(own_all, 3)
    back_key_cross, back_value_cross = apart(back_mixed[:, 2 * group_width :], 2)
    return (
        output,
        back_hidden.astype(f32),
        back_bank,
        back_query_self,
        back_key_self,
        back_value_self,
        back_mixed[:, :group_width].T,
        back_mixed[:, group_width : 2 * group_width],
        back_key_cross,
        back_value_cross,
        back_feed[:, 2 * feed_width :].T,
        back_feed[:, :feed_width],
        back_feed[:, feed_width : 2 * feed_width].T,
        back_gain,
        back_bias,
        statistics,
    )


def solution(mesh):
    return jax.shard_map(
        per_device,
        mesh=mesh,
        in_specs=(
            P("shard", ("ctx", "tp"), None),
            P(("shard", "ctx"), "tp", None),
            P(("shard", "ctx"), None),
            P(),
            P("shard", ("ctx", "tp"), None),
            P("shard", "tp"),
            P("shard", "tp"),
            P("shard", "tp"),
            P("tp", "shard"),
            P("shard", "tp"),
            P("shard", "tp"),
            P("shard", "tp"),
            P("tp", "shard"),
            P("shard", "tp"),
            P("tp", "shard"),
            P(None, "shard"),
            P(None, "shard"),
        ),
        out_specs=(
            P("shard", ("ctx", "tp"), None),
            P("shard", ("ctx", "tp"), None),
            P(("shard", "ctx"), "tp", None),
            P("shard", "tp"),
            P("shard", "tp"),
            P("shard", "tp"),
            P("tp", "shard"),
            P("shard", "tp"),
            P("shard", "tp"),
            P("shard", "tp"),
            P("tp", "shard"),
            P("shard", "tp"),
            P("tp", "shard"),
            P(None, "shard"),
            P(None, "shard"),
            P(),
        ),
        check_vma=False,
    )
```

time: 1120 us -> 807 us (0.72)
  blocking collectives: 229 us -> 28.1 us
  matrix products: 181 us -> 16.6 us
  waiting for transfers between devices: 274 us -> 132 us
  Pallas kernels: 171 us -> 297 us
  starting transfers between devices: 98.2 us -> 188 us
  local copies, waits for them, and re-layouts: 74 us -> 53.1 us
    dot_general x21 -> x2, matrix products: 181 us -> 16.6 us  [product(): return jnp.einsum(spec, left, right, preferred_element_type=f32)]
    all_to_all x10 -> x8, waiting for transfers between devices: 158 us -> 26.3 us  [exchange(): return lax.all_to_all(parts, axes, split_axis=0, concat_axis=0, tiled=True)]
    ppermute x3 -> x60, starting transfers between devices: 2.04 us -> 129 us  [the longest x56 126 us: turn(): return lax.ppermute(array, axis, [(at, at ^ step) for at in range(count)])]
    pallas_call x4 -> x18, Pallas kernels: 171 us -> 297 us  [the longest x3 49.9 us: self_forward(): pl.pallas_call(functools.partial(self_forward_kernel, begin=begin), grid_...]
    ppermute x3 -> x60, waiting for transfers between devices: 0.01 us -> 106 us  [the longest x56 106 us: turn(): return lax.ppermute(array, axis, [(at, at ^ step) for at in range(count)])]
    all_to_all x4 -> x1, blocking collectives: 131 us -> 28.1 us  [exchange(): return lax.all_to_all(parts, axes, split_axis=0, concat_axis=0, tiled=True)]
    all_gather x2 -> x3, waiting for transfers between devices: 65.5 us -> 0.04 us  [gather_all(): lax.all_gather(rows, ('tp', 'shard', 'ctx'), axis=0, tiled=True)]
    psum x1 -> x0, blocking collectives: 58.9 us -> none  [per_device(): lax.psum((square_terms, jnp.stack([gain_one, gain_two, gain_three]), jnp....]
  transfers between devices with their start and end apart: 23 -> 71, of which waited for: 12 -> 17; matrix products, arithmetic and copies ran while one was open for 21% -> 15% of each run, Pallas kernels for 12% -> 29%
where the time goes in v2:
time: 807 us; the launch traced here: 797 us
  Pallas kernels  297 us (37%)
  starting transfers between devices  188 us (23%)
  waiting for transfers between devices  132 us (16%)
  other arithmetic  65.7 us (8%)
  local copies, waits for them, and re-layouts  53.1 us (7%)
  blocking collectives  28.1 us (3%)
  matrix products  16.6 us (2%)
  between operations  15.6 us (2%)
    ppermute x56, starting transfers between devices, turn(): return lax.ppermute(array, axis, [(at, at ^ step) for at in range(count)])  126 us
    ppermute x56, waiting for transfers between devices, turn(): return lax.ppermute(array, axis, [(at, at ^ step) for at in range(count)])  106 us
    all_to_all x8, starting transfers between devices, exchange(): return lax.all_to_all(parts, axes, split_axis=0, concat_axis=0, tiled=True)  59.8 us
    pallas_call x3, Pallas kernels, self_forward(): pl.pallas_call(functools.partial(self_forward_kernel, begin=begin), grid_...  49.9 us
    pallas_call x1, Pallas kernels, feed_step(): pl.pallas_call(functools.partial(feed_kernel, quarter=quarter), grid_spec...  42.1 us
    pallas_call x3, Pallas kernels, self_backward(): pl.pallas_call(functools.partial(self_backward_kernel, begin=begin), grid...  37.5 us
    pallas_call x1, Pallas kernels, cross_backward(): pl.pallas_call(cross_backward_kernel, grid_spec=pltpu.PrefetchScalarGridS...  37.4 us
    all_to_all x1, blocking collectives, exchange(): return lax.all_to_all(parts, axes, split_axis=0, concat_axis=0, tiled=True)  28.1 us
  transfers between devices with their start and end apart: 71, of which 17 were waited for; matrix products, arithmetic and copies ran while one was open for 15% of the time, Pallas kernels for 29%

profile of v2, /device:TPU:0, one launch (start us, length us, event | category | flops | bytes accessed | tf_op | source)
XLA Modules:
  0.0 797.1 jit_solution(10789918880738421769)
XLA Ops:
  12.2 25.1 %all-to-all-start.1 = ((bf16[4,128,768]{2,1,0:T(8,128)(2,1)}), bf16[4,128,768]{2,1,0:T(8,128)(2,1)S(1)}, u32[]{:S(2)}, u32[]{:S(2)}) async-start(bf16[4,128,768]{2,1,0:T(8,128)(2,1)} %get-tuple-element.126), calls=%async_computation.1 | async-start | bytes 1572864 | tf_op jit(solution)/shard_map/all_to_all | solution.py:924
  38.5 19.2 %all-to-all-done.1 = bf16[4,128,768]{2,1,0:T(8,128)(2,1)S(1)} async-done(((bf16[4,128,768]{2,1,0:T(8,128)(2,1)}), bf16[4,128,768]{2,1,0:T(8,128)(2,1)S(1)}, u32[]{:S(2)}, u32[]{:S(2)}) %all-to-all-start.1) | async-done | bytes 786464 | tf_op jit(solution)/shard_map/all_to_all | solution.py:924
  61.2 28.1 %all_to_all.45 = bf16[4,128,768]{2,1,0:T(8,128)(2,1)S(1)} all-to-all(bf16[4,128,768]{2,1,0:T(8,128)(2,1)S(1)} %get-tuple-element.336), channel_id=1, replica_groups=mesh['shard'=2,'ctx'=4,'tp'=4] {'tp'}, dimensions={0} | all-to-all | bytes 1572864 | tf_op jit(solution)/shard_map/all_to_all | solution.py:924
  90.1 8.1 %gather_fusion = bf16[1024,768]{1,0:T(8,128)(2,1)S(1)} fusion(bf16[4096,768]{1,0:T(8,128)(2,1)} %bitcast.172, s32[1024]{0:T(1024)S(1)} %broadcast_clamp_fusion), kind=kCustom, calls=%fused_computation | custom fusion | bytes 3149824 | tf_op jit(solution)/shard_map/jit(_take)/gather | solution.py:1073
  99.8 13.0 %collective-permute-done.4.refs_4_ = bf16[512,768]{1,0:T(8,128)(2,1)} collective-permute-done((bf16[512,768]{1,0:T(8,128)(2,1)S(1)}, bf16[512,768]{1,0:T(8,128)(2,1)}, u32[]{:S(2)}, u32[]{:S(2)}) %collective-permute-start.4) | collective-permute-done | bytes 786464 | tf_op jit(solution)/shard_map/ppermute | solution.py:887
  114.7 4.5 all-to-all-start.2
  122.0 20.3 %collective-permute-done.5.refs_5_ = bf16[512,768]{1,0:T(8,128)(2,1)} collective-permute-done((bf16[512,768]{1,0:T(8,128)(2,1)S(1)}, bf16[512,768]{1,0:T(8,128)(2,1)}, u32[]{:S(2)}, u32[]{:S(2)}) %collective-permute-start.5) | collective-permute-done | bytes 786464 | tf_op jit(solution)/shard_map/ppermute | solution.py:887
  146.1 12.6 %project.1 = (bf16[4096,768]{1,0:T(8,128)(2,1)}, bf16[576,4096]{1,0:T(8,128)(2,1)}) custom-call(s32[6]{0:T(128)} %stack.24.meta_ref, bf16[576,768]{1,0:T(8,128)(2,1)} %pad_maximum_fusion.5.weight_ref, bf16[512,768]{1,0:T(8,128)(2,1)} %bitcast.194, bf16[512,768]{1,0:T(8,128)(2,1)} %bitcast.191, bf16[512,768]{1,0:T(8,128)(2,1)} %collective-permute-done.2.refs_2_, ...), custom_call_target="tpu_custom_call" | custom-call | flops 11000000512 | tf_op jit(solution)/shard_map/project/pallas_call | solution.py:472
  158.8 7.1 all-to-all-done.2
  167.0 16.4 %self_forward.3 = (bf16[1,64,1024]{2,1,0:T(8,128)(2,1)}, bf16[1,64,1024]{2,1,0:T(8,128)(2,1)}, bf16[1,64,1024]{2,1,0:T(8,128)(2,1)}, bf16[1,64,1024]{2,1,0:T(8,128)(2,1)}, f32[1,1,4096]{2,1,0:T(1,128)}) custom-call(s32[6]{0:T(128)} %stack.24.meta_ref, bf16[3,192,4096]{2,1,0:T(8,128)(2,1)} %bitcast.223), custom_call_target="tpu_custom_call" | custom-call | flops 22000001024 | tf_op jit(solution)/shard_map/self_forward/pallas_call | solution.py:167
  187.3 7.3 collective-permute-start.10
  194.7 17.1 %self_forward.4 = (bf16[1,64,1024]{2,1,0:T(8,128)(2,1)}, bf16[1,64,1024]{2,1,0:T(8,128)(2,1)}, bf16[1,64,1024]{2,1,0:T(8,128)(2,1)}, bf16[1,64,1024]{2,1,0:T(8,128)(2,1)}, f32[1,1,4096]{2,1,0:T(1,128)}) custom-call(s32[6]{0:T(128)} %stack.24.meta_ref, bf16[3,192,4096]{2,1,0:T(8,128)(2,1)} %bitcast.224), custom_call_target="tpu_custom_call" | custom-call | flops 22000001024 | tf_op jit(solution)/shard_map/self_forward/pallas_call | solution.py:167
  213.7 7.3 collective-permute-done.9
  222.6 16.4 %self_forward.5 = (bf16[1,64,1024]{2,1,0:T(8,128)(2,1)}, bf16[1,64,1024]{2,1,0:T(8,128)(2,1)}, bf16[1,64,1024]{2,1,0:T(8,128)(2,1)}, bf16[1,64,1024]{2,1,0:T(8,128)(2,1)}, f32[1,1,4096]{2,1,0:T(1,128)}) custom-call(s32[6]{0:T(128)} %stack.24.meta_ref, bf16[3,192,4096]{2,1,0:T(8,128)(2,1)} %bitcast.225), custom_call_target="tpu_custom_call" | custom-call | flops 22000001024 | tf_op jit(solution)/shard_map/self_forward/pallas_call | solution.py:167
  239.0 9.2 %all-to-all-start.3 = ((bf16[4,256,768]{2,1,0:T(8,128)(2,1)}), bf16[4,256,768]{2,1,0:T(8,128)(2,1)S(1)}, u32[]{:S(2)}, u32[]{:S(2)}) async-start(bf16[4,256,768]{2,1,0:T(8,128)(2,1)} %param.21), calls=%async_computation.3 | async-start | bytes 3145728 | tf_op jit(solution)/shard_map/all_to_all | solution.py:924
  249.6 9.0 %convolution_convert_fusion = bf16[4,384,1024]{2,1,0:T(8,128)(2,1)} fusion(bf16[4,768,966]{2,1,0:T(8,128)(2,1)} %bitcast.176, bf16[256,768]{1,0:T(8,128)(2,1)S(1)} %get-tuple-element.334, bf16[256,768]{1,0:T(8,128)(2,1)S(1)} %get-tuple-element.333, bf16[256,768]{1,0:T(8,128)(2,1)S(1)} %get-tuple-element.332, bf16[256,768]{1,0:T(8,128)(2,1)S(1)} %get-tuple-element.331), kind=kOutput, calls=%fused_computation.18 | convolution fusion | flops 2423783424 | bytes 7077888 | tf_op jit(solution)/shard_map/tdf,kd->tfk/dot_general | solution.py:882
  273.0 12.4 %first_step.1 = (f32[1024,768]{1,0:T(8,128)}, bf16[1024,768]{1,0:T(8,128)(2,1)}, bf16[768,1024]{1,0:T(8,128)(2,1)}, f32[8,768]{1,0:T(8,128)}) custom-call(s32[6]{0:T(128)} %stack.24.meta_ref, bf16[4096,768]{1,0:T(8,128)(2,1)} %get-tuple-element.226.x_ref, f32[8,768]{1,0:T(8,128)} %copy.128.norm_ref, bf16[4,768,192]{2,1,0:T(8,128)(2,1)} %get-tuple-element.318.out_w_ref, ...), custom_call_target="tpu_custom_call" | custom-call | flops 8800000000 | tf_op jit(solution)/shard_map/first_step/pallas_call | solution.py:520
  285.4 26.4 %cross_forward.1 = (bf16[768,1024]{1,0:T(8,128)(2,1)}, f32[12,1,1024]{2,1,0:T(1,128)}) custom-call(s32[6]{0:T(128)} %stack.24.meta_ref, bf16[768,1024]{1,0:T(8,128)(2,1)} %get-tuple-element.157.query_ref, bf16[4,3,128,1024]{3,2,1,0:T(8,128)(2,1)} %bitcast.229), custom_call_target="tpu_custom_call" | custom-call | flops 27499999232 | tf_op jit(solution)/shard_map/cross_forward/pallas_call | solution.py:352
  312.9 42.1 %feed_step.1 = (bf16[1024,768]{1,0:T(8,128)(2,1)}, bf16[1024,768]{1,0:T(8,128)(2,1)}, bf16[1024,3072]{1,0:T(8,128)(2,1)}, bf16[1024,3072]{1,0:T(8,128)(2,1)}, bf...) custom-call(s32[6]{0:T(128)} %stack.24.meta_ref, ...), custom_call_target="tpu_custom_call" | custom-call | flops 49500000256 | tf_op jit(solution)/shard_map/feed_step/pallas_call | solution.py:619
  355.0 25.7 %feed_grad.1 = (bf16[4,2,192,1728]{3,2,1,0:T(8,128)(2,1)}, bf16[4,2,192,1728]{3,2,1,0:T(8,128)(2,1)}) custom-call(s32[6]{0:T(128)} %stack.24.meta_ref, bf16[1024,768]{1,0:T(8,128)(2,1)} %get-tuple-element.166.low_ref, bf16[1024,3072]{1,0:T(8,128)(2,1)} %get-tuple-element.167.inner_ref, bf16[1024,768]{1,0:T(8,128)(2,1)} %get-tuple-element.168.back_ref, ...), custom_call_target="tpu_custom_call" | custom-call | flops 19800000512 | tf_op jit(solution)/shard_map/feed_grad/pallas_call | solution.py:779
  385.7 4.9 all-to-all-start.4
  390.6 37.4 %cross_backward.1 = (bf16[768,1024]{1,0:T(8,128)(2,1)}, bf16[4,3,128,1024]{3,2,1,0:T(8,128)(2,1)}) custom-call(s32[6]{0:T(128)} %stack.24.meta_ref, bf16[768,1024]{1,0:T(8,128)(2,1)} %get-tuple-element.157.query_ref, bf16[4,3,128,1024]{3,2,1,0:T(8,128)(2,1)} %bitcast.230, bf16[768,1024]{1,0:T(8,128)(2,1)} %get-tuple-element.158.att_ref.cross_ref.out_ref, ...), custom_call_target="tpu_custom_call" | custom-call | flops 39600001024 | tf_op jit(solution)/shard_map/cross_backward/pallas_call | solution.py:401
  428.2 7.6 bitcast_convert_fusion
  440.5 4.8 fusion.4
  446.8 12.4 %last_step.1 = (bf16[192,1024]{1,0:T(8,128)(2,1)}, bf16[192,1024]{1,0:T(8,128)(2,1)}, bf16[192,1024]{1,0:T(8,128)(2,1)}, bf16[192,1024]{1,0:T(8,128)(2,1)}, f32[...) custom-call(s32[6]{0:T(128)} %stack.24.meta_ref, bf16[768,1024]{1,0:T(8,128)(2,1)} %get-tuple-element.174.query_ref, ...), custom_call_target="tpu_custom_call" | custom-call | flops 8800000000 | tf_op jit(solution)/shard_map/last_step/pallas_call | solution.py:674
  461.4 14.1 %mixed_grad.1 = (bf16[4,2,192,768]{3,2,1,0:T(8,128)(2,1)}, bf16[4,2,192,768]{3,2,1,0:T(8,128)(2,1)}) custom-call(s32[6]{0:T(128)} %stack.24.meta_ref, bf16[1024,768]{1,0:T(8,128)(2,1)} %get-tuple-element.182.one_ref, bf16[1024,768]{1,0:T(8,128)(2,1)} %get-tuple-element.180.low_ref, bf16[1024,768]{1,0:T(8,128)(2,1)} %pad_maximum_fusion.selected_ref, ...), custom_call_target="tpu_custom_call" | custom-call | flops 15399999488 | tf_op jit(solution)/shard_map/mixed_grad/pallas_call | solution.py:830
  484.1 12.4 %self_backward.3 = (bf16[1,192,1024]{2,1,0:T(8,128)(2,1)}, bf16[1,192,1024]{2,1,0:T(8,128)(2,1)}, bf16[1,192,1024]{2,1,0:T(8,128)(2,1)}, bf16[1,192,1024]{2,1,0:T(8,128)(2,1)}) custom-call(s32[6]{0:T(128)} %stack.24.meta_ref, bf16[3,192,4096]{2,1,0:T(8,128)(2,1)} %bitcast.226, f32[1,1,4096]{2,1,0:T(1,128)} %get-tuple-element.135.total_ref, ...), custom_call_target="tpu_custom_call" | custom-call | flops 32999999488 | tf_op jit(solution)/shard_map/self_backward/pallas_call | solution.py:296
  496.5 8.0 collective-permute-start.32
  504.5 16.1 %collective-permute-start.31 = (bf16[256,768]{1,0:T(8,128)(2,1)S(1)}, bf16[256,768]{1,0:T(8,128)(2,1)}, u32[]{:S(2)}, u32[]{:S(2)}) collective-permute-start(bf16[256,768]{1,0:T(8,128)(2,1)S(1)} %collective-permute-done.25), channel_id=1, source_target_pairs={{0,2},{1,3},{2,0},{3,1},{4,6},{5,7},{6,4},{7,5},{8,10},{9,11},{10,... | collective-permute-start | bytes 1179656 | tf_op jit(solution)/shard_map/ppermute | solution.py:887
  523.9 4.4 all-to-all-start.6
  540.5 12.6 %self_backward.4 = (bf16[1,192,1024]{2,1,0:T(8,128)(2,1)}, bf16[1,192,1024]{2,1,0:T(8,128)(2,1)}, bf16[1,192,1024]{2,1,0:T(8,128)(2,1)}, bf16[1,192,1024]{2,1,0:T(8,128)(2,1)}) custom-call(s32[6]{0:T(128)} %stack.24.meta_ref, bf16[3,192,4096]{2,1,0:T(8,128)(2,1)} %bitcast.227, f32[1,1,4096]{2,1,0:T(1,128)} %get-tuple-element.138.total_ref, ...), custom_call_target="tpu_custom_call" | custom-call | flops 32999999488 | tf_op jit(solution)/shard_map/self_backward/pallas_call | solution.py:296
  559.3 4.5 all-to-all-start.7
  569.4 8.9 %collective-permute-done.28 = bf16[4,96,1728]{2,1,0:T(8,128)(2,1)} collective-permute-done((bf16[4,96,1728]{2,1,0:T(8,128)(2,1)}, bf16[4,96,1728]{2,1,0:T(8,128)(2,1)}, u32[]{:S(2)}, u32[]{:S(2)}) %collective-permute-start.28) | collective-permute-done | bytes 1327136 | tf_op jit(solution)/shard_map/ppermute | solution.py:887
  582.0 7.7 collective-permute-start.36
  589.7 7.3 collective-permute-start.37
  598.5 12.4 %self_backward.5 = (bf16[1,192,1024]{2,1,0:T(8,128)(2,1)}, bf16[1,192,1024]{2,1,0:T(8,128)(2,1)}, bf16[1,192,1024]{2,1,0:T(8,128)(2,1)}, bf16[1,192,1024]{2,1,0:T(8,128)(2,1)}) custom-call(s32[6]{0:T(128)} %stack.24.meta_ref, bf16[3,192,4096]{2,1,0:T(8,128)(2,1)} %bitcast.228, f32[1,1,4096]{2,1,0:T(1,128)} %get-tuple-element.161.total_ref, ...), custom_call_target="tpu_custom_call" | custom-call | flops 32999999488 | tf_op jit(solution)/shard_map/self_backward/pallas_call | solution.py:296
  615.6 5.8 collective-permute-done.38
  623.4 5.4 own_grad.5
  628.8 5.4 own_grad.3
  634.2 5.4 own_grad.4
  643.6 9.7 %collective-permute-start.57 = (f32[7,768]{1,0:T(8,128)S(1)}, f32[7,768]{1,0:T(8,128)S(1)}, u32[]{:S(2)}, u32[]{:S(2)}) collective-permute-start(f32[7,768]{1,0:T(8,128)S(1)} %add.242), channel_id=1, source_target_pairs={{0,1},{1,0},{2,3},{3,2},{4,5},{5,4},{6,7},{7,6},{8,9},{9,8},{10,11... | collective-permute-start | bytes 64520 | tf_op jit(solution)/shard_map/ppermute | solution.py:887
  654.1 7.0 collective-permute-start.40
  671.6 10.6 %hidden_step.1 = bf16[1024,768]{1,0:T(8,128)(2,1)} custom-call(s32[6]{0:T(128)} %stack.24.meta_ref, f32[1024,768]{1,0:T(8,128)} %get-tuple-element.179.back_ref, bf16[4,768,576]{2,1,0:T(8,128)(2,1)} %bitcast.216, bf16[4,192,1024]{2,1,0:T(8,128)(2,1)} %all-to-all-done.6.refs_0_, bf16[4,192,1024]{2,1,0:T(8,128)(2,1)} %all-to-all-done.7.refs_1_, ...), custom_call_target="tpu_custom_call" | custom-call | flops 8800000000 | tf_op jit(solution)/shard_map/hidden_step/pallas_call | solution.py:721
  691.1 25.6 %collective-permute-done.50 = bf16[96,768]{1,0:T(8,128)(2,1)S(1)} collective-permute-done((bf16[96,768]{1,0:T(8,128)(2,1)}, bf16[96,768]{1,0:T(8,128)(2,1)S(1)}, u32[]{:S(2)}, u32[]{:S(2)}) %collective-permute-start.50) | collective-permute-done | bytes 147488 | tf_op jit(solution)/shard_map/ppermute | solution.py:887
  724.3 11.2 %collective-permute-start.41 = (bf16[96,576]{1,0:T(8,128)(2,1)S(1)}, bf16[96,576]{1,0:T(8,128)(2,1)S(1)}, u32[]{:S(2)}, u32[]{:S(2)}) collective-permute-start(bf16[96,576]{1,0:T(8,128)(2,1)S(1)} %get-tuple-element.361), channel_id=1, source_target_pairs={{0,1},{1,0},{2,3},{3,2},{4,5},{5,4},{6,7},{7,6},{8,9},{9,8},{10,11... | collective-permute-start | bytes 331784 | tf_op jit(solution)/shard_map/ppermute | solution.py:887
  740.6 7.2 collective-permute-done.42
  753.7 3.9 collective-permute-start.45
  762.7 14.5 %scatter_custom_fusion = f32[4096,768]{1,0:T(8,128)} fusion(s32[1024]{0:T(1024)} %bitcast.213, f32[]{:T(128)} %constant.224.clone.1, bf16[256,768]{1,0:T(8,128)(2,1)} %get-tuple-element.322, bf16[]{:T(256)} %constant.234, bf16[256,768]{1,0:T(8,128)(2,1)S(1)} %get-tuple-element.321, bf16[256,768]{1,0:T(8,128)(2,1)S(1)} %get-tuple-element.320, ...), kind=kCustom, calls=%fused_computation.2 | custom fusion | flops 7864320 | bytes 14158336 | tf_op jit(solution)/shard_map/scatter-add | solution.py:1249
  (313 shorter events, 167.1 us)
Async XLA Ops:
  12.2 45.5 %all-to-all-start.1 = ((bf16[4,128,768]{2,1,0:T(8,128)(2,1)}), bf16[4,128,768]{2,1,0:T(8,128)(2,1)S(1)}, u32[]{:S(2)}, u32[]{:S(2)}) async-start(bf16[4,128,768]{2,1,0:T(8,128)(2,1)} %get-tuple-element.126), calls=%async_computation.1 | async-start | bytes 1572864 | tf_op jit(solution)/shard_map/all_to_all | solution.py:924
  37.3 212.3 %all-gather.4.cloned.1.call-start = ((), (), s32[]{:S(2)}) async-start(), calls=%async_computation.9 | async-start | bytes 6488064 | tf_op jit(solution)/shard_map/all_gather | solution.py:1065
  60.0 251.8 %all-gather.6.cloned.1.call-start = ((), (), s32[]{:S(2)}) async-start(), calls=%async_computation.10 | async-start | bytes 9732096 | tf_op jit(solution)/shard_map/all_gather | solution.py:1065
  89.4 23.4 %collective-permute-start.4 = (bf16[512,768]{1,0:T(8,128)(2,1)S(1)}, bf16[512,768]{1,0:T(8,128)(2,1)}, u32[]{:S(2)}, u32[]{:S(2)}) collective-permute-start(bf16[512,768]{1,0:T(8,128)(2,1)S(1)} %bitcast.192), channel_id=1, source_target_pairs={{0,8},{4,12},{8,0},{12,4},{1,9},{5,13},{9,1},{13,5},{2,10},{6,14},... | collective-permute-start | bytes 2359304 | tf_op jit(solution)/shard_map/ppermute | solution.py:887
  112.7 29.6 %collective-permute-start.5 = (bf16[512,768]{1,0:T(8,128)(2,1)S(1)}, bf16[512,768]{1,0:T(8,128)(2,1)}, u32[]{:S(2)}, u32[]{:S(2)}) collective-permute-start(bf16[512,768]{1,0:T(8,128)(2,1)S(1)} %bitcast.189), channel_id=1, source_target_pairs={{0,8},{4,12},{8,0},{12,4},{1,9},{5,13},{9,1},{13,5},{2,10},{6,14},... | collective-permute-start | bytes 2359304 | tf_op jit(solution)/shard_map/ppermute | solution.py:887
  114.7 51.2 %all-to-all-start.2 = ((bf16[4,256,768]{2,1,0:T(8,128)(2,1)}), bf16[4,256,768]{2,1,0:T(8,128)(2,1)S(1)}, u32[]{:S(2)}, u32[]{:S(2)}) async-start(bf16[4,256,768]{2,1,0:T(8,128)(2,1)} %bitcast.23), calls=%async_computation.2 | async-start | bytes 3145728 | tf_op jit(solution)/shard_map/all_to_all | solution.py:924
  121.4 24.7 %collective-permute-start.2 = (bf16[512,768]{1,0:T(8,128)(2,1)S(1)}, bf16[512,768]{1,0:T(8,128)(2,1)}, u32[]{:S(2)}, u32[]{:S(2)}) collective-permute-start(bf16[512,768]{1,0:T(8,128)(2,1)S(1)} %bitcast.193), channel_id=1, source_target_pairs={{0,4},{4,0},{8,12},{12,8},{1,5},{5,1},{9,13},{13,9},{2,6},{6,2},{1... | collective-permute-start | bytes 2359304 | tf_op jit(solution)/shard_map/ppermute | solution.py:887
  121.4 24.7 %collective-permute-start.3 = (bf16[512,768]{1,0:T(8,128)(2,1)S(1)}, bf16[512,768]{1,0:T(8,128)(2,1)}, u32[]{:S(2)}, u32[]{:S(2)}) collective-permute-start(bf16[512,768]{1,0:T(8,128)(2,1)S(1)} %bitcast.190), channel_id=1, source_target_pairs={{0,4},{4,0},{8,12},{12,8},{1,5},{5,1},{9,13},{13,9},{2,6},{6,2},{1... | collective-permute-start | bytes 2359304 | tf_op jit(solution)/shard_map/ppermute | solution.py:887
  121.9 24.2 %collective-permute-start.6 = (bf16[512,768]{1,0:T(8,128)(2,1)}, bf16[512,768]{1,0:T(8,128)(2,1)}, u32[]{:S(2)}, u32[]{:S(2)}) collective-permute-start(bf16[512,768]{1,0:T(8,128)(2,1)} %collective-permute-done.4.refs_4_), channel_id=1, source_target_pairs={{0,4},{4,0},{8,12},{12,8},{1,5},{5,1},{9,13},{13,9},{2,6},{6,2},{1... | collective-permute-start | bytes 2359304 | tf_op jit(solution)/shard_map/ppermute | solution.py:887
  183.4 78.2 %collective-permute-start.12 = (bf16[1,64,1024]{2,1,0:T(8,128)(2,1)}, bf16[1,64,1024]{2,1,0:T(8,128)(2,1)}, u32[]{:S(2)}, u32[]{:S(2)}) collective-permute-start(bf16[1,64,1024]{2,1,0:T(8,128)(2,1)} %get-tuple-element.145.refs_1_), channel_id=1, source_target_pairs={{0,4},{4,0},{8,12},{12,8},{1,5},{5,1},{9,13},{13,9},{2,6},{6,2},{1... | collective-permute-start | bytes 393224 | tf_op jit(solution)/shard_map/ppermute | solution.py:887
  184.1 79.2 %collective-permute-start.13 = (bf16[1,64,1024]{2,1,0:T(8,128)(2,1)}, bf16[1,64,1024]{2,1,0:T(8,128)(2,1)}, u32[]{:S(2)}, u32[]{:S(2)}) collective-permute-start(bf16[1,64,1024]{2,1,0:T(8,128)(2,1)} %get-tuple-element.146.refs_2_), channel_id=1, source_target_pairs={{0,8},{4,12},{8,0},{12,4},{1,9},{5,13},{9,1},{13,5},{2,10},{6,14},... | collective-permute-start | bytes 393224 | tf_op jit(solution)/shard_map/ppermute | solution.py:887
  187.3 24.6 %collective-permute-start.11 = (bf16[256,768]{1,0:T(8,128)(2,1)S(1)}, bf16[256,768]{1,0:T(8,128)(2,1)S(1)}, u32[]{:S(2)}, u32[]{:S(2)}) collective-permute-start(bf16[256,768]{1,0:T(8,128)(2,1)S(1)} %collective-permute-done.8), channel_id=1, source_target_pairs={{0,4},{4,0},{8,12},{12,8},{1,5},{5,1},{9,13},{13,9},{2,6},{6,2},{1... | collective-permute-start | bytes 1179656 | tf_op jit(solution)/shard_map/ppermute | solution.py:887
  187.3 26.2 %collective-permute-start.10 = (bf16[256,768]{1,0:T(8,128)(2,1)S(1)}, bf16[256,768]{1,0:T(8,128)(2,1)S(1)}, u32[]{:S(2)}, u32[]{:S(2)}) collective-permute-start(bf16[256,768]{1,0:T(8,128)(2,1)S(1)} %collective-permute-done.8), channel_id=1, source_target_pairs={{0,8},{4,12},{8,0},{12,4},{1,9},{5,13},{9,1},{13,5},{2,10},{6,14},... | collective-permute-start | bytes 1179656 | tf_op jit(solution)/shard_map/ppermute | solution.py:887
  194.6 26.4 %collective-permute-start.9 = (bf16[256,768]{1,0:T(8,128)(2,1)S(1)}, bf16[256,768]{1,0:T(8,128)(2,1)S(1)}, u32[]{:S(2)}, u32[]{:S(2)}) collective-permute-start(bf16[256,768]{1,0:T(8,128)(2,1)S(1)} %collective-permute-done.8), channel_id=1, source_target_pairs={{0,12},{4,8},{8,4},{12,0},{1,13},{5,9},{9,5},{13,1},{2,14},{6,10},... | collective-permute-start | bytes 1179656 | tf_op jit(solution)/shard_map/ppermute | solution.py:887
  211.9 51.5 %collective-permute-start.14 = (bf16[1,64,1024]{2,1,0:T(8,128)(2,1)}, bf16[1,64,1024]{2,1,0:T(8,128)(2,1)}, u32[]{:S(2)}, u32[]{:S(2)}) collective-permute-start(bf16[1,64,1024]{2,1,0:T(8,128)(2,1)} %get-tuple-element.147.refs_3_), channel_id=1, source_target_pairs={{0,12},{4,8},{8,4},{12,0},{1,13},{5,9},{9,5},{13,1},{2,14},{6,10},... | collective-permute-start | bytes 393224 | tf_op jit(solution)/shard_map/ppermute | solution.py:887
  213.5 50.3 %collective-permute-start.15 = (bf16[1,64,1024]{2,1,0:T(8,128)(2,1)}, bf16[1,64,1024]{2,1,0:T(8,128)(2,1)}, u32[]{:S(2)}, u32[]{:S(2)}) collective-permute-start(bf16[1,64,1024]{2,1,0:T(8,128)(2,1)} %get-tuple-element.149.refs_1_), channel_id=1, source_target_pairs={{0,4},{4,0},{8,12},{12,8},{1,5},{5,1},{9,13},{13,9},{2,6},{6,2},{1... | collective-permute-start | bytes 393224 | tf_op jit(solution)/shard_map/ppermute | solution.py:887
  221.0 45.1 %collective-permute-start.16 = (bf16[1,64,1024]{2,1,0:T(8,128)(2,1)}, bf16[1,64,1024]{2,1,0:T(8,128)(2,1)}, u32[]{:S(2)}, u32[]{:S(2)}) collective-permute-start(bf16[1,64,1024]{2,1,0:T(8,128)(2,1)} %get-tuple-element.150.refs_2_), channel_id=1, source_target_pairs={{0,8},{4,12},{8,0},{12,4},{1,9},{5,13},{9,1},{13,5},{2,10},{6,14},... | collective-permute-start | bytes 393224 | tf_op jit(solution)/shard_map/ppermute | solution.py:887
  239.0 72.8 %all-to-all-start.3 = ((bf16[4,256,768]{2,1,0:T(8,128)(2,1)}), bf16[4,256,768]{2,1,0:T(8,128)(2,1)S(1)}, u32[]{:S(2)}, u32[]{:S(2)}) async-start(bf16[4,256,768]{2,1,0:T(8,128)(2,1)} %param.21), calls=%async_computation.3 | async-start | bytes 3145728 | tf_op jit(solution)/shard_map/all_to_all | solution.py:924
  248.2 423.4 %all-gather.8.cloned.1.call-start = ((), (), s32[]{:S(2)}) async-start(), calls=%async_computation.11 | async-start | bytes 4055040 | tf_op jit(solution)/shard_map/all_gather | solution.py:1065
  380.7 59.8 %collective-permute-start.21 = (bf16[4,2,192,1728]{3,2,1,0:T(8,128)(2,1)}, bf16[4,2,192,1728]{3,2,1,0:T(8,128)(2,1)}, u32[]{:S(2)}, u32[]{:S(2)}) collective-permute-start(bf16[4,2,192,1728]{3,2,1,0:T(8,128)(2,1)} %get-tuple-element.171), channel_id=1, source_target_pairs={{0,4},{4,0},{8,12},{12,8},{1,5},{5,1},{9,13},{13,9},{2,6},{6,2},{1... | collective-permute-start | bytes 15925256 | tf_op jit(solution)/shard_map/ppermute | solution.py:887
  385.7 50.1 %all-to-all-start.4 = ((bf16[4,256,768]{2,1,0:T(8,128)(2,1)}), bf16[4,256,768]{2,1,0:T(8,128)(2,1)S(1)}, u32[]{:S(2)}, u32[]{:S(2)}) async-start(bf16[4,256,768]{2,1,0:T(8,128)(2,1)} %bitcast.44), calls=%async_computation.4 | async-start | bytes 3145728 | tf_op jit(solution)/shard_map/all_to_all | solution.py:924
  437.0 39.4 %all-to-all-start.5 = ((bf16[4,256,768]{2,1,0:T(8,128)(2,1)}), bf16[4,256,768]{2,1,0:T(8,128)(2,1)S(1)}, u32[]{:S(2)}, u32[]{:S(2)}) async-start(bf16[4,256,768]{2,1,0:T(8,128)(2,1)} %bitcast.187), calls=%async_computation.5 | async-start | bytes 3145728 | tf_op jit(solution)/shard_map/all_to_all | solution.py:924
  445.3 89.7 %collective-permute-start.26 = (bf16[4,192,1728]{2,1,0:T(8,128)(2,1)}, bf16[4,192,1728]{2,1,0:T(8,128)(2,1)}, u32[]{:S(2)}, u32[]{:S(2)}) collective-permute-start(bf16[4,192,1728]{2,1,0:T(8,128)(2,1)} %fusion.4), channel_id=1, source_target_pairs={{0,16},{16,0},{1,17},{17,1},{2,18},{18,2},{3,19},{19,3},{4,20},{20... | collective-permute-start | bytes 7962632 | tf_op jit(solution)/shard_map/ppermute | solution.py:887
  461.3 22.7 %collective-permute-start.24 = (bf16[192,1024]{1,0:T(8,128)(2,1)}, bf16[192,1024]{1,0:T(8,128)(2,1)}, u32[]{:S(2)}, u32[]{:S(2)}) collective-permute-start(bf16[192,1024]{1,0:T(8,128)(2,1)} %get-tuple-element.189), channel_id=1, source_target_pairs={{0,12},{4,8},{8,4},{12,0},{1,13},{5,9},{9,5},{13,1},{2,14},{6,10},... | collective-permute-start | bytes 1179656 | tf_op jit(solution)/shard_map/ppermute | solution.py:887
  476.8 51.4 %collective-permute-start.27 = (bf16[4,2,192,768]{3,2,1,0:T(8,128)(2,1)}, bf16[4,2,192,768]{3,2,1,0:T(8,128)(2,1)}, u32[]{:S(2)}, u32[]{:S(2)}) collective-permute-start(bf16[4,2,192,768]{3,2,1,0:T(8,128)(2,1)} %get-tuple-element.183), channel_id=1, source_target_pairs={{0,4},{4,0},{8,12},{12,8},{1,5},{5,1},{9,13},{13,9},{2,6},{6,2},{1... | collective-permute-start | bytes 7077896 | tf_op jit(solution)/shard_map/ppermute | solution.py:887
  496.5 56.7 %collective-permute-start.32 = (bf16[256,768]{1,0:T(8,128)(2,1)S(1)}, bf16[256,768]{1,0:T(8,128)(2,1)S(1)}, u32[]{:S(2)}, u32[]{:S(2)}) collective-permute-start(bf16[256,768]{1,0:T(8,128)(2,1)S(1)} %collective-permute-done.25), channel_id=1, source_target_pairs={{0,3},{1,2},{2,1},{3,0},{4,7},{5,6},{6,5},{7,4},{8,11},{9,10},{10,... | collective-permute-start | bytes 1179656 | tf_op jit(solution)/shard_map/ppermute | solution.py:887
  504.5 48.7 %collective-permute-start.31 = (bf16[256,768]{1,0:T(8,128)(2,1)S(1)}, bf16[256,768]{1,0:T(8,128)(2,1)}, u32[]{:S(2)}, u32[]{:S(2)}) collective-permute-start(bf16[256,768]{1,0:T(8,128)(2,1)S(1)} %collective-permute-done.25), channel_id=1, source_target_pairs={{0,2},{1,3},{2,0},{3,1},{4,6},{5,7},{6,4},{7,5},{8,10},{9,11},{10,... | collective-permute-start | bytes 1179656 | tf_op jit(solution)/shard_map/ppermute | solution.py:887
  520.5 32.6 %collective-permute-start.30 = (bf16[256,768]{1,0:T(8,128)(2,1)S(1)}, bf16[256,768]{1,0:T(8,128)(2,1)}, u32[]{:S(2)}, u32[]{:S(2)}) collective-permute-start(bf16[256,768]{1,0:T(8,128)(2,1)S(1)} %collective-permute-done.25), channel_id=1, source_target_pairs={{0,1},{1,0},{2,3},{3,2},{4,5},{5,4},{6,7},{7,6},{8,9},{9,8},{10,11... | collective-permute-start | bytes 1179656 | tf_op jit(solution)/shard_map/ppermute | solution.py:887
  523.9 32.6 %all-to-all-start.6 = ((bf16[4,192,1024]{2,1,0:T(8,128)(2,1)}), bf16[4,192,1024]{2,1,0:T(8,128)(2,1)}, u32[]{:S(2)}, u32[]{:S(2)}) async-start(bf16[4,192,1024]{2,1,0:T(8,128)(2,1)} %pad_maximum_fusion.1), calls=%async_computation.6 | async-start | bytes 3145728 | tf_op jit(solution)/shard_map/all_to_all | solution.py:924
  531.2 32.6 %collective-permute-start.29 = (bf16[4,192,768]{2,1,0:T(8,128)(2,1)}, bf16[4,192,768]{2,1,0:T(8,128)(2,1)}, u32[]{:S(2)}, u32[]{:S(2)}) collective-permute-start(bf16[4,192,768]{2,1,0:T(8,128)(2,1)} %fusion.25), channel_id=1, source_target_pairs={{0,16},{16,0},{1,17},{17,1},{2,18},{18,2},{3,19},{19,3},{4,20},{20... | collective-permute-start | bytes 3538952 | tf_op jit(solution)/shard_map/ppermute | solution.py:887
  538.5 39.8 %collective-permute-start.28 = (bf16[4,96,1728]{2,1,0:T(8,128)(2,1)}, bf16[4,96,1728]{2,1,0:T(8,128)(2,1)}, u32[]{:S(2)}, u32[]{:S(2)}) collective-permute-start(bf16[4,96,1728]{2,1,0:T(8,128)(2,1)} %fusion.9), channel_id=1, source_target_pairs={{0,8},{4,12},{8,0},{12,4},{1,9},{5,13},{9,1},{13,5},{2,10},{6,14},... | collective-permute-start | bytes 3981320 | tf_op jit(solution)/shard_map/ppermute | solution.py:887
  559.3 51.6 %all-to-all-start.7 = ((bf16[4,192,1024]{2,1,0:T(8,128)(2,1)}), bf16[4,192,1024]{2,1,0:T(8,128)(2,1)}, u32[]{:S(2)}, u32[]{:S(2)}) async-start(bf16[4,192,1024]{2,1,0:T(8,128)(2,1)} %pad_maximum_fusion.2), calls=%async_computation.7 | async-start | bytes 3145728 | tf_op jit(solution)/shard_map/all_to_all | solution.py:924
  566.3 44.6 %collective-permute-start.39 = (bf16[4,96,768]{2,1,0:T(8,128)(2,1)}, bf16[4,96,768]{2,1,0:T(8,128)(2,1)S(1)}, u32[]{:S(2)}, u32[]{:S(2)}) collective-permute-start(bf16[4,96,768]{2,1,0:T(8,128)(2,1)} %fusion.30), channel_id=1, source_target_pairs={{0,8},{4,12},{8,0},{12,4},{1,9},{5,13},{9,1},{13,5},{2,10},{6,14},... | collective-permute-start | bytes 1769480 | tf_op jit(solution)/shard_map/ppermute | solution.py:887
  582.0 31.8 %collective-permute-start.36 = (bf16[96,1728]{1,0:T(8,128)(2,1)}, bf16[96,1728]{1,0:T(8,128)(2,1)S(1)}, u32[]{:S(2)}, u32[]{:S(2)}) collective-permute-start(bf16[96,1728]{1,0:T(8,128)(2,1)} %get-tuple-element.341), channel_id=1, source_target_pairs={{0,1},{1,0},{2,3},{3,2},{4,5},{5,4},{6,7},{7,6},{8,9},{9,8},{10,11... | collective-permute-start | bytes 995336 | tf_op jit(solution)/shard_map/ppermute | solution.py:887
  589.7 25.9 %collective-permute-start.37 = (bf16[96,1728]{1,0:T(8,128)(2,1)}, bf16[96,1728]{1,0:T(8,128)(2,1)}, u32[]{:S(2)}, u32[]{:S(2)}) collective-permute-start(bf16[96,1728]{1,0:T(8,128)(2,1)} %get-tuple-element.343), channel_id=1, source_target_pairs={{0,2},{1,3},{2,0},{3,1},{4,6},{5,7},{6,4},{7,5},{8,10},{9,11},{10,... | collective-permute-start | bytes 995336 | tf_op jit(solution)/shard_map/ppermute | solution.py:887
  597.0 24.4 %collective-permute-start.38 = (bf16[96,1728]{1,0:T(8,128)(2,1)}, bf16[96,1728]{1,0:T(8,128)(2,1)}, u32[]{:S(2)}, u32[]{:S(2)}) collective-permute-start(bf16[96,1728]{1,0:T(8,128)(2,1)} %get-tuple-element.342), channel_id=1, source_target_pairs={{0,3},{1,2},{2,1},{3,0},{4,7},{5,6},{6,5},{7,4},{8,11},{9,10},{10,... | collective-permute-start | bytes 995336 | tf_op jit(solution)/shard_map/ppermute | solution.py:887
  610.9 43.2 %collective-permute-start.35 = (bf16[1,192,1024]{2,1,0:T(8,128)(2,1)}, bf16[1,192,1024]{2,1,0:T(8,128)(2,1)S(1)}, u32[]{:S(2)}, u32[]{:S(2)}) collective-permute-start(bf16[1,192,1024]{2,1,0:T(8,128)(2,1)} %get-tuple-element.219), channel_id=1, source_target_pairs={{0,12},{4,8},{8,4},{12,0},{1,13},{5,9},{9,5},{13,1},{2,14},{6,10},... | collective-permute-start | bytes 1179656 | tf_op jit(solution)/shard_map/ppermute | solution.py:887
  611.8 55.0 %collective-permute-start.33 = (bf16[1,192,1024]{2,1,0:T(8,128)(2,1)}, bf16[1,192,1024]{2,1,0:T(8,128)(2,1)S(1)}, u32[]{:S(2)}, u32[]{:S(2)}) collective-permute-start(bf16[1,192,1024]{2,1,0:T(8,128)(2,1)} %get-tuple-element.217), channel_id=1, source_target_pairs={{0,4},{4,0},{8,12},{12,8},{1,5},{5,1},{9,13},{13,9},{2,6},{6,2},{1... | collective-permute-start | bytes 1179656 | tf_op jit(solution)/shard_map/ppermute | solution.py:887
  613.8 56.1 %collective-permute-start.34 = (bf16[1,192,1024]{2,1,0:T(8,128)(2,1)S(1)}, bf16[1,192,1024]{2,1,0:T(8,128)(2,1)S(1)}, u32[]{:S(2)}, u32[]{:S(2)}) collective-permute-start(bf16[1,192,1024]{2,1,0:T(8,128)(2,1)S(1)} %copy-done.42), channel_id=1, source_target_pairs={{0,8},{4,12},{8,0},{12,4},{1,9},{5,13},{9,1},{13,5},{2,10},{6,14},... | collective-permute-start | bytes 1179656 | tf_op jit(solution)/shard_map/ppermute | solution.py:887
  622.8 95.8 %collective-permute-start.53 = (bf16[96,1728]{1,0:T(8,128)(2,1)S(1)}, bf16[96,1728]{1,0:T(8,128)(2,1)}, u32[]{:S(2)}, u32[]{:S(2)}) collective-permute-start(bf16[96,1728]{1,0:T(8,128)(2,1)S(1)} %fusion.34), channel_id=1, source_target_pairs={{0,8},{4,12},{8,0},{12,4},{1,9},{5,13},{9,1},{13,5},{2,10},{6,14},... | collective-permute-start | bytes 995336 | tf_op jit(solution)/shard_map/ppermute | solution.py:887
  654.1 69.0 %collective-permute-start.40 = (bf16[384,576]{1,0:T(8,128)(2,1)}, bf16[384,576]{1,0:T(8,128)(2,1)}, u32[]{:S(2)}, u32[]{:S(2)}) collective-permute-start(bf16[384,576]{1,0:T(8,128)(2,1)} %dynamic-slice_bitcast_fusion.2), channel_id=1, source_target_pairs={{0,16},{16,0},{1,17},{17,1},{2,18},{18,2},{3,19},{19,3},{4,20},{20... | collective-permute-start | bytes 1327112 | tf_op jit(solution)/shard_map/ppermute | solution.py:887
  666.7 24.4 %collective-permute-start.48 = (bf16[96,768]{1,0:T(8,128)(2,1)}, bf16[96,768]{1,0:T(8,128)(2,1)}, u32[]{:S(2)}, u32[]{:S(2)}) collective-permute-start(bf16[96,768]{1,0:T(8,128)(2,1)} %get-tuple-element.354), channel_id=1, source_target_pairs={{0,1},{1,0},{2,3},{3,2},{4,5},{5,4},{6,7},{7,6},{8,9},{9,8},{10,11... | collective-permute-start | bytes 442376 | tf_op jit(solution)/shard_map/ppermute | solution.py:887
  666.7 24.4 %collective-permute-start.49 = (bf16[96,768]{1,0:T(8,128)(2,1)}, bf16[96,768]{1,0:T(8,128)(2,1)}, u32[]{:S(2)}, u32[]{:S(2)}) collective-permute-start(bf16[96,768]{1,0:T(8,128)(2,1)} %get-tuple-element.356), channel_id=1, source_target_pairs={{0,2},{1,3},{2,0},{3,1},{4,6},{5,7},{6,4},{7,5},{8,10},{9,11},{10,... | collective-permute-start | bytes 442376 | tf_op jit(solution)/shard_map/ppermute | solution.py:887
  682.2 105.0 %all-to-all-start.8 = ((bf16[4,256,768]{2,1,0:T(8,128)(2,1)}), bf16[4,256,768]{2,1,0:T(8,128)(2,1)S(1)}, u32[]{:S(2)}, u32[]{:S(2)}) async-start(bf16[4,256,768]{2,1,0:T(8,128)(2,1)} %bitcast.185), calls=%async_computation.8 | async-start | bytes 3145728 | tf_op jit(solution)/shard_map/all_to_all | solution.py:924
  686.0 30.6 %collective-permute-start.50 = (bf16[96,768]{1,0:T(8,128)(2,1)}, bf16[96,768]{1,0:T(8,128)(2,1)S(1)}, u32[]{:S(2)}, u32[]{:S(2)}) collective-permute-start(bf16[96,768]{1,0:T(8,128)(2,1)} %get-tuple-element.355), channel_id=1, source_target_pairs={{0,3},{1,2},{2,1},{3,0},{4,7},{5,6},{6,5},{7,4},{8,11},{9,10},{10,... | collective-permute-start | bytes 442376 | tf_op jit(solution)/shard_map/ppermute | solution.py:887
  723.0 25.6 %collective-permute-start.52 = (bf16[192,768]{1,0:T(8,128)(2,1)S(1)}, bf16[192,768]{1,0:T(8,128)(2,1)S(1)}, u32[]{:S(2)}, u32[]{:S(2)}) collective-permute-start(bf16[192,768]{1,0:T(8,128)(2,1)S(1)} %pad_maximum_fusion.11), channel_id=1, source_target_pairs={{0,4},{4,0},{8,12},{12,8},{1,5},{5,1},{9,13},{13,9},{2,6},{6,2},{1... | collective-permute-start | bytes 884744 | tf_op jit(solution)/shard_map/ppermute | solution.py:887
  738.8 42.0 %collective-permute-start.54 = (bf16[192,1728]{1,0:T(8,128)(2,1)}, bf16[192,1728]{1,0:T(8,128)(2,1)}, u32[]{:S(2)}, u32[]{:S(2)}) collective-permute-start(bf16[192,1728]{1,0:T(8,128)(2,1)} %pad_maximum_fusion.6), channel_id=1, source_target_pairs={{0,4},{4,0},{8,12},{12,8},{1,5},{5,1},{9,13},{13,9},{2,6},{6,2},{1... | collective-permute-start | bytes 1990664 | tf_op jit(solution)/shard_map/ppermute | solution.py:887
  753.7 23.5 %collective-permute-start.45 = (bf16[96,576]{1,0:T(8,128)(2,1)S(1)}, bf16[96,576]{1,0:T(8,128)(2,1)S(1)}, u32[]{:S(2)}, u32[]{:S(2)}) collective-permute-start(bf16[96,576]{1,0:T(8,128)(2,1)S(1)} %collective-permute-done.44), channel_id=1, source_target_pairs={{0,12},{4,8},{8,4},{12,0},{1,13},{5,9},{9,5},{13,1},{2,14},{6,10},... | collective-permute-start | bytes 331784 | tf_op jit(solution)/shard_map/ppermute | solution.py:887
  (71 other events, 991.5 us)
Sparse Core Ops, SparseCore 0:
  60.2 90.1 all-gather.3
  153.9 118.6 all-gather.5
  385.8 86.6 all-gather.7

commit v3 on v2

--- a/solution.py
+++ b/solution.py
@@ -19,6 +19,7 @@
 
 KEYS = 512
 QUERIES = 1024
+CROSS = 1024
 VMEM_LIMIT = 56 * 2**20
 
 bf16 = jnp.bfloat16
@@ -69,7 +70,7 @@
 
 
 def self_forward_kernel(meta_ref, x_ref, *refs, begin):
-    out_refs, (total_ref, keys, values, held) = refs[:-4], refs[-4:]
+    out_refs, (total_ref, keys, values, even, odd) = refs[:-5], refs[-5:]
     length = meta_ref[UNIT_LENGTHS + begin + pl.program_id(0)]
     places = x_ref.shape[2]
     quarter_tiles = out_refs[0].shape[2] // QUERIES
@@ -100,27 +101,37 @@
             axis=0,
         )
 
-        def score(tile):
-            start = pl.multiple_of(tile * KEYS, KEYS)
+        def score(tile, held):
+            start = pl.multiple_of(jnp.minimum(tile, key_tiles - 1) * KEYS, KEYS)
             scores = dot_nn(keys[pl.ds(start, KEYS), :], queries)
-            held[lax.rem(tile, 2)] = scores
+            held[...] = scores
             return jnp.max(scores, axis=0, keepdims=True)
 
-        def step(tile, carry):
+        def step(tile, held, carry):
             largest, total, next_largest = carry
             updated = jnp.maximum(largest, next_largest)
             start = pl.multiple_of(tile * KEYS, KEYS)
-            chances = jnp.exp2(held[lax.rem(tile, 2)] - updated).astype(bf16)
+            chances = jnp.exp2(held[...] - updated).astype(bf16)
             total = total * jnp.exp2(largest - updated) + dot_nn(
                 values[:, pl.ds(start, KEYS)], chances
             )
-            return updated, total, score(jnp.minimum(tile + 1, key_tiles - 1))
-
+            return updated, total
+
+        def two_steps(pair, carry):
+            upper = score(2 * pair + 1, odd)
+            carry = step(2 * pair, even, carry)
+            lower = score(2 * pair + 2, even)
+            return *step(2 * pair + 1, odd, (*carry, upper)), lower
+
+        count = jnp.minimum(index * per_query, key_tiles)
         largest = jnp.full((1, QUERIES), NEGATIVE, f32)
         total = jnp.zeros((HEAD_DIM + 16, QUERIES), f32)
-        largest, total, _ = lax.fori_loop(
-            0, jnp.minimum(index * per_query, key_tiles), step, (largest, total, score(0))
-        )
+        carry = lax.fori_loop(0, count // 2, two_steps, (largest, total, score(0, even)))
+
+        def last_step_of(_, carry):
+            return *step(count - 1, even, carry), carry[2]
+
+        largest, total, _ = lax.fori_loop(0, lax.rem(count, 2), last_step_of, carry)
 
         def part(low, high, start, size, largest, total):
             scores = dot_nn(keys[pl.ds(start, size), :], queries[:, low:high])
@@ -175,7 +186,8 @@
             scratch_shapes=[
                 pltpu.VMEM((places, 128), bf16),
                 pltpu.VMEM((HEAD_DIM + 16, places), bf16),
-                pltpu.VMEM((2, KEYS, QUERIES), f32),
+                pltpu.VMEM((KEYS, QUERIES), f32),
+                pltpu.VMEM((KEYS, QUERIES), f32),
             ],
         ),
         out_shape=[jax.ShapeDtypeStruct((units, HEAD_DIM, quarter), bf16)] * quarters
@@ -327,14 +339,14 @@
     values = jnp.concatenate(
         [pair_ref[0, 0, HEAD_DIM:, :], jnp.ones((16, pair_ref.shape[3]), bf16)], axis=0
     )
-    for start in range(0, places, KEYS):
-        scores = dot_nn(keys, query_ref[:, start : start + KEYS])
+    for start in range(0, places, CROSS):
+        scores = dot_nn(keys, query_ref[:, start : start + CROSS])
         largest = jnp.max(scores, axis=0, keepdims=True)
         chances = jnp.exp2(scores - largest).astype(bf16)
         total = dot_nn(values, chances)
         row_total = total[HEAD_DIM : HEAD_DIM + 1]
-        out_ref[:, start : start + KEYS] = (total[:HEAD_DIM] / row_total).astype(bf16)
-        total_ref[0, :, start : start + KEYS] = largest + jnp.log2(row_total)
+        out_ref[:, start : start + CROSS] = (total[:HEAD_DIM] / row_total).astype(bf16)
+        total_ref[0, :, start : start + CROSS] = largest + jnp.log2(row_total)
 
 
 def pair_spec(pairs):
@@ -626,7 +638,9 @@
                 tokens,
                 whole_spec(norms),
                 whole_spec(out_w),
-                whole_spec(feed),
+                pl.BlockSpec(
+                    (groups, width, 2 * width), lambda b, n: (0, 0, 0), pipeline_mode=pl.Buffered(1)
+                ),
                 tokens,
             ],
             out_specs=[tokens, tokens, wide, wide, tokens, tokens, tokens, turned]
@@ -701,11 +715,12 @@
 
 def hidden_kernel(meta_ref, back_ref, weight_ref, *refs):
     groups = weight_ref.shape[0]
-    whole_refs, part_refs, out_ref = refs[: -1 - groups], refs[-1 - groups : -1], refs[-1]
+    whole_ref, part_refs, out_ref = refs[0], refs[1:-1], refs[-1]
     total = back_ref[...]
     for at in range(groups):
         group = meta_ref[CONTEXT] ^ at
-        part = jnp.concatenate([ref[group] for ref in whole_refs] + [part_refs[at][...]], axis=0)
+        part = [whole_ref[group]] + [ref[...] for ref in part_refs[at::groups]]
+        part = jnp.concatenate(part, axis=0)
         total = total + dot_tt(part, weight_ref[group])
     out_ref[...] = total.astype(bf16)
 
@@ -980,6 +995,10 @@
         self.terms = [add_up(self.terms).astype(bf16)]
         return self.terms[0]
 
+    def over_tensor_at_once(self):
+        self.send = add_up(self.terms).astype(bf16)
+        self.terms = [exchange(self.send, "tp")]
+
     def over_tensor(self):
         self.send = add_up(self.terms).astype(bf16)
         index = lax.axis_index("tp")
@@ -1072,33 +1091,24 @@
     owned = (owner_tensor == tensor_index)[:, None]
     picked = jnp.where(owned, jnp.take(bank[0], local_rows, axis=0), jnp.zeros((), bf16))
 
-    half = device_places // 2
-    own_self = lax.ppermute(local_self.T, ("ctx", "tp"), swap)
-    low, far = [], []
-    for at in range(2):
-        part = hidden[:, at * half : (at + 1) * half]
-        part = exchange(after(part, own_self) if at else part, "tp").reshape(quarter // 2, model_width)
-        low.append(part)
-        far.append(turn(after(part, *far), "ctx", 2))
-    own_self = gather(own_self, "shard", 1)
-    far[1] = after(far[1], own_self)
-    x_low = low[1]
-    beside = [turn(part, "ctx", 1) for part in low]
-    across = [turn(part, "ctx", 1) for part in far]
+    x_low = exchange(hidden, "tp").reshape(quarter, model_width)
+    own_self = gather(lax.ppermute(local_self.T, ("ctx", "tp"), swap), "shard", 1)
+    far = after(turn(x_low, "ctx", 2), own_self, picked, meta)
+    x_parts = [x_low, turn(x_low, "ctx", 1), far, turn(far, "ctx", 1)]
     picked = exchange(after(picked, x_low).reshape(tensor_count, -1, model_width), "tp")
-    x_all, projected = project(meta, own_self, low + beside + far + across, 2, half)
+    x_all, projected = project(meta, own_self, x_parts, 1, device_places)
     projected = projected.reshape(units, 3 * HEAD_DIM, -1)
 
     norms = jnp.concatenate([norm_gain, norm_bias], axis=0).T
-    bundle = jnp.concatenate([out_self.T, query_cross, out_cross.T, local_pair, norms], axis=1)
-    bundle = gather_all(after(bundle, x_low))
+    bundle = [up_weight, down_weight.T, out_self.T, query_cross, out_cross.T, local_pair, norms]
+    feed = gather_all(after(jnp.concatenate(bundle, axis=1), x_low))
+    bundle = feed[:, :, 2 * feed_width :]
     out_self_t = bundle[:, :, :group_width]
     query_cross_w = bundle[:, :, group_width : 2 * group_width]
     out_cross_t = bundle[:, :, 2 * group_width : 3 * group_width]
     pair_w = bundle[:, :, 3 * group_width : 3 * group_width + pair_width]
     norm_rows = bundle[0, :, 3 * group_width + pair_width :].T.astype(f32)
     norm_rows = jnp.pad(norm_rows, ((0, 2), (0, 0)))
-    feed = gather_all(after(jnp.concatenate([up_weight, down_weight.T], axis=1), x_low))
 
     self_out, self_totals, self_att = [], [], []
 
@@ -1109,20 +1119,22 @@
         self_att.extend(piece.reshape(-1, quarter) for piece in to_others(out, "ctx"))
         return total
 
-    picked = jnp.sum(after(picked, projected).astype(f32), axis=0).astype(bf16)
-    done = forward(0, picked)
+    done = forward(1, forward(0))
+    picked = jnp.sum(after(picked, done).astype(f32), axis=0).astype(bf16)
+    done = forward(2, picked, done, *self_att[:context_count])
+    self_att[context_count : 2 * context_count] = [
+        after(piece, done) for piece in self_att[context_count : 2 * context_count]
+    ]
     picked = after(lax.ppermute(picked, ("ctx", "tp"), swap), done)
-    done = forward(1, picked, done)
     lists = [picked] + [turn(picked, "ctx", at) for at in range(1, context_count)]
-    lists = [after(piece, done) for piece in lists]
-    done = forward(2, *lists, done)
+    cot = exchange(after(cotangent, *self_att[-context_count:]), "tp")
+    first_sum, first_low, cross_query, first_totals = first_step(
+        meta, after(x_all, picked), norm_rows, out_self_t, query_cross_w, self_att, device_places
+    )
+    lists = [after(piece, first_low) for piece in lists]
     selected = jnp.concatenate(in_slots(lists, context_index))
-    cot = exchange(after(cotangent, done), "tp")
     pairs = product("tdf,kd->tfk", pair_w, selected).astype(bf16)
     pairs = pairs.reshape(context_count, units, 2 * HEAD_DIM, retrieved)
-    first_sum, first_low, cross_query, first_totals = first_step(
-        meta, after(x_all, pairs), norm_rows, out_self_t, query_cross_w, self_att, device_places
-    )
     cross_att, cross_total = cross_forward(meta, cross_query, pairs)
     cot = after(cot, cross_att).reshape(quarter, model_width)
     fed = feed_step(meta, cross_att, first_sum, norm_rows, out_cross_t, feed, cot, device_places)
@@ -1206,47 +1218,52 @@
     own_grads = []
     for running in (feed_sum, mixed_sum):
         running.beside(grads[1][0])
-    feed_sum.over_tensor()
+    feed_sum.over_tensor_at_once()
     mixed_sum.over_x()
 
-    back_parts.append(exchange(jnp.concatenate(in_slots(grads[1], context_index)), "ctx"))
+    back_parts += parts_of(grads[1])
     ready = (feed_sum.send, mixed_sum.send, back_parts[0], *back_rows)
     grads.append(backward(2, *ready, *grads[1]))
-    back_parts[1] = after(back_parts[1], grads[2][0])
-    for running in (feed_sum, mixed_sum):
-        running.beside(grads[2][0])
+    back_parts[2:] = [after(part, grads[2][0]) for part in back_parts[2:]]
+    feed_sum.terms = [jnp.sum(after(feed_sum.terms[0], grads[2][0]).astype(f32), axis=0)]
+    mixed_sum.beside(grads[2][0])
     back_parts += parts_of(grads[2])
-    ready = (feed_sum.total(), mixed_sum.send_of_quarter(), back_parts[1])
+    mixed_sum.over_tensor()
+    own_grads = []
+    ready = (feed_sum.total(), *back_parts[2:5])
     for at in range(units):
         own_grads.append(
             own_grad(meta, after(x_all, *ready), [p.reshape(-1, quarter) for p in grads[at]])
         )
-    mixed_sum.terms = [after(term, back_parts[-1]) for term in mixed_sum.terms]
-    mixed_sum.over_tensor()
-    mixed_sum.total()
-    rows_steps = sum_everywhere(after(rows, own_grads[2]))
-
     own_sum = jnp.concatenate(own_grads, axis=1)
     own_sum = own_sum.reshape(shard_count, -1, own_sum.shape[1])
+    back_hidden = hidden_step(
+        meta, after(back_first_sum, own_sum), self_w, back_parts, device_places
+    )
+
     if shard_count == 2:
         mine = lax.dynamic_index_in_dim(own_sum, shard_index, 0, keepdims=False)
         other = lax.dynamic_index_in_dim(own_sum, 1 - shard_index, 0, keepdims=False)
-        own_sum = add_up([mine, turn(other, "shard", 1)])
+        own_sum = add_up([mine, after(turn(other, "shard", 1), back_hidden)])
     else:
         own_sum = jnp.sum(exchange(own_sum, "shard").astype(f32), axis=0)
+    mixed_sum.beside(back_hidden)
+    mixed_sum.total()
     own_sum = own_sum.astype(bf16).reshape(tensor_count, -1, own_sum.shape[-1])
     own_sum = [
         lax.dynamic_index_in_dim(own_sum, tensor_index ^ at, 0, keepdims=False)
         for at in range(tensor_count)
     ]
-    own_sum = add_up(to_others(own_sum, "tp")).astype(bf16)
-    own_sum = lax.ppermute(own_sum, ("ctx", "tp"), swap)
-
-    back_hidden = hidden_step(meta, back_first_sum, self_w, back_parts, device_places)
-    back_rows = jnp.concatenate(in_slots([after(p, back_hidden, own_sum) for p in back_rows], tensor_index))
+    back_rows = [after(piece, back_hidden, mixed_sum.send, *own_sum) for piece in back_rows]
+    back_rows = jnp.concatenate(in_slots(back_rows, tensor_index))
     back_hidden = exchange(back_hidden.reshape(tensor_count, device_places, model_width), "tp")
     back_rows = jnp.where(owned, back_rows.astype(f32), 0.0)
     back_bank = jnp.zeros(bank.shape[1:], f32).at[local_rows].add(back_rows)[None]
+    own_sum = to_others(own_sum, "tp")
+    own_sum = [own_sum[0]] + [after(piece, back_bank) for piece in own_sum[1:]]
+    own_sum = add_up(own_sum).astype(bf16)
+    own_sum = lax.ppermute(own_sum, ("ctx", "tp"), swap)
+    rows_steps = sum_everywhere(after(rows, back_bank))
 
     own_all = gather_direct(own_sum, "ctx", 0)
     back_mixed = mixed_sum.spread()

time: 807 us -> 743 us (0.921)
  starting transfers between devices: 188 us -> 116 us
  Pallas kernels: 297 us -> 346 us
  blocking collectives: 28.1 us -> 0 us
  waiting for transfers between devices: 132 us -> 117 us
    ppermute x56 -> x53, starting transfers between devices: 126 us -> 78.7 us  [turn(): return lax.ppermute(array, axis, [(at, at ^ step) for at in range(count)])]
    pallas_call x3, Pallas kernels: 37.5 us -> 81.5 us  [self_backward(): pl.pallas_call(functools.partial(self_backward_kernel, begin=begin), grid...]
    ppermute x56 -> x53, waiting for transfers between devices: 106 us -> 73.3 us  [turn(): return lax.ppermute(array, axis, [(at, at ^ step) for at in range(count)])]
    all_to_all x1 -> x0, blocking collectives: 28.1 us -> none  [exchange(): return lax.all_to_all(parts, axes, split_axis=0, concat_axis=0, tiled=True)]
    all_to_all x8, starting transfers between devices: 59.8 us -> 35 us  [exchange(): return lax.all_to_all(parts, axes, split_axis=0, concat_axis=0, tiled=True)]
    all_to_all x8, waiting for transfers between devices: 26.3 us -> 43.5 us  [exchange(): return lax.all_to_all(parts, axes, split_axis=0, concat_axis=0, tiled=True)]
    pallas_call x3, Pallas kernels: 49.9 us -> 60 us  [self_forward(): pl.pallas_call(functools.partial(self_forward_kernel, begin=begin), grid_...]
    unnamed x106 -> x119, local copies, waits for them, and re-layouts: 14.1 us -> 16.4 us
  transfers between devices with their start and end apart: 71 -> 67, of which waited for: 17 -> 14; matrix products, arithmetic and copies ran while one was open for 15% -> 17% of each run, Pallas kernels for 29% -> 38%
where the time goes in v3:
time: 743 us; the launch traced here: 731 us
  Pallas kernels  346 us (47%)
  waiting for transfers between devices  117 us (16%)
  starting transfers between devices  116 us (16%)
  other arithmetic  64.5 us (9%)
  local copies, waits for them, and re-layouts  55.2 us (7%)
  matrix products  16.1 us (2%)
  between operations  16 us (2%)
    pallas_call x3, Pallas kernels, self_backward(): pl.pallas_call(functools.partial(self_backward_kernel, begin=begin), grid...  81.5 us
    ppermute x53, starting transfers between devices, turn(): return lax.ppermute(array, axis, [(at, at ^ step) for at in range(count)])  78.7 us
    ppermute x53, waiting for transfers between devices, turn(): return lax.ppermute(array, axis, [(at, at ^ step) for at in range(count)])  73.3 us
    pallas_call x3, Pallas kernels, self_forward(): pl.pallas_call(functools.partial(self_forward_kernel, begin=begin), grid_...  60 us
    all_to_all x8, waiting for transfers between devices, exchange(): return lax.all_to_all(parts, axes, split_axis=0, concat_axis=0, tiled=True)  43.5 us
    pallas_call x1, Pallas kernels, feed_step(): pl.pallas_call(functools.partial(feed_kernel, quarter=quarter), grid_spec...  42.1 us
    pallas_call x1, Pallas kernels, cross_backward(): pl.pallas_call(cross_backward_kernel, grid_spec=pltpu.PrefetchScalarGridS...  37.4 us
    all_to_all x8, starting transfers between devices, exchange(): return lax.all_to_all(parts, axes, split_axis=0, concat_axis=0, tiled=True)  35 us
  transfers between devices with their start and end apart: 67, of which 14 were waited for; matrix products, arithmetic and copies ran while one was open for 17% of the time, Pallas kernels for 38%

profile of v3, /device:TPU:0, one launch (start us, length us, event | category | flops | bytes accessed | tf_op | source)
XLA Modules:
  0.0 730.7 jit_solution(12097260651784695127)
XLA Ops:
  7.2 6.5 all-to-all-start
  17.6 33.1 %all-to-all-done = bf16[4,256,768]{2,1,0:T(8,128)(2,1)} async-done(((bf16[4,256,768]{2,1,0:T(8,128)(2,1)}), bf16[4,256,768]{2,1,0:T(8,128)(2,1)}, u32[]{:S(2)}, u32[]{:S(2)}) %all-to-all-start) | async-done | bytes 1572896 | tf_op jit(solution)/shard_map/all_to_all | solution.py:939
  56.2 8.2 %gather_fusion = bf16[1024,768]{1,0:T(8,128)(2,1)S(1)} fusion(bf16[4096,768]{1,0:T(8,128)(2,1)} %bitcast.155, s32[1024]{0:T(1024)S(1)} %broadcast_clamp_fusion), kind=kCustom, calls=%fused_computation | custom fusion | bytes 3149824 | tf_op jit(solution)/shard_map/jit(_take)/gather | solution.py:1092
  70.7 5.2 collective-permute-done.1
  77.0 6.9 collective-permute-start.2
  83.8 26.6 %collective-permute-done.3.refs_2_ = bf16[1024,768]{1,0:T(8,128)(2,1)} collective-permute-done((bf16[1024,768]{1,0:T(8,128)(2,1)}, bf16[1024,768]{1,0:T(8,128)(2,1)}, u32[]{:S(2)}, u32[]{:S(2)}) %collective-permute-start.3) | collective-permute-done | bytes 1572896 | tf_op jit(solution)/shard_map/ppermute | solution.py:902
  110.4 3.6 all-to-all-start.1
  115.1 11.9 %project.1 = (bf16[4096,768]{1,0:T(8,128)(2,1)}, bf16[576,4096]{1,0:T(8,128)(2,1)}) custom-call(s32[6]{0:T(128)} %stack.24.meta_ref, bf16[576,768]{1,0:T(8,128)(2,1)} %pad_maximum_fusion.3.weight_ref, bf16[1024,768]{1,0:T(8,128)(2,1)} %bitcast.10.refs_0_, bf16[1024,768]{1,0:T(8,128)(2,1)} %copy-done.38, bf16[1024,768]{1,0:T(8,128)(2,1)} %collective-permute-done.3.refs_2_, ...), custom_call_target="tpu_custom_call" | custom-call | flops 11000000512 | tf_op jit(solution)/shard_map/project/pallas_call | solution.py:484
  127.1 19.8 %self_forward.3 = (bf16[1,64,1024]{2,1,0:T(8,128)(2,1)}, bf16[1,64,1024]{2,1,0:T(8,128)(2,1)}, bf16[1,64,1024]{2,1,0:T(8,128)(2,1)}, bf16[1,64,1024]{2,1,0:T(8,128)(2,1)}, f32[1,1,4096]{2,1,0:T(1,128)}) custom-call(s32[6]{0:T(128)} %stack.24.meta_ref, bf16[3,192,4096]{2,1,0:T(8,128)(2,1)} %bitcast.220), custom_call_target="tpu_custom_call" | custom-call | flops 22000001024 | tf_op jit(solution)/shard_map/self_forward/pallas_call | solution.py:178
  149.9 20.3 %self_forward.4 = (bf16[1,64,1024]{2,1,0:T(8,128)(2,1)}, bf16[1,64,1024]{2,1,0:T(8,128)(2,1)}, bf16[1,64,1024]{2,1,0:T(8,128)(2,1)}, bf16[1,64,1024]{2,1,0:T(8,128)(2,1)}, f32[1,1,4096]{2,1,0:T(1,128)}) custom-call(s32[6]{0:T(128)} %stack.24.meta_ref, bf16[3,192,4096]{2,1,0:T(8,128)(2,1)} %bitcast.221), custom_call_target="tpu_custom_call" | custom-call | flops 22000001024 | tf_op jit(solution)/shard_map/self_forward/pallas_call | solution.py:178
  170.2 10.4 %all-to-all-done.1 = bf16[4,256,768]{2,1,0:T(8,128)(2,1)S(1)} async-done(((bf16[4,256,768]{2,1,0:T(8,128)(2,1)}), bf16[4,256,768]{2,1,0:T(8,128)(2,1)S(1)}, u32[]{:S(2)}, u32[]{:S(2)}) %all-to-all-start.1) | async-done | bytes 1572896 | tf_op jit(solution)/shard_map/all_to_all | solution.py:939
  183.6 19.8 %self_forward.5 = (bf16[1,64,1024]{2,1,0:T(8,128)(2,1)}, bf16[1,64,1024]{2,1,0:T(8,128)(2,1)}, bf16[1,64,1024]{2,1,0:T(8,128)(2,1)}, bf16[1,64,1024]{2,1,0:T(8,128)(2,1)}, f32[1,1,4096]{2,1,0:T(1,128)}) custom-call(s32[6]{0:T(128)} %stack.24.meta_ref, bf16[3,192,4096]{2,1,0:T(8,128)(2,1)} %bitcast.222), custom_call_target="tpu_custom_call" | custom-call | flops 22000001024 | tf_op jit(solution)/shard_map/self_forward/pallas_call | solution.py:178
  206.5 5.1 collective-permute-done.13
  214.0 4.7 all-to-all-start.2
  220.6 5.9 fusion.40
  228.3 12.5 %first_step.1 = (f32[1024,768]{1,0:T(8,128)}, bf16[1024,768]{1,0:T(8,128)(2,1)}, bf16[768,1024]{1,0:T(8,128)(2,1)}, f32[8,768]{1,0:T(8,128)}) custom-call(s32[6]{0:T(128)} %stack.24.meta_ref, bf16[4096,768]{1,0:T(8,128)(2,1)} %get-tuple-element.226.x_ref, f32[8,768]{1,0:T(8,128)} %copy.176.norm_ref, bf16[4,768,192]{2,1,0:T(8,128)(2,1)} %get-tuple-element.348.out_w_ref, ...), custom_call_target="tpu_custom_call" | custom-call | flops 8800000000 | tf_op jit(solution)/shard_map/first_step/pallas_call | solution.py:532
  243.7 8.8 %convolution_convert_fusion = bf16[4,384,1024]{2,1,0:T(8,128)(2,1)} fusion(bf16[4,768,2502]{2,1,0:T(8,128)(2,1)} %bitcast.168, bf16[256,768]{1,0:T(8,128)(2,1)S(1)} %get-tuple-element.360, bf16[256,768]{1,0:T(8,128)(2,1)S(1)} %get-tuple-element.359, bf16[256,768]{1,0:T(8,128)(2,1)S(1)} %get-tuple-element.358, bf16[256,768]{1,0:T(8,128)(2,1)S(1)} %get-tuple-element.357), kind=kOutput, calls=%fused_computation.18 | convolution fusion | flops 2423783424 | bytes 7077888 | tf_op jit(solution)/shard_map/tdf,kd->tfk/dot_general | solution.py:897
  252.4 21.5 %cross_forward.1 = (bf16[768,1024]{1,0:T(8,128)(2,1)}, f32[12,1,1024]{2,1,0:T(1,128)}) custom-call(s32[6]{0:T(128)} %stack.24.meta_ref, bf16[768,1024]{1,0:T(8,128)(2,1)} %get-tuple-element.162.query_ref, bf16[4,3,128,1024]{3,2,1,0:T(8,128)(2,1)} %bitcast.226), custom_call_target="tpu_custom_call" | custom-call | flops 27499999232 | tf_op jit(solution)/shard_map/cross_forward/pallas_call | solution.py:364
  275.1 42.1 %feed_step.1 = (bf16[1024,768]{1,0:T(8,128)(2,1)}, bf16[1024,768]{1,0:T(8,128)(2,1)}, bf16[1024,3072]{1,0:T(8,128)(2,1)}, bf16[1024,3072]{1,0:T(8,128)(2,1)}, bf...) custom-call(s32[6]{0:T(128)} %stack.24.meta_ref, ...), custom_call_target="tpu_custom_call" | custom-call | flops 49500000256 | tf_op jit(solution)/shard_map/feed_step/pallas_call | solution.py:631
  317.2 25.3 %feed_grad.1 = (bf16[4,2,192,1728]{3,2,1,0:T(8,128)(2,1)}, bf16[4,2,192,1728]{3,2,1,0:T(8,128)(2,1)}) custom-call(s32[6]{0:T(128)} %stack.24.meta_ref, bf16[1024,768]{1,0:T(8,128)(2,1)} %get-tuple-element.174.low_ref, bf16[1024,3072]{1,0:T(8,128)(2,1)} %get-tuple-element.175.inner_ref, bf16[1024,768]{1,0:T(8,128)(2,1)} %get-tuple-element.176.back_ref, ...), custom_call_target="tpu_custom_call" | custom-call | flops 19800000512 | tf_op jit(solution)/shard_map/feed_grad/pallas_call | solution.py:794
  344.2 5.1 all-to-all-start.3
  349.3 37.4 %cross_backward.1 = (bf16[768,1024]{1,0:T(8,128)(2,1)}, bf16[4,3,128,1024]{3,2,1,0:T(8,128)(2,1)}) custom-call(s32[6]{0:T(128)} %stack.24.meta_ref, bf16[768,1024]{1,0:T(8,128)(2,1)} %get-tuple-element.162.query_ref, bf16[4,3,128,1024]{3,2,1,0:T(8,128)(2,1)} %bitcast.227, bf16[768,1024]{1,0:T(8,128)(2,1)} %get-tuple-element.168.att_ref.cross_ref.out_ref, ...), custom_call_target="tpu_custom_call" | custom-call | flops 39600001024 | tf_op jit(solution)/shard_map/cross_backward/pallas_call | solution.py:413
  391.8 7.3 bitcast_convert_fusion
  399.1 3.6 all-to-all-start.4
  402.7 4.8 fusion.4
  407.5 12.5 %last_step.1 = (bf16[192,1024]{1,0:T(8,128)(2,1)}, bf16[192,1024]{1,0:T(8,128)(2,1)}, bf16[192,1024]{1,0:T(8,128)(2,1)}, bf16[192,1024]{1,0:T(8,128)(2,1)}, f32[...) custom-call(s32[6]{0:T(128)} %stack.24.meta_ref, bf16[768,1024]{1,0:T(8,128)(2,1)} %get-tuple-element.182.query_ref, ...), custom_call_target="tpu_custom_call" | custom-call | flops 8800000000 | tf_op jit(solution)/shard_map/last_step/pallas_call | solution.py:688
  422.2 14.2 %mixed_grad.1 = (bf16[4,2,192,768]{3,2,1,0:T(8,128)(2,1)}, bf16[4,2,192,768]{3,2,1,0:T(8,128)(2,1)}) custom-call(s32[6]{0:T(128)} %stack.24.meta_ref, bf16[1024,768]{1,0:T(8,128)(2,1)} %get-tuple-element.188.one_ref, bf16[1024,768]{1,0:T(8,128)(2,1)} %get-tuple-element.163.low_ref, bf16[1024,768]{1,0:T(8,128)(2,1)} %pad_maximum_fusion.selected_ref, ...), custom_call_target="tpu_custom_call" | custom-call | flops 15399999488 | tf_op jit(solution)/shard_map/mixed_grad/pallas_call | solution.py:845
  440.2 8.4 %collective-permute-done.21 = bf16[192,1024]{1,0:T(8,128)(2,1)} collective-permute-done((bf16[192,1024]{1,0:T(8,128)(2,1)}, bf16[192,1024]{1,0:T(8,128)(2,1)}, u32[]{:S(2)}, u32[]{:S(2)}) %collective-permute-start.21) | collective-permute-done | bytes 393248 | tf_op jit(solution)/shard_map/ppermute | solution.py:902
  448.6 27.4 %self_backward.3 = (bf16[1,192,1024]{2,1,0:T(8,128)(2,1)}, bf16[1,192,1024]{2,1,0:T(8,128)(2,1)}, bf16[1,192,1024]{2,1,0:T(8,128)(2,1)}, bf16[1,192,1024]{2,1,0:T(8,128)(2,1)}) custom-call(s32[6]{0:T(128)} %stack.24.meta_ref, bf16[3,192,4096]{2,1,0:T(8,128)(2,1)} %bitcast.223, f32[1,1,4096]{2,1,0:T(1,128)} %get-tuple-element.137.total_ref, ...), custom_call_target="tpu_custom_call" | custom-call | flops 32999999488 | tf_op jit(solution)/shard_map/self_backward/pallas_call | solution.py:308
  476.1 7.5 %collective-permute-start.28 = (bf16[256,768]{1,0:T(8,128)(2,1)S(1)}, bf16[256,768]{1,0:T(8,128)(2,1)}, u32[]{:S(2)}, u32[]{:S(2)}) collective-permute-start(bf16[256,768]{1,0:T(8,128)(2,1)S(1)} %collective-permute-done.22), channel_id=1, source_target_pairs={{0,2},{1,3},{2,0},{3,1},{4,6},{5,7},{6,4},{7,5},{8,10},{9,11},{10,... | collective-permute-start | bytes 1179656 | tf_op jit(solution)/shard_map/ppermute | solution.py:902
  486.9 4.4 all-to-all-start.6
  501.2 3.5 fusion.6
  504.7 7.4 %collective-permute-start.25 = (bf16[4,96,1728]{2,1,0:T(8,128)(2,1)}, bf16[4,96,1728]{2,1,0:T(8,128)(2,1)}, u32[]{:S(2)}, u32[]{:S(2)}) collective-permute-start(bf16[4,96,1728]{2,1,0:T(8,128)(2,1)} %fusion.6), channel_id=1, source_target_pairs={{0,8},{4,12},{8,0},{12,4},{1,9},{5,13},{9,1},{13,5},{2,10},{6,14},... | collective-permute-start | bytes 3981320 | tf_op jit(solution)/shard_map/ppermute | solution.py:902
  512.0 27.0 %self_backward.4 = (bf16[1,192,1024]{2,1,0:T(8,128)(2,1)}, bf16[1,192,1024]{2,1,0:T(8,128)(2,1)}, bf16[1,192,1024]{2,1,0:T(8,128)(2,1)}, bf16[1,192,1024]{2,1,0:T(8,128)(2,1)}) custom-call(s32[6]{0:T(128)} %stack.24.meta_ref, bf16[3,192,4096]{2,1,0:T(8,128)(2,1)} %bitcast.224, f32[1,1,4096]{2,1,0:T(1,128)} %get-tuple-element.139.total_ref, ...), custom_call_target="tpu_custom_call" | custom-call | flops 32999999488 | tf_op jit(solution)/shard_map/self_backward/pallas_call | solution.py:308
  545.8 3.8 fusion.9
  549.6 3.5 all-to-all-start.5
  553.1 27.2 %self_backward.5 = (bf16[1,192,1024]{2,1,0:T(8,128)(2,1)}, bf16[1,192,1024]{2,1,0:T(8,128)(2,1)}, bf16[1,192,1024]{2,1,0:T(8,128)(2,1)}, bf16[1,192,1024]{2,1,0:T(8,128)(2,1)}) custom-call(s32[6]{0:T(128)} %stack.24.meta_ref, bf16[3,192,4096]{2,1,0:T(8,128)(2,1)} %bitcast.225, f32[1,1,4096]{2,1,0:T(1,128)} %get-tuple-element.146.total_ref, ...), custom_call_target="tpu_custom_call" | custom-call | flops 32999999488 | tf_op jit(solution)/shard_map/self_backward/pallas_call | solution.py:308
  587.8 5.5 own_grad.3
  593.3 5.4 own_grad.4
  598.7 5.4 own_grad.5
  607.2 10.5 %hidden_step.1 = bf16[1024,768]{1,0:T(8,128)(2,1)} custom-call(s32[6]{0:T(128)} %stack.24.meta_ref, f32[1024,768]{1,0:T(8,128)} %get-tuple-element.230.back_ref, bf16[4,768,576]{2,1,0:T(8,128)(2,1)} %bitcast.194, bf16[4,192,1024]{2,1,0:T(8,128)(2,1)} %all-to-all-done.6.refs_0_, bf16[192,1024]{1,0:T(8,128)(2,1)} %bitcast.234, ...), custom_call_target="tpu_custom_call" | custom-call | flops 8800000000 | tf_op jit(solution)/shard_map/hidden_step/pallas_call | solution.py:736
  623.1 11.1 %collective-permute-start.40 = (bf16[384,576]{1,0:T(8,128)(2,1)}, bf16[384,576]{1,0:T(8,128)(2,1)}, u32[]{:S(2)}, u32[]{:S(2)}) collective-permute-start(bf16[384,576]{1,0:T(8,128)(2,1)} %dynamic-slice_bitcast_fusion.2), channel_id=1, source_target_pairs={{0,16},{16,0},{1,17},{17,1},{2,18},{18,2},{3,19},{19,3},{4,20},{20... | collective-permute-start | bytes 1327112 | tf_op jit(solution)/shard_map/ppermute | solution.py:902
  634.2 3.8 all-to-all-start.7
  640.9 4.3 collective-permute-done.40
  651.9 14.4 %scatter_custom_fusion = f32[4096,768]{1,0:T(8,128)} fusion(s32[1024]{0:T(1024)} %bitcast.192, f32[]{:T(128)} %constant.215.clone.1, bf16[256,768]{1,0:T(8,128)(2,1)} %get-tuple-element.352, bf16[]{:T(256)} %constant.225, bf16[256,768]{1,0:T(8,128)(2,1)} %get-tuple-element.351, bf16[256,768]{1,0:T(8,128)(2,1)S(1)} %get-tuple-element.350, ...), kind=kCustom, calls=%fused_computation.2 | custom fusion | flops 7864320 | bytes 14158336 | tf_op jit(solution)/shard_map/scatter-add | solution.py:1261
  676.2 7.6 %collective-permute-done.54 = f32[7,768]{1,0:T(8,128)S(1)} collective-permute-done((f32[7,768]{1,0:T(8,128)S(1)}, f32[7,768]{1,0:T(8,128)S(1)}, u32[]{:S(2)}, u32[]{:S(2)}) %collective-permute-start.54) | collective-permute-done | bytes 21536 | tf_op jit(solution)/shard_map/ppermute | solution.py:902
  695.0 8.0 %collective-permute-start.45 = (bf16[96,576]{0,1:T(8,128)(2,1)S(1)}, bf16[96,576]{0,1:T(8,128)(2,1)S(1)}, u32[]{:S(2)}, u32[]{:S(2)}) collective-permute-start(bf16[96,576]{0,1:T(8,128)(2,1)S(1)} %collective-permute-done.44), channel_id=1, source_target_pairs={{0,12},{4,8},{8,4},{12,0},{1,13},{5,9},{9,5},{13,1},{2,14},{6,10},... | collective-permute-start | bytes 331784 | tf_op jit(solution)/shard_map/ppermute | solution.py:902
  706.0 5.5 collective-permute-done.46
  (311 shorter events, 130.4 us)
Async XLA Ops:
  7.2 43.5 %all-to-all-start = ((bf16[4,256,768]{2,1,0:T(8,128)(2,1)}), bf16[4,256,768]{2,1,0:T(8,128)(2,1)}, u32[]{:S(2)}, u32[]{:S(2)}) async-start(bf16[4,256,768]{2,1,0:T(8,128)(2,1)} %param.17), calls=%async_computation | async-start | bytes 3145728 | tf_op jit(solution)/shard_map/all_to_all | solution.py:939
  13.7 206.9 %all-gather.3.cloned.1.call-start = ((), (), s32[]{:S(2)}) async-start(), calls=%async_computation.8 | async-start | bytes 16220160 | tf_op jit(solution)/shard_map/all_gather | solution.py:1084
  51.6 58.8 %collective-permute-start.3 = (bf16[1024,768]{1,0:T(8,128)(2,1)}, bf16[1024,768]{1,0:T(8,128)(2,1)}, u32[]{:S(2)}, u32[]{:S(2)}) collective-permute-start(bf16[1024,768]{1,0:T(8,128)(2,1)} %bitcast.10.refs_0_), channel_id=1, source_target_pairs={{0,8},{4,12},{8,0},{12,4},{1,9},{5,13},{9,1},{13,5},{2,10},{6,14},... | collective-permute-start | bytes 4718600 | tf_op jit(solution)/shard_map/ppermute | solution.py:902
  77.0 37.0 %collective-permute-start.2 = (bf16[1024,768]{1,0:T(8,128)(2,1)}, bf16[1024,768]{1,0:T(8,128)(2,1)S(1)}, u32[]{:S(2)}, u32[]{:S(2)}) collective-permute-start(bf16[1024,768]{1,0:T(8,128)(2,1)} %bitcast.10.refs_0_), channel_id=1, source_target_pairs={{0,4},{4,0},{8,12},{12,8},{1,5},{5,1},{9,13},{13,9},{2,6},{6,2},{1... | collective-permute-start | bytes 4718600 | tf_op jit(solution)/shard_map/ppermute | solution.py:902
  110.4 70.1 %all-to-all-start.1 = ((bf16[4,256,768]{2,1,0:T(8,128)(2,1)}), bf16[4,256,768]{2,1,0:T(8,128)(2,1)S(1)}, u32[]{:S(2)}, u32[]{:S(2)}) async-start(bf16[4,256,768]{2,1,0:T(8,128)(2,1)} %bitcast.15), calls=%async_computation.1 | async-start | bytes 3145728 | tf_op jit(solution)/shard_map/all_to_all | solution.py:939
  146.9 35.6 %collective-permute-start.6 = (bf16[1,64,1024]{2,1,0:T(8,128)(2,1)}, bf16[1,64,1024]{2,1,0:T(8,128)(2,1)S(1)}, u32[]{:S(2)}, u32[]{:S(2)}) collective-permute-start(bf16[1,64,1024]{2,1,0:T(8,128)(2,1)} %get-tuple-element.142.refs_1_), channel_id=1, source_target_pairs={{0,4},{4,0},{8,12},{12,8},{1,5},{5,1},{9,13},{13,9},{2,6},{6,2},{1... | collective-permute-start | bytes 393224 | tf_op jit(solution)/shard_map/ppermute | solution.py:902
  147.4 35.5 %collective-permute-start.7 = (bf16[1,64,1024]{2,1,0:T(8,128)(2,1)}, bf16[1,64,1024]{2,1,0:T(8,128)(2,1)S(1)}, u32[]{:S(2)}, u32[]{:S(2)}) collective-permute-start(bf16[1,64,1024]{2,1,0:T(8,128)(2,1)} %get-tuple-element.143.refs_2_), channel_id=1, source_target_pairs={{0,8},{4,12},{8,0},{12,4},{1,9},{5,13},{9,1},{13,5},{2,10},{6,14},... | collective-permute-start | bytes 393224 | tf_op jit(solution)/shard_map/ppermute | solution.py:902
  149.9 33.7 %collective-permute-start.8 = (bf16[1,64,1024]{2,1,0:T(8,128)(2,1)}, bf16[1,64,1024]{2,1,0:T(8,128)(2,1)S(1)}, u32[]{:S(2)}, u32[]{:S(2)}) collective-permute-start(bf16[1,64,1024]{2,1,0:T(8,128)(2,1)} %get-tuple-element.144.refs_3_), channel_id=1, source_target_pairs={{0,12},{4,8},{8,4},{12,0},{1,13},{5,9},{9,5},{13,1},{2,14},{6,10},... | collective-permute-start | bytes 393224 | tf_op jit(solution)/shard_map/ppermute | solution.py:902
  180.5 24.5 %collective-permute-start.11 = (bf16[1,64,1024]{2,1,0:T(8,128)(2,1)}, bf16[1,64,1024]{2,1,0:T(8,128)(2,1)S(1)}, u32[]{:S(2)}, u32[]{:S(2)}) collective-permute-start(bf16[1,64,1024]{2,1,0:T(8,128)(2,1)} %get-tuple-element.156.refs_3_), channel_id=1, source_target_pairs={{0,12},{4,8},{8,4},{12,0},{1,13},{5,9},{9,5},{13,1},{2,14},{6,10},... | collective-permute-start | bytes 393224 | tf_op jit(solution)/shard_map/ppermute | solution.py:902
  180.5 25.7 %collective-permute-start.10 = (bf16[1,64,1024]{2,1,0:T(8,128)(2,1)}, bf16[1,64,1024]{2,1,0:T(8,128)(2,1)S(1)}, u32[]{:S(2)}, u32[]{:S(2)}) collective-permute-start(bf16[1,64,1024]{2,1,0:T(8,128)(2,1)} %get-tuple-element.154.refs_2_), channel_id=1, source_target_pairs={{0,8},{4,12},{8,0},{12,4},{1,9},{5,13},{9,1},{13,5},{2,10},{6,14},... | collective-permute-start | bytes 393224 | tf_op jit(solution)/shard_map/ppermute | solution.py:902
  182.6 23.9 %collective-permute-start.9 = (bf16[1,64,1024]{2,1,0:T(8,128)(2,1)S(1)}, bf16[1,64,1024]{2,1,0:T(8,128)(2,1)S(1)}, u32[]{:S(2)}, u32[]{:S(2)}) collective-permute-start(bf16[1,64,1024]{2,1,0:T(8,128)(2,1)S(1)} %copy-done.40), channel_id=1, source_target_pairs={{0,4},{4,0},{8,12},{12,8},{1,5},{5,1},{9,13},{13,9},{2,6},{6,2},{1... | collective-permute-start | bytes 393224 | tf_op jit(solution)/shard_map/ppermute | solution.py:902
  182.9 35.7 %collective-permute-start.5 = (bf16[256,768]{1,0:T(8,128)(2,1)S(1)}, bf16[256,768]{1,0:T(8,128)(2,1)S(1)}, u32[]{:S(2)}, u32[]{:S(2)}) collective-permute-start(bf16[256,768]{1,0:T(8,128)(2,1)S(1)} %reduce_sum.54), channel_id=1, source_target_pairs={{0,0},{1,4},{2,8},{3,12},{4,1},{5,5},{6,9},{7,13},{8,2},{9,6},{10,... | collective-permute-start | bytes 1179656 | tf_op jit(solution)/shard_map/ppermute | solution.py:1128
  214.0 60.0 %all-to-all-start.2 = ((bf16[4,256,768]{2,1,0:T(8,128)(2,1)}), bf16[4,256,768]{2,1,0:T(8,128)(2,1)S(1)}, u32[]{:S(2)}, u32[]{:S(2)}) async-start(bf16[4,256,768]{2,1,0:T(8,128)(2,1)} %param.21), calls=%async_computation.2 | async-start | bytes 3145728 | tf_op jit(solution)/shard_map/all_to_all | solution.py:939
  218.7 22.1 %collective-permute-start.17 = (bf16[256,768]{1,0:T(8,128)(2,1)S(1)}, bf16[256,768]{1,0:T(8,128)(2,1)S(1)}, u32[]{:S(2)}, u32[]{:S(2)}) collective-permute-start(bf16[256,768]{1,0:T(8,128)(2,1)S(1)} %collective-permute-done.5), channel_id=1, source_target_pairs={{0,4},{4,0},{8,12},{12,8},{1,5},{5,1},{9,13},{13,9},{2,6},{6,2},{1... | collective-permute-start | bytes 1179656 | tf_op jit(solution)/shard_map/ppermute | solution.py:902
  218.7 22.1 %collective-permute-start.16 = (bf16[256,768]{1,0:T(8,128)(2,1)S(1)}, bf16[256,768]{1,0:T(8,128)(2,1)S(1)}, u32[]{:S(2)}, u32[]{:S(2)}) collective-permute-start(bf16[256,768]{1,0:T(8,128)(2,1)S(1)} %collective-permute-done.5), channel_id=1, source_target_pairs={{0,8},{4,12},{8,0},{12,4},{1,9},{5,13},{9,1},{13,5},{2,10},{6,14},... | collective-permute-start | bytes 1179656 | tf_op jit(solution)/shard_map/ppermute | solution.py:902
  219.9 22.4 %collective-permute-start.15 = (bf16[256,768]{1,0:T(8,128)(2,1)S(1)}, bf16[256,768]{1,0:T(8,128)(2,1)}, u32[]{:S(2)}, u32[]{:S(2)}) collective-permute-start(bf16[256,768]{1,0:T(8,128)(2,1)S(1)} %collective-permute-done.5), channel_id=1, source_target_pairs={{0,12},{4,8},{8,4},{12,0},{1,13},{5,9},{9,5},{13,1},{2,14},{6,10},... | collective-permute-start | bytes 1179656 | tf_op jit(solution)/shard_map/ppermute | solution.py:902
  342.5 60.2 %collective-permute-start.18 = (bf16[4,2,192,1728]{3,2,1,0:T(8,128)(2,1)}, bf16[4,2,192,1728]{3,2,1,0:T(8,128)(2,1)}, u32[]{:S(2)}, u32[]{:S(2)}) collective-permute-start(bf16[4,2,192,1728]{3,2,1,0:T(8,128)(2,1)} %get-tuple-element.179), channel_id=1, source_target_pairs={{0,4},{4,0},{8,12},{12,8},{1,5},{5,1},{9,13},{13,9},{2,6},{6,2},{1... | collective-permute-start | bytes 15925256 | tf_op jit(solution)/shard_map/ppermute | solution.py:902
  344.2 54.9 %all-to-all-start.3 = ((bf16[4,256,768]{2,1,0:T(8,128)(2,1)}), bf16[4,256,768]{2,1,0:T(8,128)(2,1)S(1)}, u32[]{:S(2)}, u32[]{:S(2)}) async-start(bf16[4,256,768]{2,1,0:T(8,128)(2,1)} %bitcast.42), calls=%async_computation.3 | async-start | bytes 3145728 | tf_op jit(solution)/shard_map/all_to_all | solution.py:939
  349.3 257.8 %all-gather.5.cloned.1.call-start = ((), (), s32[]{:S(2)}) async-start(), calls=%async_computation.9 | async-start | bytes 4055040 | tf_op jit(solution)/shard_map/all_gather | solution.py:1084
  399.1 37.4 %all-to-all-start.4 = ((bf16[4,256,768]{2,1,0:T(8,128)(2,1)}), bf16[4,256,768]{2,1,0:T(8,128)(2,1)S(1)}, u32[]{:S(2)}, u32[]{:S(2)}) async-start(bf16[4,256,768]{2,1,0:T(8,128)(2,1)} %bitcast.165), calls=%async_computation.4 | async-start | bytes 3145728 | tf_op jit(solution)/shard_map/all_to_all | solution.py:939
  420.0 20.1 %collective-permute-start.19 = (bf16[192,1024]{1,0:T(8,128)(2,1)}, bf16[192,1024]{1,0:T(8,128)(2,1)}, u32[]{:S(2)}, u32[]{:S(2)}) collective-permute-start(bf16[192,1024]{1,0:T(8,128)(2,1)} %get-tuple-element.193), channel_id=1, source_target_pairs={{0,4},{4,0},{8,12},{12,8},{1,5},{5,1},{9,13},{13,9},{2,6},{6,2},{1... | collective-permute-start | bytes 1179656 | tf_op jit(solution)/shard_map/ppermute | solution.py:902
  422.2 26.3 %collective-permute-start.21 = (bf16[192,1024]{1,0:T(8,128)(2,1)}, bf16[192,1024]{1,0:T(8,128)(2,1)}, u32[]{:S(2)}, u32[]{:S(2)}) collective-permute-start(bf16[192,1024]{1,0:T(8,128)(2,1)} %get-tuple-element.195), channel_id=1, source_target_pairs={{0,12},{4,8},{8,4},{12,0},{1,13},{5,9},{9,5},{13,1},{2,14},{6,10},... | collective-permute-start | bytes 1179656 | tf_op jit(solution)/shard_map/ppermute | solution.py:902
  436.9 54.4 %collective-permute-start.24 = (bf16[4,2,192,768]{3,2,1,0:T(8,128)(2,1)}, bf16[4,2,192,768]{3,2,1,0:T(8,128)(2,1)}, u32[]{:S(2)}, u32[]{:S(2)}) collective-permute-start(bf16[4,2,192,768]{3,2,1,0:T(8,128)(2,1)} %get-tuple-element.189), channel_id=1, source_target_pairs={{0,4},{4,0},{8,12},{12,8},{1,5},{5,1},{9,13},{13,9},{2,6},{6,2},{1... | collective-permute-start | bytes 7077896 | tf_op jit(solution)/shard_map/ppermute | solution.py:902
  437.4 38.5 %collective-permute-start.22 = (bf16[256,768]{1,0:T(8,128)(2,1)S(1)}, bf16[256,768]{1,0:T(8,128)(2,1)S(1)}, u32[]{:S(2)}, u32[]{:S(2)}) collective-permute-start(bf16[256,768]{1,0:T(8,128)(2,1)S(1)} %reduce_sum.55), channel_id=1, source_target_pairs={{0,0},{1,4},{2,8},{3,12},{4,1},{5,5},{6,9},{7,13},{8,2},{9,6},{10,... | collective-permute-start | bytes 1179656 | tf_op jit(solution)/shard_map/ppermute | solution.py:1206
  440.1 61.1 %collective-permute-start.23 = (bf16[4,192,1728]{2,1,0:T(8,128)(2,1)}, bf16[4,192,1728]{2,1,0:T(8,128)(2,1)}, u32[]{:S(2)}, u32[]{:S(2)}) collective-permute-start(bf16[4,192,1728]{2,1,0:T(8,128)(2,1)} %fusion.4), channel_id=1, source_target_pairs={{0,16},{16,0},{1,17},{17,1},{2,18},{18,2},{3,19},{19,3},{4,20},{20... | collective-permute-start | bytes 7962632 | tf_op jit(solution)/shard_map/ppermute | solution.py:902
  476.0 63.0 %collective-permute-start.29 = (bf16[256,768]{1,0:T(8,128)(2,1)S(1)}, bf16[256,768]{1,0:T(8,128)(2,1)S(1)}, u32[]{:S(2)}, u32[]{:S(2)}) collective-permute-start(bf16[256,768]{1,0:T(8,128)(2,1)S(1)} %collective-permute-done.22), channel_id=1, source_target_pairs={{0,3},{1,2},{2,1},{3,0},{4,7},{5,6},{6,5},{7,4},{8,11},{9,10},{10,... | collective-permute-start | bytes 1179656 | tf_op jit(solution)/shard_map/ppermute | solution.py:902
  476.1 63.0 %collective-permute-start.28 = (bf16[256,768]{1,0:T(8,128)(2,1)S(1)}, bf16[256,768]{1,0:T(8,128)(2,1)}, u32[]{:S(2)}, u32[]{:S(2)}) collective-permute-start(bf16[256,768]{1,0:T(8,128)(2,1)S(1)} %collective-permute-done.22), channel_id=1, source_target_pairs={{0,2},{1,3},{2,0},{3,1},{4,6},{5,7},{6,4},{7,5},{8,10},{9,11},{10,... | collective-permute-start | bytes 1179656 | tf_op jit(solution)/shard_map/ppermute | solution.py:902
  483.5 55.5 %collective-permute-start.27 = (bf16[256,768]{1,0:T(8,128)(2,1)S(1)}, bf16[256,768]{1,0:T(8,128)(2,1)}, u32[]{:S(2)}, u32[]{:S(2)}) collective-permute-start(bf16[256,768]{1,0:T(8,128)(2,1)S(1)} %collective-permute-done.22), channel_id=1, source_target_pairs={{0,1},{1,0},{2,3},{3,2},{4,5},{5,4},{6,7},{7,6},{8,9},{9,8},{10,11... | collective-permute-start | bytes 1179656 | tf_op jit(solution)/shard_map/ppermute | solution.py:902
  486.9 52.1 %all-to-all-start.6 = ((bf16[4,192,1024]{2,1,0:T(8,128)(2,1)}), bf16[4,192,1024]{2,1,0:T(8,128)(2,1)}, u32[]{:S(2)}, u32[]{:S(2)}) async-start(bf16[4,192,1024]{2,1,0:T(8,128)(2,1)} %pad_maximum_fusion.1), calls=%async_computation.6 | async-start | bytes 3145728 | tf_op jit(solution)/shard_map/all_to_all | solution.py:939
  494.2 48.5 %collective-permute-start.26 = (bf16[4,192,768]{2,1,0:T(8,128)(2,1)}, bf16[4,192,768]{2,1,0:T(8,128)(2,1)}, u32[]{:S(2)}, u32[]{:S(2)}) collective-permute-start(bf16[4,192,768]{2,1,0:T(8,128)(2,1)} %fusion.25), channel_id=1, source_target_pairs={{0,16},{16,0},{1,17},{17,1},{2,18},{18,2},{3,19},{19,3},{4,20},{20... | collective-permute-start | bytes 3538952 | tf_op jit(solution)/shard_map/ppermute | solution.py:902
  504.7 41.1 %collective-permute-start.25 = (bf16[4,96,1728]{2,1,0:T(8,128)(2,1)}, bf16[4,96,1728]{2,1,0:T(8,128)(2,1)}, u32[]{:S(2)}, u32[]{:S(2)}) collective-permute-start(bf16[4,96,1728]{2,1,0:T(8,128)(2,1)} %fusion.6), channel_id=1, source_target_pairs={{0,8},{4,12},{8,0},{12,4},{1,9},{5,13},{9,1},{13,5},{2,10},{6,14},... | collective-permute-start | bytes 3981320 | tf_op jit(solution)/shard_map/ppermute | solution.py:902
  540.8 39.5 %collective-permute-start.32 = (bf16[1,192,1024]{2,1,0:T(8,128)(2,1)}, bf16[1,192,1024]{2,1,0:T(8,128)(2,1)S(1)}, u32[]{:S(2)}, u32[]{:S(2)}) collective-permute-start(bf16[1,192,1024]{2,1,0:T(8,128)(2,1)} %get-tuple-element.219), channel_id=1, source_target_pairs={{0,12},{4,8},{8,4},{12,0},{1,13},{5,9},{9,5},{13,1},{2,14},{6,10},... | collective-permute-start | bytes 1179656 | tf_op jit(solution)/shard_map/ppermute | solution.py:902
  540.8 39.4 %collective-permute-start.31 = (bf16[1,192,1024]{2,1,0:T(8,128)(2,1)}, bf16[1,192,1024]{2,1,0:T(8,128)(2,1)}, u32[]{:S(2)}, u32[]{:S(2)}) collective-permute-start(bf16[1,192,1024]{2,1,0:T(8,128)(2,1)} %get-tuple-element.218), channel_id=1, source_target_pairs={{0,8},{4,12},{8,0},{12,4},{1,9},{5,13},{9,1},{13,5},{2,10},{6,14},... | collective-permute-start | bytes 1179656 | tf_op jit(solution)/shard_map/ppermute | solution.py:902
  542.5 37.8 %collective-permute-start.30 = (bf16[1,192,1024]{2,1,0:T(8,128)(2,1)}, bf16[1,192,1024]{2,1,0:T(8,128)(2,1)}, u32[]{:S(2)}, u32[]{:S(2)}) collective-permute-start(bf16[1,192,1024]{2,1,0:T(8,128)(2,1)} %get-tuple-element.217), channel_id=1, source_target_pairs={{0,4},{4,0},{8,12},{12,8},{1,5},{5,1},{9,13},{13,9},{2,6},{6,2},{1... | collective-permute-start | bytes 1179656 | tf_op jit(solution)/shard_map/ppermute | solution.py:902
  544.2 38.0 %collective-permute-start.36 = (bf16[4,96,768]{2,1,0:T(8,128)(2,1)S(1)}, bf16[4,96,768]{2,1,0:T(8,128)(2,1)}, u32[]{:S(2)}, u32[]{:S(2)}) collective-permute-start(bf16[4,96,768]{2,1,0:T(8,128)(2,1)S(1)} %fusion.30), channel_id=1, source_target_pairs={{0,8},{4,12},{8,0},{12,4},{1,9},{5,13},{9,1},{13,5},{2,10},{6,14},... | collective-permute-start | bytes 1769480 | tf_op jit(solution)/shard_map/ppermute | solution.py:902
  549.6 38.0 %all-to-all-start.5 = ((bf16[4,96,1728]{2,1,0:T(8,128)(2,1)}), bf16[4,96,1728]{2,1,0:T(8,128)(2,1)S(1)}, u32[]{:S(2)}, u32[]{:S(2)}) async-start(bf16[4,96,1728]{2,1,0:T(8,128)(2,1)} %fusion.9), calls=%async_computation.5 | async-start | bytes 2752512 | tf_op jit(solution)/shard_map/all_to_all | solution.py:939
  580.3 25.2 %collective-permute-start.33 = (bf16[1,192,1024]{2,1,0:T(8,128)(2,1)}, bf16[1,192,1024]{2,1,0:T(8,128)(2,1)}, u32[]{:S(2)}, u32[]{:S(2)}) collective-permute-start(bf16[1,192,1024]{2,1,0:T(8,128)(2,1)} %get-tuple-element.227), channel_id=1, source_target_pairs={{0,4},{4,0},{8,12},{12,8},{1,5},{5,1},{9,13},{13,9},{2,6},{6,2},{1... | collective-permute-start | bytes 1179656 | tf_op jit(solution)/shard_map/ppermute | solution.py:902
  580.6 26.6 %collective-permute-start.34 = (bf16[1,192,1024]{2,1,0:T(8,128)(2,1)}, bf16[1,192,1024]{2,1,0:T(8,128)(2,1)}, u32[]{:S(2)}, u32[]{:S(2)}) collective-permute-start(bf16[1,192,1024]{2,1,0:T(8,128)(2,1)} %get-tuple-element.228), channel_id=1, source_target_pairs={{0,8},{4,12},{8,0},{12,4},{1,9},{5,13},{9,1},{13,5},{2,10},{6,14},... | collective-permute-start | bytes 1179656 | tf_op jit(solution)/shard_map/ppermute | solution.py:902
  582.1 25.0 %collective-permute-start.35 = (bf16[1,192,1024]{2,1,0:T(8,128)(2,1)}, bf16[1,192,1024]{2,1,0:T(8,128)(2,1)}, u32[]{:S(2)}, u32[]{:S(2)}) collective-permute-start(bf16[1,192,1024]{2,1,0:T(8,128)(2,1)} %get-tuple-element.229), channel_id=1, source_target_pairs={{0,12},{4,8},{8,4},{12,0},{1,13},{5,9},{9,5},{13,1},{2,14},{6,10},... | collective-permute-start | bytes 1179656 | tf_op jit(solution)/shard_map/ppermute | solution.py:902
  584.6 33.0 %collective-permute-start.37 = (bf16[96,768]{1,0:T(8,128)(2,1)}, bf16[96,768]{1,0:T(8,128)(2,1)S(1)}, u32[]{:S(2)}, u32[]{:S(2)}) collective-permute-start(bf16[96,768]{1,0:T(8,128)(2,1)} %get-tuple-element.379), channel_id=1, source_target_pairs={{0,1},{1,0},{2,3},{3,2},{4,5},{5,4},{6,7},{7,6},{8,9},{9,8},{10,11... | collective-permute-start | bytes 442376 | tf_op jit(solution)/shard_map/ppermute | solution.py:902
  584.7 33.0 %collective-permute-start.38 = (bf16[96,768]{1,0:T(8,128)(2,1)}, bf16[96,768]{1,0:T(8,128)(2,1)}, u32[]{:S(2)}, u32[]{:S(2)}) collective-permute-start(bf16[96,768]{1,0:T(8,128)(2,1)} %get-tuple-element.381), channel_id=1, source_target_pairs={{0,2},{1,3},{2,0},{3,1},{4,6},{5,7},{6,4},{7,5},{8,10},{9,11},{10,... | collective-permute-start | bytes 442376 | tf_op jit(solution)/shard_map/ppermute | solution.py:902
  623.1 22.1 %collective-permute-start.40 = (bf16[384,576]{1,0:T(8,128)(2,1)}, bf16[384,576]{1,0:T(8,128)(2,1)}, u32[]{:S(2)}, u32[]{:S(2)}) collective-permute-start(bf16[384,576]{1,0:T(8,128)(2,1)} %dynamic-slice_bitcast_fusion.2), channel_id=1, source_target_pairs={{0,16},{16,0},{1,17},{17,1},{2,18},{18,2},{3,19},{19,3},{4,20},{20... | collective-permute-start | bytes 1327112 | tf_op jit(solution)/shard_map/ppermute | solution.py:902
  634.2 86.4 %all-to-all-start.7 = ((bf16[4,256,768]{2,1,0:T(8,128)(2,1)}), bf16[4,256,768]{2,1,0:T(8,128)(2,1)S(1)}, u32[]{:S(2)}, u32[]{:S(2)}) async-start(bf16[4,256,768]{2,1,0:T(8,128)(2,1)} %bitcast.163), calls=%async_computation.7 | async-start | bytes 3145728 | tf_op jit(solution)/shard_map/all_to_all | solution.py:939
  639.7 32.4 %collective-permute-start.49 = (bf16[192,768]{1,0:T(8,128)(2,1)}, bf16[192,768]{1,0:T(8,128)(2,1)}, u32[]{:S(2)}, u32[]{:S(2)}) collective-permute-start(bf16[192,768]{1,0:T(8,128)(2,1)} %pad_maximum_fusion.9), channel_id=1, source_target_pairs={{0,4},{4,0},{8,12},{12,8},{1,5},{5,1},{9,13},{13,9},{2,6},{6,2},{1... | collective-permute-start | bytes 884744 | tf_op jit(solution)/shard_map/ppermute | solution.py:902
  667.3 46.9 %collective-permute-start.51 = (bf16[192,1728]{1,0:T(8,128)(2,1)}, bf16[192,1728]{1,0:T(8,128)(2,1)}, u32[]{:S(2)}, u32[]{:S(2)}) collective-permute-start(bf16[192,1728]{1,0:T(8,128)(2,1)} %pad_maximum_fusion.4), channel_id=1, source_target_pairs={{0,4},{4,0},{8,12},{12,8},{1,5},{5,1},{9,13},{13,9},{2,6},{6,2},{1... | collective-permute-start | bytes 1990664 | tf_op jit(solution)/shard_map/ppermute | solution.py:902
  667.8 24.8 %collective-permute-start.41 = (bf16[96,576]{0,1:T(8,128)(2,1)}, bf16[96,576]{0,1:T(8,128)(2,1)}, u32[]{:S(2)}, u32[]{:S(2)}) collective-permute-start(bf16[96,576]{0,1:T(8,128)(2,1)} %bitcast.188), channel_id=1, source_target_pairs={{0,1},{1,0},{2,3},{3,2},{4,5},{5,4},{6,7},{7,6},{8,9},{9,8},{10,11... | collective-permute-start | bytes 331784 | tf_op jit(solution)/shard_map/ppermute | solution.py:902
  668.6 24.0 %collective-permute-start.42 = (bf16[96,576]{0,1:T(8,128)(2,1)}, bf16[96,576]{0,1:T(8,128)(2,1)}, u32[]{:S(2)}, u32[]{:S(2)}) collective-permute-start(bf16[96,576]{0,1:T(8,128)(2,1)} %bitcast.187), channel_id=1, source_target_pairs={{0,2},{1,3},{2,0},{3,1},{4,6},{5,7},{6,4},{7,5},{8,10},{9,11},{10,... | collective-permute-start | bytes 331784 | tf_op jit(solution)/shard_map/ppermute | solution.py:902
  669.8 22.8 %collective-permute-start.43 = (bf16[96,576]{0,1:T(8,128)(2,1)}, bf16[96,576]{0,1:T(8,128)(2,1)}, u32[]{:S(2)}, u32[]{:S(2)}) collective-permute-start(bf16[96,576]{0,1:T(8,128)(2,1)} %bitcast.186), channel_id=1, source_target_pairs={{0,3},{1,2},{2,1},{3,0},{4,7},{5,6},{6,5},{7,4},{8,11},{9,10},{10,... | collective-permute-start | bytes 331784 | tf_op jit(solution)/shard_map/ppermute | solution.py:902
  (72 other events, 754.7 us)
Sparse Core Ops, SparseCore 0:
  51.7 165.9 all-gather.2
  389.5 77.6 all-gather.4

commit v4 on v3

--- a/solution.py
+++ b/solution.py
@@ -1147,8 +1147,9 @@
     )
     feed_sum.over_core()
     output = exchange(output.reshape(tensor_count, device_places, model_width), "tp")
+    self_w = gather_all(after(local_self, first_low))
     back_query, back_pairs = cross_backward(
-        meta, cross_query, pairs, cross_att, after(back_cross, feed_sum.send), cross_total
+        meta, cross_query, pairs, cross_att, after(back_cross, feed_sum.send, self_w), cross_total
     )
     back_pairs = back_pairs.reshape(context_count, pair_width, retrieved)
     feed_sum.over_shard()
@@ -1171,7 +1172,6 @@
             meta, back_one, first_low, selected, back_query, back_pairs, self_att, shard_count
         )
     )
-    self_w = gather_all(after(local_self, first_low))
 
     squares = jnp.sum(jnp.concatenate([first_totals[:3], totals[:3]], axis=0), axis=1)
     rows = jnp.stack(

time: 743 us -> 773 us (1.040)
  waiting for transfers between devices: 117 us -> 141 us
  Pallas kernels: 346 us -> 367 us
  starting transfers between devices: 116 us -> 101 us
    all_to_all x8, waiting for transfers between devices: 43.5 us -> 75.5 us  [exchange(): return lax.all_to_all(parts, axes, split_axis=0, concat_axis=0, tiled=True)]
    pallas_call x3, Pallas kernels: 81.5 us -> 100 us  [self_backward(): pl.pallas_call(functools.partial(self_backward_kernel, begin=begin), grid...]
    ppermute x53, starting transfers between devices: 78.7 us -> 60.4 us  [turn(): return lax.ppermute(array, axis, [(at, at ^ step) for at in range(count)])]
    ppermute x53, waiting for transfers between devices: 73.3 us -> 65.3 us  [turn(): return lax.ppermute(array, axis, [(at, at ^ step) for at in range(count)])]
    unnamed x119 -> x125, local copies, waits for them, and re-layouts: 16.4 us -> 15.5 us
  transfers between devices with their start and end apart: 67 -> 67, of which waited for: 14 -> 15; matrix products, arithmetic and copies ran while one was open for 17% -> 17% of each run, Pallas kernels for 38% -> 48%
where the time goes in v4:
time: 773 us; the launch traced here: 763 us
  Pallas kernels  367 us (47%)
  waiting for transfers between devices  141 us (18%)
  starting transfers between devices  101 us (13%)
  other arithmetic  65.9 us (9%)
  local copies, waits for them, and re-layouts  55.7 us (7%)
  matrix products  16.3 us (2%)
  between operations  16.1 us (2%)
    pallas_call x3, Pallas kernels, self_backward(): pl.pallas_call(functools.partial(self_backward_kernel, begin=begin), grid...  100 us
    all_to_all x8, waiting for transfers between devices, exchange(): return lax.all_to_all(parts, axes, split_axis=0, concat_axis=0, tiled=True)  75.5 us
    ppermute x53, waiting for transfers between devices, turn(): return lax.ppermute(array, axis, [(at, at ^ step) for at in range(count)])  65.3 us
    pallas_call x3, Pallas kernels, self_forward(): pl.pallas_call(functools.partial(self_forward_kernel, begin=begin), grid_...  61.8 us
    ppermute x53, starting transfers between devices, turn(): return lax.ppermute(array, axis, [(at, at ^ step) for at in range(count)])  60.4 us
    pallas_call x1, Pallas kernels, feed_step(): pl.pallas_call(functools.partial(feed_kernel, quarter=quarter), grid_spec...  42.1 us
    all_to_all x8, starting transfers between devices, exchange(): return lax.all_to_all(parts, axes, split_axis=0, concat_axis=0, tiled=True)  37.5 us
    pallas_call x1, Pallas kernels, cross_backward(): pl.pallas_call(cross_backward_kernel, grid_spec=pltpu.PrefetchScalarGridS...  37.3 us
  transfers between devices with their start and end apart: 67, of which 15 were waited for; matrix products, arithmetic and copies ran while one was open for 17% of the time, Pallas kernels for 48%

profile of v4, /device:TPU:0, one launch (start us, length us, event | category | flops | bytes accessed | tf_op | source)
XLA Modules:
  0.0 762.7 jit_solution(4809889826365769520)
XLA Ops:
  7.2 6.5 all-to-all-start
  17.6 33.1 %all-to-all-done = bf16[4,256,768]{2,1,0:T(8,128)(2,1)} async-done(((bf16[4,256,768]{2,1,0:T(8,128)(2,1)}), bf16[4,256,768]{2,1,0:T(8,128)(2,1)}, u32[]{:S(2)}, u32[]{:S(2)}) %all-to-all-start) | async-done | bytes 1572896 | tf_op jit(solution)/shard_map/all_to_all | solution.py:939
  56.2 8.2 %gather_fusion = bf16[1024,768]{1,0:T(8,128)(2,1)S(1)} fusion(bf16[4096,768]{1,0:T(8,128)(2,1)} %bitcast.155, s32[1024]{0:T(1024)S(1)} %broadcast_clamp_fusion), kind=kCustom, calls=%fused_computation | custom fusion | bytes 3149824 | tf_op jit(solution)/shard_map/jit(_take)/gather | solution.py:1092
  70.8 5.2 collective-permute-done.1
  77.0 6.8 collective-permute-start.2
  83.8 26.6 %collective-permute-done.3.refs_2_ = bf16[1024,768]{1,0:T(8,128)(2,1)} collective-permute-done((bf16[1024,768]{1,0:T(8,128)(2,1)}, bf16[1024,768]{1,0:T(8,128)(2,1)}, u32[]{:S(2)}, u32[]{:S(2)}) %collective-permute-start.3) | collective-permute-done | bytes 1572896 | tf_op jit(solution)/shard_map/ppermute | solution.py:902
  110.4 3.6 all-to-all-start.1
  115.1 11.9 %project.1 = (bf16[4096,768]{1,0:T(8,128)(2,1)}, bf16[576,4096]{1,0:T(8,128)(2,1)}) custom-call(s32[6]{0:T(128)} %stack.24.meta_ref, bf16[576,768]{1,0:T(8,128)(2,1)} %pad_maximum_fusion.3.weight_ref, bf16[1024,768]{1,0:T(8,128)(2,1)} %bitcast.10.refs_0_, bf16[1024,768]{1,0:T(8,128)(2,1)} %copy-done.42, bf16[1024,768]{1,0:T(8,128)(2,1)} %collective-permute-done.3.refs_2_, ...), custom_call_target="tpu_custom_call" | custom-call | flops 11000000512 | tf_op jit(solution)/shard_map/project/pallas_call | solution.py:484
  127.1 20.5 %self_forward.3 = (bf16[1,64,1024]{2,1,0:T(8,128)(2,1)}, bf16[1,64,1024]{2,1,0:T(8,128)(2,1)}, bf16[1,64,1024]{2,1,0:T(8,128)(2,1)}, bf16[1,64,1024]{2,1,0:T(8,128)(2,1)}, f32[1,1,4096]{2,1,0:T(1,128)}) custom-call(s32[6]{0:T(128)} %stack.24.meta_ref, bf16[3,192,4096]{2,1,0:T(8,128)(2,1)} %bitcast.217), custom_call_target="tpu_custom_call" | custom-call | flops 22000001024 | tf_op jit(solution)/shard_map/self_forward/pallas_call | solution.py:178
  150.5 20.8 %self_forward.4 = (bf16[1,64,1024]{2,1,0:T(8,128)(2,1)}, bf16[1,64,1024]{2,1,0:T(8,128)(2,1)}, bf16[1,64,1024]{2,1,0:T(8,128)(2,1)}, bf16[1,64,1024]{2,1,0:T(8,128)(2,1)}, f32[1,1,4096]{2,1,0:T(1,128)}) custom-call(s32[6]{0:T(128)} %stack.24.meta_ref, bf16[3,192,4096]{2,1,0:T(8,128)(2,1)} %bitcast.218), custom_call_target="tpu_custom_call" | custom-call | flops 22000001024 | tf_op jit(solution)/shard_map/self_forward/pallas_call | solution.py:178
  171.3 9.2 %all-to-all-done.1 = bf16[4,256,768]{2,1,0:T(8,128)(2,1)S(1)} async-done(((bf16[4,256,768]{2,1,0:T(8,128)(2,1)}), bf16[4,256,768]{2,1,0:T(8,128)(2,1)S(1)}, u32[]{:S(2)}, u32[]{:S(2)}) %all-to-all-start.1) | async-done | bytes 1572896 | tf_op jit(solution)/shard_map/all_to_all | solution.py:939
  183.7 20.5 %self_forward.5 = (bf16[1,64,1024]{2,1,0:T(8,128)(2,1)}, bf16[1,64,1024]{2,1,0:T(8,128)(2,1)}, bf16[1,64,1024]{2,1,0:T(8,128)(2,1)}, bf16[1,64,1024]{2,1,0:T(8,128)(2,1)}, f32[1,1,4096]{2,1,0:T(1,128)}) custom-call(s32[6]{0:T(128)} %stack.24.meta_ref, bf16[3,192,4096]{2,1,0:T(8,128)(2,1)} %bitcast.219), custom_call_target="tpu_custom_call" | custom-call | flops 22000001024 | tf_op jit(solution)/shard_map/self_forward/pallas_call | solution.py:178
  207.2 5.1 collective-permute-done.13
  214.5 4.3 all-to-all-start.2
  221.2 5.7 fusion.40
  228.8 12.4 %first_step.1 = (f32[1024,768]{1,0:T(8,128)}, bf16[1024,768]{1,0:T(8,128)(2,1)}, bf16[768,1024]{1,0:T(8,128)(2,1)}, f32[8,768]{1,0:T(8,128)}) custom-call(s32[6]{0:T(128)} %stack.24.meta_ref, bf16[4096,768]{1,0:T(8,128)(2,1)} %get-tuple-element.227.x_ref, f32[8,768]{1,0:T(8,128)} %copy.176.norm_ref, bf16[4,768,192]{2,1,0:T(8,128)(2,1)} %get-tuple-element.348.out_w_ref, ...), custom_call_target="tpu_custom_call" | custom-call | flops 8800000000 | tf_op jit(solution)/shard_map/first_step/pallas_call | solution.py:532
  244.1 8.8 %convolution_convert_fusion = bf16[4,384,1024]{2,1,0:T(8,128)(2,1)} fusion(bf16[4,768,2502]{2,1,0:T(8,128)(2,1)} %bitcast.168, bf16[256,768]{1,0:T(8,128)(2,1)S(1)} %get-tuple-element.360, bf16[256,768]{1,0:T(8,128)(2,1)S(1)} %get-tuple-element.359, bf16[256,768]{1,0:T(8,128)(2,1)S(1)} %get-tuple-element.358, bf16[256,768]{1,0:T(8,128)(2,1)S(1)} %get-tuple-element.357), kind=kOutput, calls=%fused_computation.18 | convolution fusion | flops 2423783424 | bytes 7077888 | tf_op jit(solution)/shard_map/tdf,kd->tfk/dot_general | solution.py:897
  252.9 21.6 %cross_forward.1 = (bf16[768,1024]{1,0:T(8,128)(2,1)}, f32[12,1,1024]{2,1,0:T(1,128)}) custom-call(s32[6]{0:T(128)} %stack.24.meta_ref, bf16[768,1024]{1,0:T(8,128)(2,1)} %get-tuple-element.162.query_ref, bf16[4,3,128,1024]{3,2,1,0:T(8,128)(2,1)} %bitcast.223), custom_call_target="tpu_custom_call" | custom-call | flops 27499999232 | tf_op jit(solution)/shard_map/cross_forward/pallas_call | solution.py:364
  276.6 42.1 %feed_step.1 = (bf16[1024,768]{1,0:T(8,128)(2,1)}, bf16[1024,768]{1,0:T(8,128)(2,1)}, bf16[1024,3072]{1,0:T(8,128)(2,1)}, bf16[1024,3072]{1,0:T(8,128)(2,1)}, bf...) custom-call(s32[6]{0:T(128)} %stack.24.meta_ref, ...), custom_call_target="tpu_custom_call" | custom-call | flops 49500000256 | tf_op jit(solution)/shard_map/feed_step/pallas_call | solution.py:631
  318.7 25.7 %feed_grad.1 = (bf16[4,2,192,1728]{3,2,1,0:T(8,128)(2,1)}, bf16[4,2,192,1728]{3,2,1,0:T(8,128)(2,1)}) custom-call(s32[6]{0:T(128)} %stack.24.meta_ref, bf16[1024,768]{1,0:T(8,128)(2,1)} %get-tuple-element.174.low_ref, bf16[1024,3072]{1,0:T(8,128)(2,1)} %get-tuple-element.175.inner_ref, bf16[1024,768]{1,0:T(8,128)(2,1)} %get-tuple-element.176.back_ref, ...), custom_call_target="tpu_custom_call" | custom-call | flops 19800000512 | tf_op jit(solution)/shard_map/feed_grad/pallas_call | solution.py:794
  344.9 5.3 all-to-all-start.3
  354.2 33.2 %all-to-all-done.3 = bf16[4,256,768]{2,1,0:T(8,128)(2,1)S(1)} async-done(((bf16[4,256,768]{2,1,0:T(8,128)(2,1)}), bf16[4,256,768]{2,1,0:T(8,128)(2,1)S(1)}, u32[]{:S(2)}, u32[]{:S(2)}) %all-to-all-start.3) | async-done | bytes 1572896 | tf_op jit(solution)/shard_map/all_to_all | solution.py:939
  387.4 5.3 fusion.4
  396.8 37.3 %cross_backward.1 = (bf16[768,1024]{1,0:T(8,128)(2,1)}, bf16[4,3,128,1024]{3,2,1,0:T(8,128)(2,1)}) custom-call(s32[6]{0:T(128)} %stack.24.meta_ref, bf16[768,1024]{1,0:T(8,128)(2,1)} %get-tuple-element.162.query_ref, bf16[4,3,128,1024]{3,2,1,0:T(8,128)(2,1)} %bitcast.224, bf16[768,1024]{1,0:T(8,128)(2,1)} %get-tuple-element.168.att_ref.cross_ref.out_ref, ...), custom_call_target="tpu_custom_call" | custom-call | flops 39600001024 | tf_op jit(solution)/shard_map/cross_backward/pallas_call | solution.py:413
  434.1 7.5 bitcast_convert_fusion
  441.6 4.8 all-to-all-start.4
  446.4 12.4 %last_step.1 = (bf16[192,1024]{1,0:T(8,128)(2,1)}, bf16[192,1024]{1,0:T(8,128)(2,1)}, bf16[192,1024]{1,0:T(8,128)(2,1)}, bf16[192,1024]{1,0:T(8,128)(2,1)}, f32[...) custom-call(s32[6]{0:T(128)} %stack.24.meta_ref, bf16[768,1024]{1,0:T(8,128)(2,1)} %get-tuple-element.183.query_ref, ...), custom_call_target="tpu_custom_call" | custom-call | flops 8800000000 | tf_op jit(solution)/shard_map/last_step/pallas_call | solution.py:688
  461.1 14.1 %mixed_grad.1 = (bf16[4,2,192,768]{3,2,1,0:T(8,128)(2,1)}, bf16[4,2,192,768]{3,2,1,0:T(8,128)(2,1)}) custom-call(s32[6]{0:T(128)} %stack.24.meta_ref, bf16[1024,768]{1,0:T(8,128)(2,1)} %get-tuple-element.189.one_ref, bf16[1024,768]{1,0:T(8,128)(2,1)} %get-tuple-element.163.low_ref, bf16[1024,768]{1,0:T(8,128)(2,1)} %pad_maximum_fusion.selected_ref, ...), custom_call_target="tpu_custom_call" | custom-call | flops 15399999488 | tf_op jit(solution)/shard_map/mixed_grad/pallas_call | solution.py:845
  478.2 4.7 collective-permute-done.21
  482.9 33.5 %self_backward.3 = (bf16[1,192,1024]{2,1,0:T(8,128)(2,1)}, bf16[1,192,1024]{2,1,0:T(8,128)(2,1)}, bf16[1,192,1024]{2,1,0:T(8,128)(2,1)}, bf16[1,192,1024]{2,1,0:T(8,128)(2,1)}) custom-call(s32[6]{0:T(128)} %stack.24.meta_ref, bf16[3,192,4096]{2,1,0:T(8,128)(2,1)} %bitcast.220, f32[1,1,4096]{2,1,0:T(1,128)} %get-tuple-element.137.total_ref, ...), custom_call_target="tpu_custom_call" | custom-call | flops 32999999488 | tf_op jit(solution)/shard_map/self_backward/pallas_call | solution.py:308
  519.2 4.4 all-to-all-start.6
  523.6 3.5 fusion.6
  532.3 4.3 collective-permute-start.27
  539.2 33.5 %self_backward.4 = (bf16[1,192,1024]{2,1,0:T(8,128)(2,1)}, bf16[1,192,1024]{2,1,0:T(8,128)(2,1)}, bf16[1,192,1024]{2,1,0:T(8,128)(2,1)}, bf16[1,192,1024]{2,1,0:T(8,128)(2,1)}) custom-call(s32[6]{0:T(128)} %stack.24.meta_ref, bf16[3,192,4096]{2,1,0:T(8,128)(2,1)} %bitcast.221, f32[1,1,4096]{2,1,0:T(1,128)} %get-tuple-element.139.total_ref, ...), custom_call_target="tpu_custom_call" | custom-call | flops 32999999488 | tf_op jit(solution)/shard_map/self_backward/pallas_call | solution.py:308
  577.8 3.8 fusion.9
  581.6 3.8 all-to-all-start.5
  587.3 33.3 %self_backward.5 = (bf16[1,192,1024]{2,1,0:T(8,128)(2,1)}, bf16[1,192,1024]{2,1,0:T(8,128)(2,1)}, bf16[1,192,1024]{2,1,0:T(8,128)(2,1)}, bf16[1,192,1024]{2,1,0:T(8,128)(2,1)}) custom-call(s32[6]{0:T(128)} %stack.24.meta_ref, bf16[3,192,4096]{2,1,0:T(8,128)(2,1)} %bitcast.222, f32[1,1,4096]{2,1,0:T(1,128)} %get-tuple-element.146.total_ref, ...), custom_call_target="tpu_custom_call" | custom-call | flops 32999999488 | tf_op jit(solution)/shard_map/self_backward/pallas_call | solution.py:308
  626.4 5.5 own_grad.3
  631.9 5.4 own_grad.4
  637.3 5.4 own_grad.5
  644.1 4.5 collective-permute-start.39
  648.6 10.6 %hidden_step.1 = bf16[1024,768]{1,0:T(8,128)(2,1)} custom-call(s32[6]{0:T(128)} %stack.24.meta_ref, f32[1024,768]{1,0:T(8,128)} %get-tuple-element.231.back_ref, bf16[4,768,576]{2,1,0:T(8,128)(2,1)} %bitcast.194, bf16[4,192,1024]{2,1,0:T(8,128)(2,1)} %all-to-all-done.6.refs_0_, bf16[192,1024]{1,0:T(8,128)(2,1)} %bitcast.231, ...), custom_call_target="tpu_custom_call" | custom-call | flops 8800000000 | tf_op jit(solution)/shard_map/hidden_step/pallas_call | solution.py:736
  664.7 4.9 all-to-all-start.7
  683.8 14.4 %scatter_custom_fusion = f32[4096,768]{1,0:T(8,128)} fusion(s32[1024]{0:T(1024)} %bitcast.192, f32[]{:T(128)} %constant.215.clone.1, bf16[256,768]{1,0:T(8,128)(2,1)} %get-tuple-element.352, bf16[]{:T(256)} %constant.225, bf16[256,768]{1,0:T(8,128)(2,1)} %get-tuple-element.351, bf16[256,768]{1,0:T(8,128)(2,1)S(1)} %get-tuple-element.350, ...), kind=kCustom, calls=%fused_computation.2 | custom fusion | flops 7864320 | bytes 14158336 | tf_op jit(solution)/shard_map/scatter-add | solution.py:1261
  708.1 6.7 collective-permute-done.54
  716.0 3.4 collective-permute-done.55
  726.7 8.3 %collective-permute-start.45 = (bf16[96,576]{0,1:T(8,128)(2,1)S(1)}, bf16[96,576]{0,1:T(8,128)(2,1)S(1)}, u32[]{:S(2)}, u32[]{:S(2)}) collective-permute-start(bf16[96,576]{0,1:T(8,128)(2,1)S(1)} %collective-permute-done.44), channel_id=1, source_target_pairs={{0,12},{4,8},{8,4},{12,0},{1,13},{5,9},{9,5},{13,1},{2,14},{6,10},... | collective-permute-start | bytes 331784 | tf_op jit(solution)/shard_map/ppermute | solution.py:902
  737.9 5.5 collective-permute-done.46
  (317 shorter events, 128.6 us)
Async XLA Ops:
  7.2 43.5 %all-to-all-start = ((bf16[4,256,768]{2,1,0:T(8,128)(2,1)}), bf16[4,256,768]{2,1,0:T(8,128)(2,1)}, u32[]{:S(2)}, u32[]{:S(2)}) async-start(bf16[4,256,768]{2,1,0:T(8,128)(2,1)} %param.17), calls=%async_computation | async-start | bytes 3145728 | tf_op jit(solution)/shard_map/all_to_all | solution.py:939
  13.7 207.5 %all-gather.3.cloned.1.call-start = ((), (), s32[]{:S(2)}) async-start(), calls=%async_computation.8 | async-start | bytes 16220160 | tf_op jit(solution)/shard_map/all_gather | solution.py:1084
  51.6 58.8 %collective-permute-start.3 = (bf16[1024,768]{1,0:T(8,128)(2,1)}, bf16[1024,768]{1,0:T(8,128)(2,1)}, u32[]{:S(2)}, u32[]{:S(2)}) collective-permute-start(bf16[1024,768]{1,0:T(8,128)(2,1)} %bitcast.10.refs_0_), channel_id=1, source_target_pairs={{0,8},{4,12},{8,0},{12,4},{1,9},{5,13},{9,1},{13,5},{2,10},{6,14},... | collective-permute-start | bytes 4718600 | tf_op jit(solution)/shard_map/ppermute | solution.py:902
  77.0 36.9 %collective-permute-start.2 = (bf16[1024,768]{1,0:T(8,128)(2,1)}, bf16[1024,768]{1,0:T(8,128)(2,1)S(1)}, u32[]{:S(2)}, u32[]{:S(2)}) collective-permute-start(bf16[1024,768]{1,0:T(8,128)(2,1)} %bitcast.10.refs_0_), channel_id=1, source_target_pairs={{0,4},{4,0},{8,12},{12,8},{1,5},{5,1},{9,13},{13,9},{2,6},{6,2},{1... | collective-permute-start | bytes 4718600 | tf_op jit(solution)/shard_map/ppermute | solution.py:902
  110.4 70.2 %all-to-all-start.1 = ((bf16[4,256,768]{2,1,0:T(8,128)(2,1)}), bf16[4,256,768]{2,1,0:T(8,128)(2,1)S(1)}, u32[]{:S(2)}, u32[]{:S(2)}) async-start(bf16[4,256,768]{2,1,0:T(8,128)(2,1)} %bitcast.15), calls=%async_computation.1 | async-start | bytes 3145728 | tf_op jit(solution)/shard_map/all_to_all | solution.py:939
  147.6 35.0 %collective-permute-start.6 = (bf16[1,64,1024]{2,1,0:T(8,128)(2,1)}, bf16[1,64,1024]{2,1,0:T(8,128)(2,1)S(1)}, u32[]{:S(2)}, u32[]{:S(2)}) collective-permute-start(bf16[1,64,1024]{2,1,0:T(8,128)(2,1)} %get-tuple-element.142.refs_1_), channel_id=1, source_target_pairs={{0,4},{4,0},{8,12},{12,8},{1,5},{5,1},{9,13},{13,9},{2,6},{6,2},{1... | collective-permute-start | bytes 393224 | tf_op jit(solution)/shard_map/ppermute | solution.py:902
  148.1 34.9 %collective-permute-start.7 = (bf16[1,64,1024]{2,1,0:T(8,128)(2,1)}, bf16[1,64,1024]{2,1,0:T(8,128)(2,1)S(1)}, u32[]{:S(2)}, u32[]{:S(2)}) collective-permute-start(bf16[1,64,1024]{2,1,0:T(8,128)(2,1)} %get-tuple-element.143.refs_2_), channel_id=1, source_target_pairs={{0,8},{4,12},{8,0},{12,4},{1,9},{5,13},{9,1},{13,5},{2,10},{6,14},... | collective-permute-start | bytes 393224 | tf_op jit(solution)/shard_map/ppermute | solution.py:902
  150.5 33.1 %collective-permute-start.8 = (bf16[1,64,1024]{2,1,0:T(8,128)(2,1)}, bf16[1,64,1024]{2,1,0:T(8,128)(2,1)S(1)}, u32[]{:S(2)}, u32[]{:S(2)}) collective-permute-start(bf16[1,64,1024]{2,1,0:T(8,128)(2,1)} %get-tuple-element.144.refs_3_), channel_id=1, source_target_pairs={{0,12},{4,8},{8,4},{12,0},{1,13},{5,9},{9,5},{13,1},{2,14},{6,10},... | collective-permute-start | bytes 393224 | tf_op jit(solution)/shard_map/ppermute | solution.py:902
  180.6 25.2 %collective-permute-start.11 = (bf16[1,64,1024]{2,1,0:T(8,128)(2,1)}, bf16[1,64,1024]{2,1,0:T(8,128)(2,1)S(1)}, u32[]{:S(2)}, u32[]{:S(2)}) collective-permute-start(bf16[1,64,1024]{2,1,0:T(8,128)(2,1)} %get-tuple-element.156.refs_3_), channel_id=1, source_target_pairs={{0,12},{4,8},{8,4},{12,0},{1,13},{5,9},{9,5},{13,1},{2,14},{6,10},... | collective-permute-start | bytes 393224 | tf_op jit(solution)/shard_map/ppermute | solution.py:902
  180.6 26.3 %collective-permute-start.10 = (bf16[1,64,1024]{2,1,0:T(8,128)(2,1)}, bf16[1,64,1024]{2,1,0:T(8,128)(2,1)S(1)}, u32[]{:S(2)}, u32[]{:S(2)}) collective-permute-start(bf16[1,64,1024]{2,1,0:T(8,128)(2,1)} %get-tuple-element.154.refs_2_), channel_id=1, source_target_pairs={{0,8},{4,12},{8,0},{12,4},{1,9},{5,13},{9,1},{13,5},{2,10},{6,14},... | collective-permute-start | bytes 393224 | tf_op jit(solution)/shard_map/ppermute | solution.py:902
  182.6 24.6 %collective-permute-start.9 = (bf16[1,64,1024]{2,1,0:T(8,128)(2,1)S(1)}, bf16[1,64,1024]{2,1,0:T(8,128)(2,1)S(1)}, u32[]{:S(2)}, u32[]{:S(2)}) collective-permute-start(bf16[1,64,1024]{2,1,0:T(8,128)(2,1)S(1)} %copy-done.44), channel_id=1, source_target_pairs={{0,4},{4,0},{8,12},{12,8},{1,5},{5,1},{9,13},{13,9},{2,6},{6,2},{1... | collective-permute-start | bytes 393224 | tf_op jit(solution)/shard_map/ppermute | solution.py:902
  182.9 36.3 %collective-permute-start.5 = (bf16[256,768]{1,0:T(8,128)(2,1)S(1)}, bf16[256,768]{1,0:T(8,128)(2,1)S(1)}, u32[]{:S(2)}, u32[]{:S(2)}) collective-permute-start(bf16[256,768]{1,0:T(8,128)(2,1)S(1)} %reduce_sum.54), channel_id=1, source_target_pairs={{0,0},{1,4},{2,8},{3,12},{4,1},{5,5},{6,9},{7,13},{8,2},{9,6},{10,... | collective-permute-start | bytes 1179656 | tf_op jit(solution)/shard_map/ppermute | solution.py:1128
  214.5 59.9 %all-to-all-start.2 = ((bf16[4,256,768]{2,1,0:T(8,128)(2,1)}), bf16[4,256,768]{2,1,0:T(8,128)(2,1)S(1)}, u32[]{:S(2)}, u32[]{:S(2)}) async-start(bf16[4,256,768]{2,1,0:T(8,128)(2,1)} %param.21), calls=%async_computation.2 | async-start | bytes 3145728 | tf_op jit(solution)/shard_map/all_to_all | solution.py:939
  218.8 178.0 %all-gather.5.cloned.1.call-start = ((), (), s32[]{:S(2)}) async-start(), calls=%async_computation.9 | async-start | bytes 4055040 | tf_op jit(solution)/shard_map/all_gather | solution.py:1084
  219.3 21.9 %collective-permute-start.17 = (bf16[256,768]{1,0:T(8,128)(2,1)S(1)}, bf16[256,768]{1,0:T(8,128)(2,1)S(1)}, u32[]{:S(2)}, u32[]{:S(2)}) collective-permute-start(bf16[256,768]{1,0:T(8,128)(2,1)S(1)} %collective-permute-done.5), channel_id=1, source_target_pairs={{0,4},{4,0},{8,12},{12,8},{1,5},{5,1},{9,13},{13,9},{2,6},{6,2},{1... | collective-permute-start | bytes 1179656 | tf_op jit(solution)/shard_map/ppermute | solution.py:902
  219.4 21.9 %collective-permute-start.16 = (bf16[256,768]{1,0:T(8,128)(2,1)S(1)}, bf16[256,768]{1,0:T(8,128)(2,1)S(1)}, u32[]{:S(2)}, u32[]{:S(2)}) collective-permute-start(bf16[256,768]{1,0:T(8,128)(2,1)S(1)} %collective-permute-done.5), channel_id=1, source_target_pairs={{0,8},{4,12},{8,0},{12,4},{1,9},{5,13},{9,1},{13,5},{2,10},{6,14},... | collective-permute-start | bytes 1179656 | tf_op jit(solution)/shard_map/ppermute | solution.py:902
  220.8 21.9 %collective-permute-start.15 = (bf16[256,768]{1,0:T(8,128)(2,1)S(1)}, bf16[256,768]{1,0:T(8,128)(2,1)}, u32[]{:S(2)}, u32[]{:S(2)}) collective-permute-start(bf16[256,768]{1,0:T(8,128)(2,1)S(1)} %collective-permute-done.5), channel_id=1, source_target_pairs={{0,12},{4,8},{8,4},{12,0},{1,13},{5,9},{9,5},{13,1},{2,14},{6,10},... | collective-permute-start | bytes 1179656 | tf_op jit(solution)/shard_map/ppermute | solution.py:902
  344.4 43.0 %collective-permute-start.18 = (bf16[4,2,192,1728]{3,2,1,0:T(8,128)(2,1)}, bf16[4,2,192,1728]{3,2,1,0:T(8,128)(2,1)}, u32[]{:S(2)}, u32[]{:S(2)}) collective-permute-start(bf16[4,2,192,1728]{3,2,1,0:T(8,128)(2,1)} %get-tuple-element.179), channel_id=1, source_target_pairs={{0,4},{4,0},{8,12},{12,8},{1,5},{5,1},{9,13},{13,9},{2,6},{6,2},{1... | collective-permute-start | bytes 15925256 | tf_op jit(solution)/shard_map/ppermute | solution.py:902
  344.9 42.6 %all-to-all-start.3 = ((bf16[4,256,768]{2,1,0:T(8,128)(2,1)}), bf16[4,256,768]{2,1,0:T(8,128)(2,1)S(1)}, u32[]{:S(2)}, u32[]{:S(2)}) async-start(bf16[4,256,768]{2,1,0:T(8,128)(2,1)} %bitcast.42), calls=%async_computation.3 | async-start | bytes 3145728 | tf_op jit(solution)/shard_map/all_to_all | solution.py:939
  392.7 123.6 %collective-permute-start.23 = (bf16[4,192,1728]{2,1,0:T(8,128)(2,1)}, bf16[4,192,1728]{2,1,0:T(8,128)(2,1)}, u32[]{:S(2)}, u32[]{:S(2)}) collective-permute-start(bf16[4,192,1728]{2,1,0:T(8,128)(2,1)} %fusion.4), channel_id=1, source_target_pairs={{0,16},{16,0},{1,17},{17,1},{2,18},{18,2},{3,19},{19,3},{4,20},{20... | collective-permute-start | bytes 7962632 | tf_op jit(solution)/shard_map/ppermute | solution.py:902
  441.6 34.1 %all-to-all-start.4 = ((bf16[4,256,768]{2,1,0:T(8,128)(2,1)}), bf16[4,256,768]{2,1,0:T(8,128)(2,1)}, u32[]{:S(2)}, u32[]{:S(2)}) async-start(bf16[4,256,768]{2,1,0:T(8,128)(2,1)} %bitcast.165), calls=%async_computation.4 | async-start | bytes 3145728 | tf_op jit(solution)/shard_map/all_to_all | solution.py:939
  458.8 18.7 %collective-permute-start.19 = (bf16[192,1024]{1,0:T(8,128)(2,1)}, bf16[192,1024]{1,0:T(8,128)(2,1)}, u32[]{:S(2)}, u32[]{:S(2)}) collective-permute-start(bf16[192,1024]{1,0:T(8,128)(2,1)} %get-tuple-element.194), channel_id=1, source_target_pairs={{0,4},{4,0},{8,12},{12,8},{1,5},{5,1},{9,13},{13,9},{2,6},{6,2},{1... | collective-permute-start | bytes 1179656 | tf_op jit(solution)/shard_map/ppermute | solution.py:902
  459.4 18.8 %collective-permute-start.20 = (bf16[192,1024]{1,0:T(8,128)(2,1)}, bf16[192,1024]{1,0:T(8,128)(2,1)}, u32[]{:S(2)}, u32[]{:S(2)}) collective-permute-start(bf16[192,1024]{1,0:T(8,128)(2,1)} %get-tuple-element.195), channel_id=1, source_target_pairs={{0,8},{4,12},{8,0},{12,4},{1,9},{5,13},{9,1},{13,5},{2,10},{6,14},... | collective-permute-start | bytes 1179656 | tf_op jit(solution)/shard_map/ppermute | solution.py:902
  461.1 21.8 %collective-permute-start.21 = (bf16[192,1024]{1,0:T(8,128)(2,1)}, bf16[192,1024]{1,0:T(8,128)(2,1)}, u32[]{:S(2)}, u32[]{:S(2)}) collective-permute-start(bf16[192,1024]{1,0:T(8,128)(2,1)} %get-tuple-element.196), channel_id=1, source_target_pairs={{0,12},{4,8},{8,4},{12,0},{1,13},{5,9},{9,5},{13,1},{2,14},{6,10},... | collective-permute-start | bytes 1179656 | tf_op jit(solution)/shard_map/ppermute | solution.py:902
  475.2 61.4 %collective-permute-start.24 = (bf16[4,2,192,768]{3,2,1,0:T(8,128)(2,1)}, bf16[4,2,192,768]{3,2,1,0:T(8,128)(2,1)}, u32[]{:S(2)}, u32[]{:S(2)}) collective-permute-start(bf16[4,2,192,768]{3,2,1,0:T(8,128)(2,1)} %get-tuple-element.190), channel_id=1, source_target_pairs={{0,4},{4,0},{8,12},{12,8},{1,5},{5,1},{9,13},{13,9},{2,6},{6,2},{1... | collective-permute-start | bytes 7077896 | tf_op jit(solution)/shard_map/ppermute | solution.py:902
  477.5 54.7 %collective-permute-start.22 = (bf16[256,768]{1,0:T(8,128)(2,1)S(1)}, bf16[256,768]{1,0:T(8,128)(2,1)S(1)}, u32[]{:S(2)}, u32[]{:S(2)}) collective-permute-start(bf16[256,768]{1,0:T(8,128)(2,1)S(1)} %reduce_sum.55), channel_id=1, source_target_pairs={{0,0},{1,4},{2,8},{3,12},{4,1},{5,5},{6,9},{7,13},{8,2},{9,6},{10,... | collective-permute-start | bytes 1179656 | tf_op jit(solution)/shard_map/ppermute | solution.py:1206
  519.2 54.3 %all-to-all-start.6 = ((bf16[4,192,1024]{2,1,0:T(8,128)(2,1)}), bf16[4,192,1024]{2,1,0:T(8,128)(2,1)}, u32[]{:S(2)}, u32[]{:S(2)}) async-start(bf16[4,192,1024]{2,1,0:T(8,128)(2,1)} %pad_maximum_fusion.1), calls=%async_computation.6 | async-start | bytes 3145728 | tf_op jit(solution)/shard_map/all_to_all | solution.py:939
  527.1 50.7 %collective-permute-start.25 = (bf16[4,96,1728]{2,1,0:T(8,128)(2,1)}, bf16[4,96,1728]{2,1,0:T(8,128)(2,1)}, u32[]{:S(2)}, u32[]{:S(2)}) collective-permute-start(bf16[4,96,1728]{2,1,0:T(8,128)(2,1)} %fusion.6), channel_id=1, source_target_pairs={{0,8},{4,12},{8,0},{12,4},{1,9},{5,13},{9,1},{13,5},{2,10},{6,14},... | collective-permute-start | bytes 3981320 | tf_op jit(solution)/shard_map/ppermute | solution.py:902
  532.2 40.6 %collective-permute-start.29 = (bf16[256,768]{1,0:T(8,128)(2,1)S(1)}, bf16[256,768]{1,0:T(8,128)(2,1)S(1)}, u32[]{:S(2)}, u32[]{:S(2)}) collective-permute-start(bf16[256,768]{1,0:T(8,128)(2,1)S(1)} %collective-permute-done.22), channel_id=1, source_target_pairs={{0,3},{1,2},{2,1},{3,0},{4,7},{5,6},{6,5},{7,4},{8,11},{9,10},{10,... | collective-permute-start | bytes 1179656 | tf_op jit(solution)/shard_map/ppermute | solution.py:902
  532.2 40.6 %collective-permute-start.28 = (bf16[256,768]{1,0:T(8,128)(2,1)S(1)}, bf16[256,768]{1,0:T(8,128)(2,1)S(1)}, u32[]{:S(2)}, u32[]{:S(2)}) collective-permute-start(bf16[256,768]{1,0:T(8,128)(2,1)S(1)} %collective-permute-done.22), channel_id=1, source_target_pairs={{0,2},{1,3},{2,0},{3,1},{4,6},{5,7},{6,4},{7,5},{8,10},{9,11},{10,... | collective-permute-start | bytes 1179656 | tf_op jit(solution)/shard_map/ppermute | solution.py:902
  532.3 41.3 %collective-permute-start.27 = (bf16[256,768]{1,0:T(8,128)(2,1)S(1)}, bf16[256,768]{1,0:T(8,128)(2,1)}, u32[]{:S(2)}, u32[]{:S(2)}) collective-permute-start(bf16[256,768]{1,0:T(8,128)(2,1)S(1)} %collective-permute-done.22), channel_id=1, source_target_pairs={{0,1},{1,0},{2,3},{3,2},{4,5},{5,4},{6,7},{7,6},{8,9},{9,8},{10,11... | collective-permute-start | bytes 1179656 | tf_op jit(solution)/shard_map/ppermute | solution.py:902
  539.2 46.2 %collective-permute-start.26 = (bf16[4,192,768]{2,1,0:T(8,128)(2,1)}, bf16[4,192,768]{2,1,0:T(8,128)(2,1)}, u32[]{:S(2)}, u32[]{:S(2)}) collective-permute-start(bf16[4,192,768]{2,1,0:T(8,128)(2,1)} %fusion.25), channel_id=1, source_target_pairs={{0,16},{16,0},{1,17},{17,1},{2,18},{18,2},{3,19},{19,3},{4,20},{20... | collective-permute-start | bytes 3538952 | tf_op jit(solution)/shard_map/ppermute | solution.py:902
  575.9 44.7 %collective-permute-start.32 = (bf16[1,192,1024]{2,1,0:T(8,128)(2,1)}, bf16[1,192,1024]{2,1,0:T(8,128)(2,1)S(1)}, u32[]{:S(2)}, u32[]{:S(2)}) collective-permute-start(bf16[1,192,1024]{2,1,0:T(8,128)(2,1)} %get-tuple-element.220), channel_id=1, source_target_pairs={{0,12},{4,8},{8,4},{12,0},{1,13},{5,9},{9,5},{13,1},{2,14},{6,10},... | collective-permute-start | bytes 1179656 | tf_op jit(solution)/shard_map/ppermute | solution.py:902
  575.9 44.8 %collective-permute-start.31 = (bf16[1,192,1024]{2,1,0:T(8,128)(2,1)}, bf16[1,192,1024]{2,1,0:T(8,128)(2,1)}, u32[]{:S(2)}, u32[]{:S(2)}) collective-permute-start(bf16[1,192,1024]{2,1,0:T(8,128)(2,1)} %get-tuple-element.219), channel_id=1, source_target_pairs={{0,8},{4,12},{8,0},{12,4},{1,9},{5,13},{9,1},{13,5},{2,10},{6,14},... | collective-permute-start | bytes 1179656 | tf_op jit(solution)/shard_map/ppermute | solution.py:902
  576.6 44.1 %collective-permute-start.30 = (bf16[1,192,1024]{2,1,0:T(8,128)(2,1)}, bf16[1,192,1024]{2,1,0:T(8,128)(2,1)}, u32[]{:S(2)}, u32[]{:S(2)}) collective-permute-start(bf16[1,192,1024]{2,1,0:T(8,128)(2,1)} %get-tuple-element.218), channel_id=1, source_target_pairs={{0,4},{4,0},{8,12},{12,8},{1,5},{5,1},{9,13},{13,9},{2,6},{6,2},{1... | collective-permute-start | bytes 1179656 | tf_op jit(solution)/shard_map/ppermute | solution.py:902
  581.6 44.6 %all-to-all-start.5 = ((bf16[4,96,1728]{2,1,0:T(8,128)(2,1)}), bf16[4,96,1728]{2,1,0:T(8,128)(2,1)S(1)}, u32[]{:S(2)}, u32[]{:S(2)}) async-start(bf16[4,96,1728]{2,1,0:T(8,128)(2,1)} %fusion.9), calls=%async_computation.5 | async-start | bytes 2752512 | tf_op jit(solution)/shard_map/all_to_all | solution.py:939
  587.0 36.8 %collective-permute-start.36 = (bf16[4,96,768]{2,1,0:T(8,128)(2,1)S(1)}, bf16[4,96,768]{2,1,0:T(8,128)(2,1)S(1)}, u32[]{:S(2)}, u32[]{:S(2)}) collective-permute-start(bf16[4,96,768]{2,1,0:T(8,128)(2,1)S(1)} %fusion.30), channel_id=1, source_target_pairs={{0,8},{4,12},{8,0},{12,4},{1,9},{5,13},{9,1},{13,5},{2,10},{6,14},... | collective-permute-start | bytes 1769480 | tf_op jit(solution)/shard_map/ppermute | solution.py:902
  620.7 23.4 %collective-permute-start.33 = (bf16[1,192,1024]{2,1,0:T(8,128)(2,1)}, bf16[1,192,1024]{2,1,0:T(8,128)(2,1)}, u32[]{:S(2)}, u32[]{:S(2)}) collective-permute-start(bf16[1,192,1024]{2,1,0:T(8,128)(2,1)} %get-tuple-element.228), channel_id=1, source_target_pairs={{0,4},{4,0},{8,12},{12,8},{1,5},{5,1},{9,13},{13,9},{2,6},{6,2},{1... | collective-permute-start | bytes 1179656 | tf_op jit(solution)/shard_map/ppermute | solution.py:902
  620.9 27.7 %collective-permute-start.34 = (bf16[1,192,1024]{2,1,0:T(8,128)(2,1)}, bf16[1,192,1024]{2,1,0:T(8,128)(2,1)}, u32[]{:S(2)}, u32[]{:S(2)}) collective-permute-start(bf16[1,192,1024]{2,1,0:T(8,128)(2,1)} %get-tuple-element.229), channel_id=1, source_target_pairs={{0,8},{4,12},{8,0},{12,4},{1,9},{5,13},{9,1},{13,5},{2,10},{6,14},... | collective-permute-start | bytes 1179656 | tf_op jit(solution)/shard_map/ppermute | solution.py:902
  622.6 26.0 %collective-permute-start.35 = (bf16[1,192,1024]{2,1,0:T(8,128)(2,1)}, bf16[1,192,1024]{2,1,0:T(8,128)(2,1)}, u32[]{:S(2)}, u32[]{:S(2)}) collective-permute-start(bf16[1,192,1024]{2,1,0:T(8,128)(2,1)} %get-tuple-element.230), channel_id=1, source_target_pairs={{0,12},{4,8},{8,4},{12,0},{1,13},{5,9},{9,5},{13,1},{2,14},{6,10},... | collective-permute-start | bytes 1179656 | tf_op jit(solution)/shard_map/ppermute | solution.py:902
  626.1 33.1 %collective-permute-start.37 = (bf16[96,768]{1,0:T(8,128)(2,1)}, bf16[96,768]{1,0:T(8,128)(2,1)S(1)}, u32[]{:S(2)}, u32[]{:S(2)}) collective-permute-start(bf16[96,768]{1,0:T(8,128)(2,1)} %get-tuple-element.379), channel_id=1, source_target_pairs={{0,1},{1,0},{2,3},{3,2},{4,5},{5,4},{6,7},{7,6},{8,9},{9,8},{10,11... | collective-permute-start | bytes 442376 | tf_op jit(solution)/shard_map/ppermute | solution.py:902
  626.1 33.1 %collective-permute-start.38 = (bf16[96,768]{1,0:T(8,128)(2,1)}, bf16[96,768]{1,0:T(8,128)(2,1)}, u32[]{:S(2)}, u32[]{:S(2)}) collective-permute-start(bf16[96,768]{1,0:T(8,128)(2,1)} %get-tuple-element.381), channel_id=1, source_target_pairs={{0,2},{1,3},{2,0},{3,1},{4,6},{5,7},{6,4},{7,5},{8,10},{9,11},{10,... | collective-permute-start | bytes 442376 | tf_op jit(solution)/shard_map/ppermute | solution.py:902
  664.7 87.8 %all-to-all-start.7 = ((bf16[4,256,768]{2,1,0:T(8,128)(2,1)}), bf16[4,256,768]{2,1,0:T(8,128)(2,1)S(1)}, u32[]{:S(2)}, u32[]{:S(2)}) async-start(bf16[4,256,768]{2,1,0:T(8,128)(2,1)} %bitcast.163), calls=%async_computation.7 | async-start | bytes 3145728 | tf_op jit(solution)/shard_map/all_to_all | solution.py:939
  671.3 32.7 %collective-permute-start.49 = (bf16[192,768]{1,0:T(8,128)(2,1)}, bf16[192,768]{1,0:T(8,128)(2,1)}, u32[]{:S(2)}, u32[]{:S(2)}) collective-permute-start(bf16[192,768]{1,0:T(8,128)(2,1)} %pad_maximum_fusion.9), channel_id=1, source_target_pairs={{0,4},{4,0},{8,12},{12,8},{1,5},{5,1},{9,13},{13,9},{2,6},{6,2},{1... | collective-permute-start | bytes 884744 | tf_op jit(solution)/shard_map/ppermute | solution.py:902
  699.2 46.9 %collective-permute-start.51 = (bf16[192,1728]{1,0:T(8,128)(2,1)}, bf16[192,1728]{1,0:T(8,128)(2,1)}, u32[]{:S(2)}, u32[]{:S(2)}) collective-permute-start(bf16[192,1728]{1,0:T(8,128)(2,1)} %pad_maximum_fusion.4), channel_id=1, source_target_pairs={{0,4},{4,0},{8,12},{12,8},{1,5},{5,1},{9,13},{13,9},{2,6},{6,2},{1... | collective-permute-start | bytes 1990664 | tf_op jit(solution)/shard_map/ppermute | solution.py:902
  699.7 24.6 %collective-permute-start.41 = (bf16[96,576]{0,1:T(8,128)(2,1)}, bf16[96,576]{0,1:T(8,128)(2,1)}, u32[]{:S(2)}, u32[]{:S(2)}) collective-permute-start(bf16[96,576]{0,1:T(8,128)(2,1)} %bitcast.188), channel_id=1, source_target_pairs={{0,1},{1,0},{2,3},{3,2},{4,5},{5,4},{6,7},{7,6},{8,9},{9,8},{10,11... | collective-permute-start | bytes 331784 | tf_op jit(solution)/shard_map/ppermute | solution.py:902
  699.7 24.6 %collective-permute-start.42 = (bf16[96,576]{0,1:T(8,128)(2,1)}, bf16[96,576]{0,1:T(8,128)(2,1)}, u32[]{:S(2)}, u32[]{:S(2)}) collective-permute-start(bf16[96,576]{0,1:T(8,128)(2,1)} %bitcast.187), channel_id=1, source_target_pairs={{0,2},{1,3},{2,0},{3,1},{4,6},{5,7},{6,4},{7,5},{8,10},{9,11},{10,... | collective-permute-start | bytes 331784 | tf_op jit(solution)/shard_map/ppermute | solution.py:902
  701.9 22.4 %collective-permute-start.43 = (bf16[96,576]{0,1:T(8,128)(2,1)}, bf16[96,576]{0,1:T(8,128)(2,1)}, u32[]{:S(2)}, u32[]{:S(2)}) collective-permute-start(bf16[96,576]{0,1:T(8,128)(2,1)} %bitcast.186), channel_id=1, source_target_pairs={{0,3},{1,2},{2,1},{3,0},{4,7},{5,6},{6,5},{7,4},{8,11},{9,10},{10,... | collective-permute-start | bytes 331784 | tf_op jit(solution)/shard_map/ppermute | solution.py:902
  (75 other events, 708.3 us)
Sparse Core Ops, SparseCore 0:
  51.7 165.9 all-gather.2
  276.7 62.2 all-gather.4
